TPU v7x, 32 devices: a whole 2x2x4 slice. The times are simulated.
32 devices in a mesh: dp: 8 (over z, core), fsdp: 4 (over y, x).
Axes of the slice: x: 2, y: 2, z: 4, core: 2. Of those that a mesh axis runs over, the one named last changes fastest.
Arguments:
- units: bfloat16 [32, 1024, 1024], P(None, ('dp', 'fsdp')), may hold values from -6 to 6
- encoder: bfloat16 [32, 256, 1024], P(None, ('dp', 'fsdp')), may hold values from -6 to 6
- cotangent: bfloat16 [32, 1024, 1024], P(None, ('dp', 'fsdp')), may hold values from -6 to 6
- deal: int32 [32], replicated, may hold values from 0 to 31, each once
- lengths: int32 [32], replicated, may hold values from 256 to 1024, as said below
- enc_counts: int32 [32], replicated, may hold values from 128 to 256, as said below
- self_qkv: bfloat16 [3, 1024, 1024], P(None, ('dp', 'fsdp')), may hold values from -0.1875 to 0.1875
- self_out: bfloat16 [1024, 1024], P(('dp', 'fsdp')), may hold values from -1.5 to 1.5
- cross_qkv: bfloat16 [3, 1024, 1024], P(None, ('dp', 'fsdp')), may hold values from -0.1875 to 0.1875
- cross_out: bfloat16 [1024, 1024], P(('dp', 'fsdp')), may hold values from -1.5 to 1.5
- ffn_up: bfloat16 [1024, 4096], P(('dp', 'fsdp')), may hold values from -0.1875 to 0.1875
- ffn_down: bfloat16 [4096, 1024], P(('dp', 'fsdp')), may hold values from -0.125 to 0.125
- biases: bfloat16 [6, 1024], P(None, ('dp', 'fsdp')), may hold values from -1.75 to 1.75
- ffn_bias_up: bfloat16 [4096], P(('dp', 'fsdp')), may hold values from -1.75 to 1.75
- ffn_bias_down: bfloat16 [1024], P(('dp', 'fsdp')), may hold values from -1.75 to 1.75
- norm_gain: bfloat16 [3, 1024], P(None, ('dp', 'fsdp')), may hold values from 0.5 to 1.5
- norm_shift: bfloat16 [3, 1024], P(None, ('dp', 'fsdp')), may hold values from -1.75 to 1.75
Outputs:
- output: bfloat16 [32, 1024, 1024], P(None, ('dp', 'fsdp'))
- grad_units: bfloat16 [32, 1024, 1024], P(None, ('dp', 'fsdp'))
- grad_encoder: bfloat16 [32, 256, 1024], P(None, ('dp', 'fsdp'))
- grad_self_qkv: float32 [3, 1024, 1024], P(None, ('dp', 'fsdp'))
- grad_self_out: float32 [1024, 1024], P(('dp', 'fsdp'))
- grad_cross_qkv: float32 [3, 1024, 1024], P(None, ('dp', 'fsdp'))
- grad_cross_out: float32 [1024, 1024], P(('dp', 'fsdp'))
- grad_ffn_up: float32 [1024, 4096], P(('dp', 'fsdp'))
- grad_ffn_down: float32 [4096, 1024], P(('dp', 'fsdp'))
- grad_biases: float32 [6, 1024], P(None, ('dp', 'fsdp'))
- grad_ffn_bias_up: float32 [4096], P(('dp', 'fsdp'))
- grad_ffn_bias_down: float32 [1024], P(('dp', 'fsdp'))
- grad_norm_gain: float32 [3, 1024], P(None, ('dp', 'fsdp'))
- grad_norm_shift: float32 [3, 1024], P(None, ('dp', 'fsdp'))
Inputs may be any that keep to these rules, and one draw needn't show every extreme that they name: `deal`: every sequence number appears exactly once. `lengths`: each sequence has at least 256 tokens, and some sequence fills all 1024 slots. `enc_counts`: each sequence has at least 128 encoder states, and some sequence fills all 256 slots.
All inputs are finite; a program needn't handle non-finite values.
Results may differ from a plain program's by a relative error of at most 0.02.
Values may be sent and summed in bfloat16 or wider, within the bound.
A program may use at most 384 MiB of HBM per device.

v0:
```python
import jax
import jax.numpy as jnp
from jax import lax
from jax.sharding import PartitionSpec as P

HD = 64


EPSILON = 1e-05
SCALE = 0.125
NEGATIVE = -1e30


def layer_norm(value, gain, shift):
    mean = jnp.mean(value, axis=-1, keepdims=True)
    centred = value - mean
    spread = jnp.mean(centred * centred, axis=-1, keepdims=True)
    return centred * lax.rsqrt(spread + EPSILON) * gain + shift


def smooth_gate(value):
    return jax.nn.gelu(value, approximate=True)


def product(left, right):
    return jnp.dot(left, right, preferred_element_type=jnp.float32)


def product_tn(left, right):
    return lax.dot_general(
        left, right, (((0,), (0,)), ((), ())), preferred_element_type=jnp.float32
    )


def product_nt(left, right):
    return lax.dot_general(
        left, right, (((1,), (1,)), ((), ())), preferred_element_type=jnp.float32
    )


def column_sum(value):
    return jnp.sum(value.astype(jnp.float32), axis=0)


def attend_forward(query, keys, values, allowed):
    rows, width = query.shape
    heads = width // HD
    block = min(512, rows)
    keys3 = keys.reshape(keys.shape[0], heads, HD)
    values3 = values.reshape(values.shape[0], heads, HD)

    def one_block(start):
        query3 = lax.dynamic_slice_in_dim(query, start, block, 0).reshape(block, heads, HD)
        scores = jnp.einsum("qhd,khd->hqk", query3, keys3, preferred_element_type=jnp.float32)
        scores = jnp.where(allowed(start, block)[None], scores, NEGATIVE)
        top = jnp.max(scores, axis=-1, keepdims=True)
        weights = jnp.exp(scores - top)
        total = jnp.sum(weights, axis=-1, keepdims=True)
        probs = (weights / total).astype(jnp.bfloat16)
        mixed = jnp.einsum("hqk,khd->qhd", probs, values3, preferred_element_type=jnp.float32)
        return (mixed.reshape(block, width), top + jnp.log(total))

    starts = jnp.arange(rows // block, dtype=jnp.int32) * block
    mixed, summary = lax.map(one_block, starts)
    return (mixed.reshape(rows, width).astype(jnp.bfloat16), summary)


def attend_backward(query, keys, values, summary, grad_mixed, allowed):
    rows, width = query.shape
    heads = width // HD
    block = min(512, rows)
    count = keys.shape[0]
    keys3 = keys.reshape(count, heads, HD)
    values3 = values.reshape(count, heads, HD)

    def one_block(carry, item):
        grad_keys, grad_values = carry
        start, logsum = item
        query3 = lax.dynamic_slice_in_dim(query, start, block, 0).reshape(block, heads, HD)
        grad3 = lax.dynamic_slice_in_dim(grad_mixed, start, block, 0).reshape(block, heads, HD)
        scores = jnp.einsum("qhd,khd->hqk", query3, keys3, preferred_element_type=jnp.float32)
        scores = jnp.where(allowed(start, block)[None], scores, NEGATIVE)
        probs = jnp.exp(scores - logsum)
        grad_values = grad_values + jnp.einsum(
            "hqk,qhd->khd", probs.astype(jnp.bfloat16), grad3, preferred_element_type=jnp.float32
        )
        grad_probs = jnp.einsum("qhd,khd->hqk", grad3, values3, preferred_element_type=jnp.float32)
        inner = jnp.sum(probs * grad_probs, axis=-1, keepdims=True)
        grad_scores = (probs * (grad_probs - inner)).astype(jnp.bfloat16)
        grad_query = jnp.einsum(
            "hqk,khd->qhd", grad_scores, keys3, preferred_element_type=jnp.float32
        )
        grad_keys = grad_keys + jnp.einsum(
            "hqk,qhd->khd", grad_scores, query3, preferred_element_type=jnp.float32
        )
        return ((grad_keys, grad_values), grad_query.reshape(block, width))

    empty = jnp.zeros((count, heads, HD), jnp.float32)
    starts = jnp.arange(rows // block, dtype=jnp.int32) * block
    (grad_keys, grad_values), grad_query = lax.scan(one_block, (empty, empty), (starts, summary))
    return (
        grad_query.reshape(rows, width).astype(jnp.bfloat16),
        grad_keys.reshape(count, width).astype(jnp.bfloat16),
        grad_values.reshape(count, width).astype(jnp.bfloat16),
    )


def per_device(
    units,
    encoder,
    cotangent,
    deal,
    lengths,
    enc_counts,
    self_qkv,
    self_out,
    cross_qkv,
    cross_out,
    ffn_up,
    ffn_down,
    biases,
    ffn_bias_up,
    ffn_bias_down,
    norm_gain,
    norm_shift,
):
    slots = deal.shape[0]
    inverse = jnp.zeros((slots,), jnp.int32).at[deal].set(jnp.arange(slots, dtype=jnp.int32))
    dealt_units = jnp.take(units, deal, axis=0)
    dealt_enc = jnp.take(encoder, deal, axis=0)
    dealt_cot = jnp.take(cotangent, deal, axis=0)
    arrived, enc_arrived, cot_arrived = (
        lax.all_to_all(dealt_units, ("dp", "fsdp"), split_axis=0, concat_axis=1, tiled=True),
        lax.all_to_all(dealt_enc, ("dp", "fsdp"), split_axis=0, concat_axis=1, tiled=True),
        lax.all_to_all(dealt_cot, ("dp", "fsdp"), split_axis=0, concat_axis=1, tiled=True),
    )
    place = lax.axis_index(("dp", "fsdp"))
    length = lax.dynamic_index_in_dim(lengths, place, keepdims=False)
    enc_count = lax.dynamic_index_in_dim(enc_counts, place, keepdims=False)
    states = arrived[0].astype(jnp.float32)
    memory = enc_arrived[0]
    rows = states.shape[0]
    positions = jnp.arange(rows, dtype=jnp.int32)
    enc_positions = jnp.arange(memory.shape[0], dtype=jnp.int32)
    valid = (positions < length).astype(jnp.float32)[:, None]
    grad_out = cot_arrived[0].astype(jnp.float32) * valid

    def causal(start, block):
        query_rows = start + jnp.arange(block, dtype=jnp.int32)
        return (positions[None, :] <= query_rows[:, None]) & (positions[None, :] < length)

    def across(start, block):
        return jnp.broadcast_to(enc_positions[None, :] < enc_count, (block, enc_positions.shape[0]))

    weights = (
        lax.all_gather(self_qkv, ("dp", "fsdp"), axis=1, tiled=True),
        lax.all_gather(self_out, ("dp", "fsdp"), axis=0, tiled=True),
        lax.all_gather(cross_qkv, ("dp", "fsdp"), axis=1, tiled=True),
        lax.all_gather(cross_out, ("dp", "fsdp"), axis=0, tiled=True),
        lax.all_gather(ffn_up, ("dp", "fsdp"), axis=0, tiled=True),
        lax.all_gather(ffn_down, ("dp", "fsdp"), axis=0, tiled=True),
        lax.all_gather(biases, ("dp", "fsdp"), axis=1, tiled=True),
        lax.all_gather(ffn_bias_up, ("dp", "fsdp"), axis=0, tiled=True),
        lax.all_gather(ffn_bias_down, ("dp", "fsdp"), axis=0, tiled=True),
        lax.all_gather(norm_gain, ("dp", "fsdp"), axis=1, tiled=True),
        lax.all_gather(norm_shift, ("dp", "fsdp"), axis=1, tiled=True),
    )
    s_qkv, s_out, c_qkv, c_out, w_up, w_down = (
        weights[0],
        weights[1],
        weights[2],
        weights[3],
        weights[4],
        weights[5],
    )
    bias_rows = weights[6].astype(jnp.float32)
    bias_up = weights[7].astype(jnp.float32)
    bias_down = weights[8].astype(jnp.float32)
    gains = weights[9].astype(jnp.float32)
    shifts = weights[10].astype(jnp.float32)
    normed0 = layer_norm(states, gains[0], shifts[0]).astype(jnp.bfloat16)
    query0 = ((product(normed0, s_qkv[0]) + bias_rows[0]) * SCALE).astype(jnp.bfloat16)
    keys0 = product(normed0, s_qkv[1]).astype(jnp.bfloat16)
    values0 = (product(normed0, s_qkv[2]) + bias_rows[1]).astype(jnp.bfloat16)
    mixed0, summary0 = attend_forward(query0, keys0, values0, causal)
    first = states + (product(mixed0, s_out) + bias_rows[2])
    normed1 = layer_norm(first, gains[1], shifts[1]).astype(jnp.bfloat16)
    query1 = ((product(normed1, c_qkv[0]) + bias_rows[3]) * SCALE).astype(jnp.bfloat16)
    keys1 = product(memory, c_qkv[1]).astype(jnp.bfloat16)
    values1 = (product(memory, c_qkv[2]) + bias_rows[4]).astype(jnp.bfloat16)
    mixed1, summary1 = attend_forward(query1, keys1, values1, across)
    second = first + (product(mixed1, c_out) + bias_rows[5])
    normed2 = layer_norm(second, gains[2], shifts[2]).astype(jnp.bfloat16)
    before = product(normed2, w_up) + bias_up
    activated, pull_gate = jax.vjp(smooth_gate, before)
    hidden = activated.astype(jnp.bfloat16)
    result = (second + (product(hidden, w_down) + bias_down)) * valid
    regathered = (
        lax.all_gather(self_qkv, ("dp", "fsdp"), axis=1, tiled=True),
        lax.all_gather(self_out, ("dp", "fsdp"), axis=0, tiled=True),
        lax.all_gather(cross_qkv, ("dp", "fsdp"), axis=1, tiled=True),
        lax.all_gather(cross_out, ("dp", "fsdp"), axis=0, tiled=True),
        lax.all_gather(ffn_up, ("dp", "fsdp"), axis=0, tiled=True),
        lax.all_gather(ffn_down, ("dp", "fsdp"), axis=0, tiled=True),
        lax.all_gather(biases, ("dp", "fsdp"), axis=1, tiled=True),
        lax.all_gather(ffn_bias_up, ("dp", "fsdp"), axis=0, tiled=True),
        lax.all_gather(ffn_bias_down, ("dp", "fsdp"), axis=0, tiled=True),
        lax.all_gather(norm_gain, ("dp", "fsdp"), axis=1, tiled=True),
        lax.all_gather(norm_shift, ("dp", "fsdp"), axis=1, tiled=True),
    )
    s_qkv, s_out, c_qkv, c_out, w_up, w_down = (
        regathered[0],
        regathered[1],
        regathered[2],
        regathered[3],
        regathered[4],
        regathered[5],
    )
    branch = grad_out.astype(jnp.bfloat16)
    grad_down = product_tn(hidden, branch)
    grad_bias_down = column_sum(branch)
    grad_hidden = product_nt(branch, w_down)
    grad_before = pull_gate(grad_hidden)[0].astype(jnp.bfloat16)
    grad_up = product_tn(normed2, grad_before)
    grad_bias_up = column_sum(grad_before)
    _, pull_two = jax.vjp(layer_norm, second, gains[2], shifts[2])
    grad_from, grad_gain_two, grad_shift_two = pull_two(product_nt(grad_before, w_up))
    grad_second = grad_out + grad_from
    branch = grad_second.astype(jnp.bfloat16)
    grad_cross_out = product_tn(mixed1, branch)
    grad_bias_five = column_sum(branch)
    grad_mixed = product_nt(branch, c_out).astype(jnp.bfloat16)
    grad_query, grad_keys, grad_values = attend_backward(
        query1, keys1, values1, summary1, grad_mixed, across
    )
    grad_cross_query = product_tn(normed1, grad_query) * SCALE
    grad_bias_three = column_sum(grad_query) * SCALE
    grad_cross_keys = product_tn(memory, grad_keys)
    grad_cross_values = product_tn(memory, grad_values)
    grad_bias_four = column_sum(grad_values)
    grad_memory = product_nt(grad_keys, c_qkv[1]) + product_nt(grad_values, c_qkv[2])
    _, pull_one = jax.vjp(layer_norm, first, gains[1], shifts[1])
    grad_from, grad_gain_one, grad_shift_one = pull_one(product_nt(grad_query, c_qkv[0]) * SCALE)
    grad_first = grad_second + grad_from
    branch = grad_first.astype(jnp.bfloat16)
    grad_self_out = product_tn(mixed0, branch)
    grad_bias_two = column_sum(branch)
    grad_mixed = product_nt(branch, s_out).astype(jnp.bfloat16)
    grad_query, grad_keys, grad_values = attend_backward(
        query0, keys0, values0, summary0, grad_mixed, causal
    )
    grad_self_query = product_tn(normed0, grad_query) * SCALE
    grad_bias_zero = column_sum(grad_query) * SCALE
    grad_self_keys = product_tn(normed0, grad_keys)
    grad_self_values = product_tn(normed0, grad_values)
    grad_bias_one = column_sum(grad_values)
    grad_normed = (
        product_nt(grad_query, s_qkv[0]) * SCALE
        + product_nt(grad_keys, s_qkv[1])
        + product_nt(grad_values, s_qkv[2])
    )
    _, pull_zero = jax.vjp(layer_norm, states, gains[0], shifts[0])
    grad_from, grad_gain_zero, grad_shift_zero = pull_zero(grad_normed)
    grad_states = grad_first + grad_from
    grad_self_qkv = jnp.stack([grad_self_query, grad_self_keys, grad_self_values])
    grad_cross_qkv = jnp.stack([grad_cross_query, grad_cross_keys, grad_cross_values])
    grad_biases = jnp.stack(
        [
            grad_bias_zero,
            grad_bias_one,
            grad_bias_two,
            grad_bias_three,
            grad_bias_four,
            grad_bias_five,
        ]
    )
    grad_gains = jnp.stack([grad_gain_zero, grad_gain_one, grad_gain_two])
    grad_shifts = jnp.stack([grad_shift_zero, grad_shift_one, grad_shift_two])
    summed = (
        lax.psum_scatter(grad_self_qkv, ("dp", "fsdp"), scatter_dimension=1, tiled=True),
        lax.psum_scatter(grad_self_out, ("dp", "fsdp"), scatter_dimension=0, tiled=True),
        lax.psum_scatter(grad_cross_qkv, ("dp", "fsdp"), scatter_dimension=1, tiled=True),
        lax.psum_scatter(grad_cross_out, ("dp", "fsdp"), scatter_dimension=0, tiled=True),
        lax.psum_scatter(grad_up, ("dp", "fsdp"), scatter_dimension=0, tiled=True),
        lax.psum_scatter(grad_down, ("dp", "fsdp"), scatter_dimension=0, tiled=True),
        lax.psum_scatter(grad_biases, ("dp", "fsdp"), scatter_dimension=1, tiled=True),
        lax.psum_scatter(grad_bias_up, ("dp", "fsdp"), scatter_dimension=0, tiled=True),
        lax.psum_scatter(grad_bias_down, ("dp", "fsdp"), scatter_dimension=0, tiled=True),
        lax.psum_scatter(grad_gains, ("dp", "fsdp"), scatter_dimension=1, tiled=True),
        lax.psum_scatter(grad_shifts, ("dp", "fsdp"), scatter_dimension=1, tiled=True),
    )
    leaving = result.astype(jnp.bfloat16)[None]
    grad_leaving = grad_states.astype(jnp.bfloat16)[None]
    grad_enc_leaving = grad_memory.astype(jnp.bfloat16)[None]
    returned, grad_returned, grad_enc_returned = (
        lax.all_to_all(leaving, ("dp", "fsdp"), split_axis=1, concat_axis=0, tiled=True),
        lax.all_to_all(grad_leaving, ("dp", "fsdp"), split_axis=1, concat_axis=0, tiled=True),
        lax.all_to_all(grad_enc_leaving, ("dp", "fsdp"), split_axis=1, concat_axis=0, tiled=True),
    )
    returned = jnp.take(returned, inverse, axis=0)
    grad_returned = jnp.take(grad_returned, inverse, axis=0)
    grad_enc_returned = jnp.take(grad_enc_returned, inverse, axis=0)
    return (
        returned,
        grad_returned,
        grad_enc_returned,
        summed[0],
        summed[1],
        summed[2],
        summed[3],
        summed[4],
        summed[5],
        summed[6],
        summed[7],
        summed[8],
        summed[9],
        summed[10],
    )


def solution(mesh):
    placed = (
        P(None, ("dp", "fsdp"), None),
        P(None, ("dp", "fsdp"), None),
        P(None, ("dp", "fsdp"), None),
        P(),
        P(),
        P(),
        P(None, ("dp", "fsdp"), None),
        P(("dp", "fsdp"), None),
        P(None, ("dp", "fsdp"), None),
        P(("dp", "fsdp"), None),
        P(("dp", "fsdp"), None),
        P(("dp", "fsdp"), None),
        P(None, ("dp", "fsdp")),
        P(("dp", "fsdp")),
        P(("dp", "fsdp")),
        P(None, ("dp", "fsdp")),
        P(None, ("dp", "fsdp")),
    )
    return jax.shard_map(
        per_device,
        mesh=mesh,
        in_specs=placed,
        out_specs=(
            P(None, ("dp", "fsdp"), None),
            P(None, ("dp", "fsdp"), None),
            P(None, ("dp", "fsdp"), None),
            P(None, ("dp", "fsdp"), None),
            P(("dp", "fsdp"), None),
            P(None, ("dp", "fsdp"), None),
            P(("dp", "fsdp"), None),
            P(("dp", "fsdp"), None),
            P(("dp", "fsdp"), None),
            P(None, ("dp", "fsdp")),
            P(("dp", "fsdp")),
            P(("dp", "fsdp")),
            P(None, ("dp", "fsdp")),
            P(None, ("dp", "fsdp")),
        ),
        check_vma=False,
    )
```

profile of v0, /device:TPU:0, one launch (start us, length us, event | category | flops | bytes accessed | tf_op | source)
XLA Modules:
  0.0 2957.0 jit_solution(6512052173217909079)
XLA Ops:
  20.9 82.9 %all_to_all.63 = bf16[32,32,1024]{2,1,0:T(8,128)(2,1)S(1)} all-to-all(bf16[32,32,1024]{2,1,0:T(8,128)(2,1)S(1)} %get-tuple-element.737), channel_id=1, replica_groups=mesh['dp'=8,'fsdp'=4] {'dp','fsdp'}, dimensions={0} | all-to-all | bytes 4194304 | tf_op jit(solution)/shard_map/all_to_all | solution.py:133
  109.3 101.9 %all-gather.3 = bf16[32,1,128]{2,1,0:T(2,128)(2,1)S(1)} all-gather(bf16[1,1,128]{2,1,0:T(2,128)(2,1)S(1)} %bitcast.471), channel_id=1, replica_groups=mesh['dp'=8,'fsdp'=4] {'dp','fsdp'}, dimensions={0}, use_global_device_ids=true | all-gather | bytes 8448 | tf_op jit(solution)/shard_map/all_gather | solution.py:163
  211.8 64.8 %all-gather = bf16[32,32,3]{1,2,0:T(4,128)(2,1)S(1)} all-gather(bf16[1,32,3]{1,2,0:T(4,128)(2,1)S(1)} %bitcast.469), channel_id=1, replica_groups=mesh['dp'=8,'fsdp'=4] {'dp','fsdp'}, dimensions={0}, use_global_device_ids=true | all-gather | bytes 6336 | tf_op jit(solution)/shard_map/all_gather | solution.py:165
  276.7 64.4 %all-gather.1 = bf16[32,32,3]{1,2,0:T(4,128)(2,1)S(1)} all-gather(bf16[1,32,3]{1,2,0:T(4,128)(2,1)S(1)} %bitcast.470), channel_id=1, replica_groups=mesh['dp'=8,'fsdp'=4] {'dp','fsdp'}, dimensions={0}, use_global_device_ids=true | all-gather | bytes 6336 | tf_op jit(solution)/shard_map/all_gather | solution.py:166
  341.2 66.0 %all-gather.2 = bf16[32,32,6]{1,2,0:T(8,128)(2,1)S(1)} all-gather(bf16[1,32,6]{1,2,0:T(8,128)(2,1)S(1)} %bitcast.468), channel_id=1, replica_groups=mesh['dp'=8,'fsdp'=4] {'dp','fsdp'}, dimensions={0}, use_global_device_ids=true | all-gather | bytes 12672 | tf_op jit(solution)/shard_map/all_gather | solution.py:162
  442.7 103.6 %while.59 = (s32[]{:T(128)}, bf16[2,512,1024]{2,1,0:T(8,128)(2,1)}, f32[2,16,512,1]{2,1,3,0:T(8,128)S(1)}, s32[2]{0:T(128)S(1)}, s32[]{:T(128)}, /*index=5*/bf16...) while((s32[]{:T(128)}, bf16[2,512,1024]{2,1,0:T(8,128)(2,1)}, ...), condition=%wide.region_5.7_spmd.clone.clone, body=%wide.region_2.6_spmd.clone.clone.sunk | while | flops 2224023040 | bytes 124000464 | solution.py:64
  570.6 24.1 while.58
  620.6 24.5 convert_reduce_fusion
  673.2 45.8 %while.60 = (s32[]{:T(128)}, f32[256,16,64]{0,2,1:T(8,128)}, f32[256,16,64]{0,2,1:T(8,128)}, bf16[2,512,1024]{2,1,0:T(8,128)(2,1)}, s32[2]{0:T(128)S(1)}, /*inde...) while((s32[]{:T(128)}, f32[256,16,64]{0,2,1:T(8,128)}, ...), condition=%wide.region_19.22_spmd.clone, body=%wide.region_17.21_spmd.clone.sunk | while | flops 1368383744 | bytes 84640984 | solution.py:100
  742.2 227.1 %while.61 = (s32[]{:T(128)}, f32[1024,16,64]{0,2,1:T(8,128)}, f32[1024,16,64]{0,2,1:T(8,128)}, bf16[2,512,1024]{2,1,0:T(8,128)(2,1)}, s32[2]{0:T(128)S(1)}, /*in...) while((s32[]{:T(128)}, f32[1024,16,64]{0,2,1:T(8,128)}, ...), condition=%wide.region_24.27_spmd.clone.clone, body=%wide.region_22.26_spmd.clone.clone.sunk | while | flops 5474608640 | bytes 334731584 | solution.py:100
  780.1 25.0 multiply_reduce_fusion.12
  805.0 27.8 multiply_convert_fusion.12
  894.0 25.0 multiply_reduce_fusion.12
  919.0 27.8 multiply_convert_fusion.12
  1074.1 41.2 %all-reduce = bf16[1024]{0:T(1024)(128)(2,1)S(1)} all-reduce(bf16[1024]{0:T(1024)(128)(2,1)S(1)} %dynamic-update-slice), channel_id=1, replica_groups=mesh['dp'=8,'fsdp'=4] {'dp','fsdp'}, use_global_device_ids=true, to_apply=%add | all-reduce | flops 1024 | bytes 4096
  1205.5 24.7 all-to-all-done.2
  1238.0 66.3 %all-reduce.3 = (f32[4096]{0:T(1024)S(1)}, f32[1024]{0:T(1024)S(1)}) all-reduce(f32[4096]{0:T(1024)S(1)} %copy-done.60, f32[1024]{0:T(1024)S(1)} %convert_reduce_fusion.2), channel_id=9, replica_groups=mesh['dp'=8,'fsdp'=4] {'dp','fsdp'}, use_global_device_ids=true, to_apply=%region_41.44.clone | all-reduce | flops 5120 | bytes 40960
  1308.2 88.7 %reduce-scatter.28.cloned.1.call-done = f32[32,6]{1,0:T(8,128)} async-done(((f32[1024,6]{1,0:T(8,128)}), f32[32,6]{1,0:T(8,128)}) %reduce-scatter.28.cloned.1.call-update) | async-done | bytes 784
  1443.4 93.9 %reduce-scatter.22.cloned.1.call-done = f32[32,1024]{1,0:T(8,128)} async-done(((f32[1024,1024]{1,0:T(8,128)}), f32[32,1024]{1,0:T(8,128)}) %reduce-scatter.22.cloned.1.call-update) | async-done | bytes 131088 | tf_op jit(solution)/shard_map/reduce_scatter | solution.py:283
  1537.3 142.3 %reduce-scatter.18.cloned.1.call-done = f32[32,1024]{1,0:T(8,128)} async-done(((f32[1024,1024]{1,0:T(8,128)}), f32[32,1024]{1,0:T(8,128)}) %reduce-scatter.18.cloned.1.call-update) | async-done | bytes 131088 | tf_op jit(solution)/shard_map/reduce_scatter | solution.py:281
  1679.7 271.5 %reduce-scatter.20.cloned.1.call-done = f32[3,32,1024]{2,1,0:T(8,128)} async-done(((f32[3,1024,1024]{2,1,0:T(8,128)}), f32[3,32,1024]{2,1,0:T(8,128)}) %reduce-scatter.20.cloned.1.call-update) | async-done | bytes 393232 | tf_op jit(solution)/shard_map/reduce_scatter | solution.py:282
  1951.1 275.0 %reduce-scatter.16.cloned.1.call-done = f32[3,32,1024]{2,1,0:T(8,128)} async-done(((f32[3,1024,1024]{2,1,0:T(8,128)}), f32[3,32,1024]{2,1,0:T(8,128)}) %reduce-scatter.16.cloned.1.call-update) | async-done | bytes 393232 | tf_op jit(solution)/shard_map/reduce_scatter | solution.py:280
  2226.2 362.2 %reduce-scatter.26.cloned.1.call-done = f32[128,1024]{1,0:T(8,128)} async-done(((f32[4096,1024]{1,0:T(8,128)}), f32[128,1024]{1,0:T(8,128)}) %reduce-scatter.26.cloned.1.call-update) | async-done | bytes 524304 | tf_op jit(solution)/shard_map/reduce_scatter | solution.py:285
  2588.3 361.9 %reduce-scatter.24.cloned.1.call-done = f32[32,4096]{1,0:T(8,128)} async-done(((f32[1024,4096]{1,0:T(8,128)}), f32[32,4096]{1,0:T(8,128)}) %reduce-scatter.24.cloned.1.call-update) | async-done | bytes 524304 | tf_op jit(solution)/shard_map/reduce_scatter | solution.py:284
  (479 shorter events, 686.8 us)
Async XLA Ops:
  7.2 416.6 %all-gather.11.cloned.1.call-start = ((), (), s32[]{:S(2)}) async-start(), calls=%async_computation.15 | async-start | bytes 6488064 | tf_op jit(solution)/shard_map/all_gather | solution.py:156
  7.9 538.4 %all-gather.15.cloned.1.call-start = ((), (), s32[]{:S(2)}) async-start(), calls=%async_computation.17 | async-start | bytes 6488064 | tf_op jit(solution)/shard_map/all_gather | solution.py:158
  8.7 545.7 %all-gather.13.cloned.1.call-start = ((), (), s32[]{:S(2)}) async-start(), calls=%async_computation.16 | async-start | bytes 2162688 | tf_op jit(solution)/shard_map/all_gather | solution.py:157
  9.4 585.4 %all-gather.17.cloned.1.call-start = ((), (), s32[]{:S(2)}) async-start(), calls=%async_computation.18 | async-start | bytes 2162688 | tf_op jit(solution)/shard_map/all_gather | solution.py:159
  10.0 593.2 %all-gather.19.cloned.1.call-start = ((), (), s32[]{:S(2)}) async-start(), calls=%async_computation.19 | async-start | bytes 8650752 | tf_op jit(solution)/shard_map/all_gather | solution.py:160
  20.9 320.3 %copy-start.79 = (bf16[6,32]{1,0:T(8,128)(2,1)S(1)}, bf16[6,32]{1,0:T(8,128)(2,1)}, u32[]{:S(2)}) copy-start(bf16[6,32]{1,0:T(8,128)(2,1)} %param.41) | copy-start | bytes 1156
  20.9 386.4 %copy-start.34 = (bf16[32,8,1024]{2,1,0:T(8,128)(2,1)S(1)}, bf16[32,8,1024]{2,1,0:T(8,128)(2,1)}, u32[]{:S(2)}) copy-start(bf16[32,8,1024]{2,1,0:T(8,128)(2,1)} %param.30) | copy-start | bytes 1572868
  103.8 317.8 %copy-start.8 = (bf16[32,32,1024]{2,1,0:T(8,128)(2,1)}, bf16[32,32,1024]{2,1,0:T(8,128)(2,1)S(1)}, u32[]{:S(2)}) copy-start(bf16[32,32,1024]{2,1,0:T(8,128)(2,1)S(1)} %all_to_all.63) | copy-start | bytes 6291460
  103.8 310.6 %all-to-all-start.3 = ((bf16[32,32,1024]{2,1,0:T(8,128)(2,1)}), bf16[32,32,1024]{2,1,0:T(8,128)(2,1)}, u32[]{:S(2)}, u32[]{:S(2)}) async-start(bf16[32,32,1024]{2,1,0:T(8,128)(2,1)} %get-tuple-element.736), calls=%async_computation.3 | async-start | bytes 4194304 | tf_op jit(solution)/shard_map/all_to_all | solution.py:135
  107.5 513.1 %all-gather.21.cloned.1.call-start = ((), (), s32[]{:S(2)}) async-start(), calls=%async_computation.20 | async-start | bytes 8650752 | tf_op jit(solution)/shard_map/all_gather | solution.py:161
  414.4 132.0 %all-to-all-start.1 = ((bf16[32,8,1024]{2,1,0:T(8,128)(2,1)}), bf16[32,8,1024]{2,1,0:T(8,128)(2,1)}, u32[]{:S(2)}, u32[]{:S(2)}) async-start(bf16[32,8,1024]{2,1,0:T(8,128)(2,1)} %broadcast_select_fusion.5), calls=%async_computation.1 | async-start | bytes 1048576 | tf_op jit(solution)/shard_map/all_to_all | solution.py:134
  417.7 887.7 %reduce-scatter.30.cloned.1.call-start = ((), (), s32[]{:S(2)}) async-start(), calls=%async_computation.28 | async-start | bytes 540672
  990.4 316.4 %reduce-scatter.32.cloned.1.call-start = ((), (), s32[]{:S(2)}) async-start(), calls=%async_computation.29 | async-start | bytes 540672
  991.5 405.3 %reduce-scatter.28.cloned.1.call-start = ((), (), s32[]{:S(2)}) async-start(), calls=%async_computation.27 | async-start | bytes 540672
  992.9 544.5 %reduce-scatter.22.cloned.1.call-start = ((), (), s32[]{:S(2)}) async-start(), calls=%async_computation.24 | async-start | bytes 4325376 | tf_op jit(solution)/shard_map/reduce_scatter | solution.py:283
  999.9 679.7 %reduce-scatter.18.cloned.1.call-start = ((), (), s32[]{:S(2)}) async-start(), calls=%async_computation.22 | async-start | bytes 4325376 | tf_op jit(solution)/shard_map/reduce_scatter | solution.py:281
  1007.2 944.0 %reduce-scatter.20.cloned.1.call-start = ((), (), s32[]{:S(2)}) async-start(), calls=%async_computation.23 | async-start | bytes 12976128 | tf_op jit(solution)/shard_map/reduce_scatter | solution.py:282
  1020.2 1206.0 %reduce-scatter.16.cloned.1.call-start = ((), (), s32[]{:S(2)}) async-start(), calls=%async_computation.21 | async-start | bytes 12976128 | tf_op jit(solution)/shard_map/reduce_scatter | solution.py:280
  1035.0 1553.4 %reduce-scatter.26.cloned.1.call-start = ((), (), s32[]{:S(2)}) async-start(), calls=%async_computation.26 | async-start | bytes 17301504 | tf_op jit(solution)/shard_map/reduce_scatter | solution.py:285
  1055.9 1894.4 %reduce-scatter.24.cloned.1.call-start = ((), (), s32[]{:S(2)}) async-start(), calls=%async_computation.25 | async-start | bytes 17301504 | tf_op jit(solution)/shard_map/reduce_scatter | solution.py:284
  1128.0 46.2 %all-to-all-start.5 = ((bf16[32,2,4096]{2,1,0:T(2,128)(2,1)}), bf16[32,2,4096]{2,1,0:T(2,128)(2,1)S(1)}, u32[]{:S(2)}, u32[]{:S(2)}) async-start(bf16[32,2,4096]{2,1,0:T(2,128)(2,1)} %reshape.742), calls=%async_computation.5 | async-start | bytes 1048576 | tf_op jit(solution)/shard_map/all_to_all | solution.py:298
  1174.2 56.0 %all-to-all-start.2 = ((bf16[32,2,16384]{2,1,0:T(2,128)(2,1)}), bf16[32,2,16384]{2,1,0:T(2,128)(2,1)}, u32[]{:S(2)}, u32[]{:S(2)}) async-start(bf16[32,2,16384]{2,1,0:T(2,128)(2,1)} %reshape.738), calls=%async_computation.2 | async-start | bytes 4194304 | tf_op jit(solution)/shard_map/all_to_all | solution.py:296
  1230.2 193.7 %all-to-all-start.4 = ((bf16[32,2,16384]{2,1,0:T(2,128)(2,1)}), bf16[32,2,16384]{2,1,0:T(2,128)(2,1)S(1)}, u32[]{:S(2)}, u32[]{:S(2)}) async-start(bf16[32,2,16384]{2,1,0:T(2,128)(2,1)} %reshape.740), calls=%async_computation.4 | async-start | bytes 4194304 | tf_op jit(solution)/shard_map/all_to_all | solution.py:297
  1435.0 1515.2 %copy-start.1 = (bf16[32,32,1024]{2,1,0:T(8,128)(2,1)S(1)}, bf16[32,32,1024]{2,1,0:T(8,128)(2,1)}, u32[]{:S(2)}) copy-start(bf16[32,32,1024]{2,1,0:T(8,128)(2,1)} %param.31) | copy-start | bytes 6291460
  (91 other events, 1530.4 us)
Sparse Core Ops, SparseCore 0:
  11.0 92.5 all-gather.10
  106.4 83.2 all-gather.14
  192.6 54.8 all-gather.12
  250.2 55.2 all-gather.16
  308.2 76.8 all-gather.18
  387.8 83.6 all-gather.20
  990.5 135.4 reduce-scatter.29
  1128.3 135.7 reduce-scatter.31
  1266.3 130.4 reduce-scatter.27
  1399.6 137.6 reduce-scatter.21
  1540.3 139.3 reduce-scatter.17
  1682.5 268.6 reduce-scatter.19
  1954.1 271.9 reduce-scatter.15
  2229.0 359.3 reduce-scatter.25
  2591.2 359.0 reduce-scatter.23
where the time goes:
time: 2960 us
  waiting for transfers between devices  1620 us (55%)
  blocking collectives  487 us (16%)
  matrix products  441 us (15%)
  other arithmetic  195 us (7%)
  local copies, waits for them, and re-layouts  153 us (5%)
    reduce_scatter x1, waiting for transfers between devices, per_device(): lax.psum_scatter(grad_down, ('dp', 'fsdp'), scatter_dimension=0, tiled=True)  362 us
    reduce_scatter x1, waiting for transfers between devices, per_device(): lax.psum_scatter(grad_up, ('dp', 'fsdp'), scatter_dimension=0, tiled=True)  362 us
    reduce_scatter x1, waiting for transfers between devices, per_device(): lax.psum_scatter(grad_self_qkv, ('dp', 'fsdp'), scatter_dimension=1, tile...  275 us
    reduce_scatter x1, waiting for transfers between devices, per_device(): lax.psum_scatter(grad_cross_qkv, ('dp', 'fsdp'), scatter_dimension=1, til...  271 us
    reduce_scatter x1, waiting for transfers between devices, per_device(): lax.psum_scatter(grad_self_out, ('dp', 'fsdp'), scatter_dimension=0, tile...  142 us
    unnamed x2, blocking collectives  107 us
    all_gather x1, blocking collectives, per_device(): lax.all_gather(ffn_bias_up, ('dp', 'fsdp'), axis=0, tiled=True)  102 us
    reduce_scatter x1, waiting for transfers between devices, per_device(): lax.psum_scatter(grad_cross_out, ('dp', 'fsdp'), scatter_dimension=0, til...  93.9 us
  transfers between devices with their start and end apart: 20, of which 8 were waited for; matrix products, arithmetic and copies ran while one was open for 14% of the time, Pallas kernels for 0%

commit v1 on v0

--- a/solution.py
+++ b/solution.py
@@ -1,9 +1,368 @@
+import functools
+
 import jax
 import jax.numpy as jnp
 from jax import lax
+from jax.experimental import pallas as pl
+from jax.experimental.pallas import tpu as pltpu
 from jax.sharding import PartitionSpec as P
 
 HD = 64
+MESH = pl.DeviceIdType.MESH
+ANY = pl.BlockSpec(memory_space=pl.ANY)
+
+
+def ring_place(f, ring):
+    half = ring // 2
+    upper, rest = f // half, f % half
+    return upper * half + rest + upper * (half - 1 - 2 * rest)
+
+
+def position(depth, ring):
+    d, f = lax.axis_index("dp"), lax.axis_index("fsdp")
+    return d // 2, d % 2, ring_place(f, ring), f
+
+
+def greet(z, c, right, left, depth, f):
+    barrier = pltpu.get_barrier_semaphore()
+
+    def hail(d, g):
+        pl.semaphore_signal(barrier, inc=1, device_id=(d, g), device_id_type=MESH)
+
+    for s in range(1, depth):
+        hail((z + s) % depth * 2 + c, f)
+    hail(z * 2 + c, right)
+    hail(z * 2 + c, left)
+    hail(z * 2 + 1 - c, f)
+    pl.semaphore_wait(barrier, depth + 2)
+
+
+def gather_kernel(depth, ring, units, n_in, *refs):
+    shards, fulls = refs[:n_in], refs[n_in : 2 * n_in]
+    local_sem, z_send, z_recv, r_send, r_recv, c_send, c_recv = refs[2 * n_in :]
+    half = ring // 2
+    z, c, place, f = position(depth, ring)
+    right = ring_place((place + 1) % ring, ring)
+    left = ring_place((place + ring - 1) % ring, ring)
+    greet(z, c, right, left, depth, f)
+
+    def own(u):
+        which, lead, rows, cols = units[u]
+        return shards[which].at[lead, rows, cols]
+
+    def chunk(u, zs, cc, g):
+        which, lead, rows, cols = units[u]
+        return fulls[which].at[lead, zs, cc, g, rows, cols]
+
+    def remote(src, dst, send, recv, d, g):
+        return pltpu.make_async_remote_copy(
+            src_ref=src, dst_ref=dst, send_sem=send, recv_sem=recv,
+            device_id=(d, g), device_id_type=MESH,
+        )
+
+    def kept(u):
+        return pltpu.make_async_copy(own(u), chunk(u, z, c, f), local_sem.at[u])
+
+    def z_out(u, s):
+        return remote(own(u), chunk(u, z, c, f), z_send.at[u, s], z_recv.at[u, s],
+                      (z + s) % depth * 2 + c, f)
+
+    def z_in(u, s):
+        src = (z + depth - s) % depth
+        return remote(own(u), chunk(u, src, c, f), z_send.at[u, s], z_recv.at[u, s],
+                      (z + s) % depth * 2 + c, f)
+
+    all_z, low_z, high_z = slice(0, depth), slice(0, depth // 2), slice(depth // 2, depth)
+
+    def zs_of(t, way):
+        return all_z if t < half else (low_z, high_z)[way]
+
+    def ring_copy(u, t, way, incoming):
+        back = t - 1 + incoming
+        origin = (place + ring - back) % ring if way == 0 else (place + back) % ring
+        piece = chunk(u, zs_of(t, way), c, ring_place(origin, ring))
+        return remote(piece, piece, r_send.at[u, t - 1, way], r_recv.at[u, t - 1, way],
+                      z * 2 + c, (right, left)[way])
+
+    def core_copy(u, origin, slot, cc):
+        piece = chunk(u, all_z, cc, ring_place(origin % ring, ring))
+        return remote(piece, piece, c_send.at[u, slot], c_recv.at[u, slot], z * 2 + 1 - c, f)
+
+    def start_z(u):
+        kept(u).start()
+        for s in range(1, depth):
+            z_out(u, s).start()
+
+    def end_z(u):
+        kept(u).wait()
+        for s in range(1, depth):
+            z_in(u, s).wait_recv()
+
+    def start_ring(u, t):
+        for way in range(2):
+            ring_copy(u, t, way, 0).start()
+
+    def end_ring(u, t):
+        for way in range(2):
+            ring_copy(u, t, way, 1).wait_recv()
+
+    def sets_after(t):
+        if t == 0:
+            return [0]
+        return [t] if t == half else [ring - t, t]
+
+    def start_core(u, t):
+        for shift in sets_after(t):
+            core_copy(u, place + shift, shift, c).start()
+
+    count = len(units)
+    ahead = 2
+    for u in range(min(ahead, count)):
+        start_z(u)
+    for i in range(count + half):
+        if i + ahead < count:
+            start_z(i + ahead)
+        if i < count:
+            end_z(i)
+            start_ring(i, 1)
+            start_core(i, 0)
+        for t in range(1, half + 1):
+            u = i - t
+            if 0 <= u < count:
+                end_ring(u, t)
+                if t < half:
+                    start_ring(u, t + 1)
+                start_core(u, t)
+    for u in range(count):
+        for s in range(1, depth):
+            z_out(u, s).wait_send()
+        for t in range(1, half + 1):
+            for way in range(2):
+                ring_copy(u, t, way, 0).wait_send()
+        for shift in range(ring):
+            core_copy(u, place + shift, shift, c).wait_send()
+            core_copy(u, place + shift, shift, 1 - c).wait_recv()
+
+
+def gather_weights(mesh, shards, units, ident):
+    depth, ring = mesh.shape["dp"] // 2, mesh.shape["fsdp"]
+    n = len(units)
+    half = ring // 2
+    dma = pltpu.SemaphoreType.DMA
+    return pl.pallas_call(
+        functools.partial(gather_kernel, depth, ring, units, len(shards)),
+        out_shape=[
+            jax.ShapeDtypeStruct((a.shape[0], depth, 2, ring) + a.shape[1:], a.dtype)
+            for a in shards
+        ],
+        in_specs=[ANY] * len(shards),
+        out_specs=[ANY] * len(shards),
+        scratch_shapes=[
+            dma((n,)),
+            dma((n, depth)),
+            dma((n, depth)),
+            dma((n, half, 2)),
+            dma((n, half, 2)),
+            dma((n, ring)),
+            dma((n, ring)),
+        ],
+        compiler_params=pltpu.CompilerParams(collective_id=ident, has_side_effects=True),
+        cost_estimate=pl.CostEstimate(flops=120_000_000_000, bytes_accessed=2 * 33_554_432, transcendentals=0),
+        name="gather_weights",
+    )(*shards)
+
+
+def scatter_kernel(depth, ring, units, n_in, *refs):
+    fulls, outs = refs[:n_in], refs[n_in : 2 * n_in]
+    mine, theirs, rhalf, rfull, zbuf = refs[2 * n_in : 2 * n_in + 5]
+    l_sem, c_send, c_recv, r_send, r_recv, z_send, z_recv = refs[2 * n_in + 5 :]
+    half = ring // 2
+    hz = depth // 2
+    z, c, place, f = position(depth, ring)
+    right = ring_place((place + 1) % ring, ring)
+    left = ring_place((place + ring - 1) % ring, ring)
+    greet(z, c, right, left, depth, f)
+    count = len(units)
+
+    def chunk(u, cc):
+        which, lead, rows, cols = units[u]
+        return fulls[which].at[lead, slice(0, depth), cc, slice(0, ring), rows, cols]
+
+    def remote(src, dst, send, recv, d, g):
+        return pltpu.make_async_remote_copy(
+            src_ref=src, dst_ref=dst, send_sem=send, recv_sem=recv,
+            device_id=(d, g), device_id_type=MESH,
+        )
+
+    def load(u):
+        return pltpu.make_async_copy(chunk(u, c), mine.at[u], l_sem.at[u])
+
+    def core(u):
+        return remote(chunk(u, 1 - c), theirs.at[u], c_send.at[u], c_recv.at[u], z * 2 + 1 - c, f)
+
+    def dest(t, way):
+        ahead = half - t + 1
+        return ring_place((place + ahead) % ring if way == 0 else (place + ring - ahead) % ring, ring)
+
+    def ring_copy(u, t, way):
+        g = dest(t, way)
+        if t == 1:
+            src = mine.at[u, slice(0, hz) if way == 0 else slice(hz, depth), g]
+            dst = rhalf.at[u, way]
+        else:
+            src = mine.at[u, slice(0, depth), g]
+            dst = rfull.at[u, t - 2, way]
+        return remote(src, dst, r_send.at[u, t - 1, way], r_recv.at[u, t - 1, way],
+                      z * 2 + c, (right, left)[way])
+
+    def z_copy(u, s):
+        to = (z + s) % depth
+        return remote(mine.at[u, to, f], zbuf.at[u, s - 1], z_send.at[u, s], z_recv.at[u, s],
+                      to * 2 + c, f)
+
+    def first_sum(u):
+        core(u).wait_recv()
+        load(u).wait()
+
+        def body(i, carry):
+            a, g = i // ring, i % ring
+            mine[u, a, g] = (
+                mine[u, a, g].astype(jnp.float32) + theirs[u, a, g].astype(jnp.float32)
+            ).astype(mine.dtype)
+            return carry
+
+        lax.fori_loop(0, depth * ring, body, 0)
+        for way in range(2):
+            ring_copy(u, 1, way).start()
+
+    def next_sum(u, t):
+        for way in range(2):
+            ring_copy(u, t, way).wait_recv()
+        if t < half:
+            for way in range(2):
+                g = dest(t + 1, way)
+                low = hz * way if t == 1 else 0
+                many = hz if t == 1 else depth
+                src = rhalf.at[u, way] if t == 1 else rfull.at[u, t - 2, way]
+
+                def body(i, carry, g=g, low=low, src=src):
+                    mine[u, low + i, g] = (
+                        mine[u, low + i, g].astype(jnp.float32) + src[i].astype(jnp.float32)
+                    ).astype(mine.dtype)
+                    return carry
+
+                lax.fori_loop(0, many, body, 0)
+                ring_copy(u, t + 1, way).start()
+        else:
+            one, two = rfull.at[u, t - 2, 0], rfull.at[u, t - 2, 1]
+
+            def body(i, carry):
+                mine[u, i, f] = (
+                    mine[u, i, f].astype(jnp.float32)
+                    + one[i].astype(jnp.float32)
+                    + two[i].astype(jnp.float32)
+                ).astype(mine.dtype)
+                return carry
+
+            lax.fori_loop(0, depth, body, 0)
+            for s in range(1, depth):
+                z_copy(u, s).start()
+
+    def last_sum(u):
+        for s in range(1, depth):
+            z_copy(u, s).wait_recv()
+        which, lead, rows, cols = units[u]
+        total = mine[u, z, f].astype(jnp.float32)
+        for s in range(1, depth):
+            total = total + zbuf[u, s - 1].astype(jnp.float32)
+        outs[which][lead, rows, cols] = total
+
+    for u in range(count):
+        core(u).start()
+        load(u).start()
+    for i in range(count + half + 1):
+        if i < count:
+            first_sum(i)
+        for t in range(1, half + 1):
+            u = i - t
+            if 0 <= u < count:
+                next_sum(u, t)
+        u = i - half - 1
+        if 0 <= u < count:
+            last_sum(u)
+    for u in range(count):
+        core(u).wait_send()
+        for t in range(1, half + 1):
+            for way in range(2):
+                ring_copy(u, t, way).wait_send()
+        for s in range(1, depth):
+            z_copy(u, s).wait_send()
+
+
+def scatter_grads(mesh, fulls, units, ident):
+    depth, ring = mesh.shape["dp"] // 2, mesh.shape["fsdp"]
+    n = len(units)
+    half = ring // 2
+    hz = depth // 2
+    dma = pltpu.SemaphoreType.DMA
+    low = fulls[0].dtype
+    rows = fulls[0].shape[-2]
+    cols = fulls[0].shape[-1]
+    vm = pl.BlockSpec(memory_space=pltpu.VMEM)
+    return pl.pallas_call(
+        functools.partial(scatter_kernel, depth, ring, units, len(fulls)),
+        out_shape=[jax.ShapeDtypeStruct((a.shape[0],) + a.shape[4:], jnp.float32) for a in fulls],
+        in_specs=[ANY] * len(fulls),
+        out_specs=[vm] * len(fulls),
+        scratch_shapes=[
+            pltpu.VMEM((n, depth, ring, rows, cols), low),
+            pltpu.VMEM((n, depth, ring, rows, cols), low),
+            pltpu.VMEM((n, 2, hz, rows, cols), low),
+            pltpu.VMEM((n, half - 1, 2, depth, rows, cols), low),
+            pltpu.VMEM((n, depth - 1, rows, cols), low),
+            dma((n,)),
+            dma((n,)),
+            dma((n,)),
+            dma((n, half, 2)),
+            dma((n, half, 2)),
+            dma((n, depth)),
+            dma((n, depth)),
+        ],
+        compiler_params=pltpu.CompilerParams(
+            collective_id=ident, has_side_effects=True, vmem_limit_bytes=60 * 2**20
+        ),
+        name="scatter_grads",
+    )(*fulls)
+
+
+def units_of(shards):
+    base = shards[0].shape[1]
+    wide = shards[0].shape[2]
+    found = []
+    for which, (lead, rows, cols) in enumerate(a.shape for a in shards):
+        for l in range(lead):
+            for r in range(rows // base):
+                for k in range(cols // wide):
+                    found.append((which, l, slice(r * base, (r + 1) * base), slice(k * wide, (k + 1) * wide)))
+    return tuple(found)
+
+
+def packed(parts):
+    flat = jnp.concatenate([p.reshape(-1) for p in parts])
+    size = -(-flat.shape[0] // 2048) * 2048
+    return jnp.pad(flat, (0, size - flat.shape[0])).reshape(1, size // 128, 128)
+
+
+def unpacked(flat, shapes):
+    parts, at = [], 0
+    for shape in shapes:
+        size = 1
+        for d in shape:
+            size *= d
+        part = flat[:, at : at + size].reshape((-1,) + shape)
+        parts.append(jnp.moveaxis(part, 0, -2).reshape(shape[:-1] + (-1,)))
+        at += size
+    return parts
 
 
 EPSILON = 1e-05
@@ -106,6 +465,7 @@
 
 
 def per_device(
+    mesh,
     units,
     encoder,
     cotangent,
@@ -152,27 +512,17 @@
     def across(start, block):
         return jnp.broadcast_to(enc_positions[None, :] < enc_count, (block, enc_positions.shape[0]))
 
-    weights = (
-        lax.all_gather(self_qkv, ("dp", "fsdp"), axis=1, tiled=True),
-        lax.all_gather(self_out, ("dp", "fsdp"), axis=0, tiled=True),
-        lax.all_gather(cross_qkv, ("dp", "fsdp"), axis=1, tiled=True),
-        lax.all_gather(cross_out, ("dp", "fsdp"), axis=0, tiled=True),
-        lax.all_gather(ffn_up, ("dp", "fsdp"), axis=0, tiled=True),
-        lax.all_gather(ffn_down, ("dp", "fsdp"), axis=0, tiled=True),
-        lax.all_gather(biases, ("dp", "fsdp"), axis=1, tiled=True),
-        lax.all_gather(ffn_bias_up, ("dp", "fsdp"), axis=0, tiled=True),
-        lax.all_gather(ffn_bias_down, ("dp", "fsdp"), axis=0, tiled=True),
-        lax.all_gather(norm_gain, ("dp", "fsdp"), axis=1, tiled=True),
-        lax.all_gather(norm_shift, ("dp", "fsdp"), axis=1, tiled=True),
-    )
+    big = [self_qkv, self_out[None], cross_qkv, cross_out[None], ffn_up[None], ffn_down[None]]
+    units_list = units_of(big)
+    small = (biases, ffn_bias_up, ffn_bias_down, norm_gain, norm_shift)
+    little = packed(small)
+    little_unit = ((len(big), 0, slice(0, little.shape[1]), slice(0, 128)),)
+    gathered = gather_weights(mesh, big + [little], little_unit + units_list, 0)
     s_qkv, s_out, c_qkv, c_out, w_up, w_down = (
-        weights[0],
-        weights[1],
-        weights[2],
-        weights[3],
-        weights[4],
-        weights[5],
-    )
+        g.reshape(g.shape[0], -1, g.shape[-1]) for g in gathered[:6]
+    )
+    s_out, c_out, w_up, w_down = s_out[0], c_out[0], w_up[0], w_down[0]
+    weights = [None] * 6 + unpacked(gathered[6].reshape(slots, -1), [p.shape for p in small])
     bias_rows = weights[6].astype(jnp.float32)
     bias_up = weights[7].astype(jnp.float32)
     bias_down = weights[8].astype(jnp.float32)
@@ -195,27 +545,6 @@
     activated, pull_gate = jax.vjp(smooth_gate, before)
     hidden = activated.astype(jnp.bfloat16)
     result = (second + (product(hidden, w_down) + bias_down)) * valid
-    regathered = (
-        lax.all_gather(self_qkv, ("dp", "fsdp"), axis=1, tiled=True),
-        lax.all_gather(self_out, ("dp", "fsdp"), axis=0, tiled=True),
-        lax.all_gather(cross_qkv, ("dp", "fsdp"), axis=1, tiled=True),
-        lax.all_gather(cross_out, ("dp", "fsdp"), axis=0, tiled=True),
-        lax.all_gather(ffn_up, ("dp", "fsdp"), axis=0, tiled=True),
-        lax.all_gather(ffn_down, ("dp", "fsdp"), axis=0, tiled=True),
-        lax.all_gather(biases, ("dp", "fsdp"), axis=1, tiled=True),
-        lax.all_gather(ffn_bias_up, ("dp", "fsdp"), axis=0, tiled=True),
-        lax.all_gather(ffn_bias_down, ("dp", "fsdp"), axis=0, tiled=True),
-        lax.all_gather(norm_gain, ("dp", "fsdp"), axis=1, tiled=True),
-        lax.all_gather(norm_shift, ("dp", "fsdp"), axis=1, tiled=True),
-    )
-    s_qkv, s_out, c_qkv, c_out, w_up, w_down = (
-        regathered[0],
-        regathered[1],
-        regathered[2],
-        regathered[3],
-        regathered[4],
-        regathered[5],
-    )
     branch = grad_out.astype(jnp.bfloat16)
     grad_down = product_tn(hidden, branch)
     grad_bias_down = column_sum(branch)
@@ -276,19 +605,30 @@
     )
     grad_gains = jnp.stack([grad_gain_zero, grad_gain_one, grad_gain_two])
     grad_shifts = jnp.stack([grad_shift_zero, grad_shift_one, grad_shift_two])
-    summed = (
-        lax.psum_scatter(grad_self_qkv, ("dp", "fsdp"), scatter_dimension=1, tiled=True),
-        lax.psum_scatter(grad_self_out, ("dp", "fsdp"), scatter_dimension=0, tiled=True),
-        lax.psum_scatter(grad_cross_qkv, ("dp", "fsdp"), scatter_dimension=1, tiled=True),
-        lax.psum_scatter(grad_cross_out, ("dp", "fsdp"), scatter_dimension=0, tiled=True),
-        lax.psum_scatter(grad_up, ("dp", "fsdp"), scatter_dimension=0, tiled=True),
-        lax.psum_scatter(grad_down, ("dp", "fsdp"), scatter_dimension=0, tiled=True),
-        lax.psum_scatter(grad_biases, ("dp", "fsdp"), scatter_dimension=1, tiled=True),
-        lax.psum_scatter(grad_bias_up, ("dp", "fsdp"), scatter_dimension=0, tiled=True),
-        lax.psum_scatter(grad_bias_down, ("dp", "fsdp"), scatter_dimension=0, tiled=True),
-        lax.psum_scatter(grad_gains, ("dp", "fsdp"), scatter_dimension=1, tiled=True),
-        lax.psum_scatter(grad_shifts, ("dp", "fsdp"), scatter_dimension=1, tiled=True),
-    )
+    low = jnp.bfloat16
+    depth, ring = mesh.shape["dp"] // 2, mesh.shape["fsdp"]
+
+    def cut(g):
+        g = g if g.ndim == 3 else g[None]
+        return g.astype(low).reshape(g.shape[0], depth, 2, ring, -1, g.shape[-1])
+
+    big_grads = [cut(g) for g in (grad_self_qkv, grad_self_out, grad_cross_qkv, grad_cross_out, grad_up, grad_down)]
+    sums = scatter_grads(mesh, big_grads, units_list, 1)
+    small_grads = (grad_biases, grad_bias_up, grad_bias_down, grad_gains, grad_shifts)
+    terms = jnp.concatenate(
+        [
+            jnp.moveaxis(g.reshape(g.shape[:-1] + (slots, -1)), -2, 0).reshape(slots, -1)
+            for g in small_grads
+        ],
+        axis=1,
+    )
+    terms = lax.all_to_all(terms, ("dp", "fsdp"), split_axis=0, concat_axis=0, tiled=True)
+    flat = jnp.sum(terms, axis=0)
+    small_sums, at = [], 0
+    for p in small:
+        small_sums.append(flat[at : at + p.size].reshape(p.shape))
+        at += p.size
+    summed = (sums[0], sums[1][0], sums[2], sums[3][0], sums[4][0], sums[5][0], *small_sums)
     leaving = result.astype(jnp.bfloat16)[None]
     grad_leaving = grad_states.astype(jnp.bfloat16)[None]
     grad_enc_leaving = grad_memory.astype(jnp.bfloat16)[None]
@@ -339,7 +679,7 @@
         P(None, ("dp", "fsdp")),
     )
     return jax.shard_map(
-        per_device,
+        functools.partial(per_device, mesh),
         mesh=mesh,
         in_specs=placed,
         out_specs=(

time: 2960 us -> 1250 us (0.42)
  waiting for transfers between devices: 1620 us -> 19.9 us
  blocking collectives: 487 us -> 0 us
  Pallas kernels: 0 us -> 360 us
    reduce_scatter x6 -> x0, waiting for transfers between devices: 1510 us -> none  [the longest x1 362 us: per_device(): lax.psum_scatter(grad_down, ('dp', 'fsdp'), scatter_dimension=0, tiled=True)]
    pallas_call x0 -> x2, Pallas kernels: none -> 360 us  [the longest x1 201 us: gather_weights(): pl.pallas_call(functools.partial(gather_kernel, depth, ring, units, len(s...]
    all_gather x4 -> x0, blocking collectives: 297 us -> none  [the longest x1 102 us: per_device(): lax.all_gather(ffn_bias_up, ('dp', 'fsdp'), axis=0, tiled=True)]
    unnamed x2 -> x0, blocking collectives: 107 us -> none
    unnamed x18 -> x0, waiting for transfers between devices: 92.5 us -> none
    all_to_all x1 -> x0, blocking collectives: 82.9 us -> none  [per_device(): lax.all_to_all(dealt_units, ('dp', 'fsdp'), split_axis=0, concat_axis=1,...]
    unnamed x196 -> x231, local copies, waits for them, and re-layouts: 66.7 us -> 57.4 us
  transfers between devices with their start and end apart: 20 -> 7, of which waited for: 8 -> 2; matrix products, arithmetic and copies ran while one was open for 14% -> 17% of each run, Pallas kernels for 0% -> 29%
where the time goes in v1:
time: 1250 us; the launch traced here: 1240 us
  matrix products  436 us (35%)
  Pallas kernels  360 us (29%)
  other arithmetic  198 us (16%)
  local copies, waits for them, and re-layouts  174 us (14%)
  starting transfers between devices  38.3 us (3%)
  waiting for transfers between devices  19.9 us (2%)
  loops' own time  17.2 us (1%)
    pallas_call x1, Pallas kernels, gather_weights(): pl.pallas_call(functools.partial(gather_kernel, depth, ring, units, len(s...  201 us
    pallas_call x1, Pallas kernels, scatter_grads(): pl.pallas_call(functools.partial(scatter_kernel, depth, ring, units, len(...  158 us
    dot_general x10, matrix products, product_nt(): lax.dot_general(left, right, (((1,), (1,)), ((), ())), preferred_element_...  77.2 us
    dot_general x10, matrix products, product_tn(): lax.dot_general(left, right, (((0,), (0,)), ((), ())), preferred_element_...  62.9 us
    convert_element_type x4, other arithmetic, one_block(): grad_scores = (probs * (grad_probs - inner)).astype(jnp.bfloat16)  61.4 us
    dot_general x10, matrix products, product(): return jnp.dot(left, right, preferred_element_type=jnp.float32)  61.3 us
    dot_general x8, matrix products, one_block(): jnp.einsum('qhd,khd->hqk', query3, keys3, preferred_element_type=jnp.floa...  59.1 us
    unnamed x231, local copies, waits for them, and re-layouts  57.4 us
  transfers between devices with their start and end apart: 7, of which 2 were waited for; matrix products, arithmetic and copies ran while one was open for 17% of the time, Pallas kernels for 29%

profile of v1, /device:TPU:0, one launch (start us, length us, event | category | flops | bytes accessed | tf_op | source)
XLA Modules:
  0.0 1244.8 jit_solution(9534159552727408206)
XLA Ops:
  31.0 201.2 %gather_weights.1 = (bf16[3,4,2,4,32,1024]{5,4,3,2,1,0:T(8,128)(2,1)}, bf16[1,4,2,4,32,1024]{5,4,3,2,1,0:T(8,128)(2,1)}, bf16[3,4,2,4,32,1024]{5,4,3,2,1,0:T(8,1...) custom-call(bf16[3,32,1024]{2,1,0:T(8,128)(2,1)} %refs_0_.1, ...), custom_call_target="tpu_custom_call" | custom-call | flops 120000004096 | bytes 67108864 | tf_op jit(solution)/shard_map/gather_weights/pallas_call | solution.py:152
  270.9 16.4 %all-to-all-done.3 = bf16[32,32,1024]{2,1,0:T(8,128)(2,1)} async-done(((bf16[32,32,1024]{2,1,0:T(8,128)(2,1)}), bf16[32,32,1024]{2,1,0:T(8,128)(2,1)}, u32[]{:S(2)}, u32[]{:S(2)}) %all-to-all-start.3) | async-done | bytes 2097184 | tf_op jit(solution)/shard_map/all_to_all | solution.py:495
  308.8 103.0 %while.59 = (s32[]{:T(128)}, bf16[2,512,1024]{2,1,0:T(8,128)(2,1)}, f32[2,16,512,1]{2,1,3,0:T(8,128)S(1)}, s32[2]{0:T(128)S(1)}, s32[]{:T(128)}, /*index=5*/bf16...) while((s32[]{:T(128)}, bf16[2,512,1024]{2,1,0:T(8,128)(2,1)}, ...), condition=%wide.region_5.7_spmd.clone.clone, body=%wide.region_2.6_spmd.clone.clone.sunk | while | flops 2224023040 | bytes 124000464 | solution.py:423
  315.0 13.3 %select_reduce_fusion.5 = (f32[16,512]{1,0:T(8,128)S(1)}, f32[16,512,1024]{2,1,0:T(8,128)}) fusion(pred[512,1024]{1,0:T(8,128)(4,1)S(1)} %fusion.216, bf16[512,16,64]{0,2,1:T(8,128)(2,1)S(1)} %bitcast.367, bf16[1024,16,64]{0,2,1:T(8,128)(2,1)S(1)} %get-tuple-element.1026), kind=kOutput, calls=%fused_computation.23.clone.1 | convolution fusion | flops 1090510848 | bytes 37257216 | tf_op jit(solution)/shard_map/while/body/eval_jaxpr/qhd,khd->hqk/dot_general | solution.py:413
  328.3 14.7 %fusion.217 = f32[16,512]{1,0:T(8,128)S(1)} fusion(f32[16,512,1024]{2,1,0:T(8,128)} %get-tuple-element.970, f32[16,512]{1,0:T(8,128)S(1)} %get-tuple-element.971, pred[512,1024]{1,0:T(8,128)(4,1)S(1)} %fusion.216), kind=kLoop, calls=%fused_computation.24.clone.1 | loop fusion | flops 25157632 | bytes 34144256 | tf_op jit(solution)/shard_map/while/body/eval_jaxpr/reduce_sum | solution.py:417
  343.0 14.8 %fusion.218 = bf16[16,512,64]{1,2,0:T(8,128)(2,1)} fusion(bf16[1024,16,64]{0,2,1:T(8,128)(2,1)S(1)} %copy-done.8, f32[16,512,1024]{2,1,0:T(8,128)} %get-tuple-element.970, f32[16,512]{1,0:T(8,128)S(1)} %fusion.217, f32[16,512]{1,0:T(8,128)S(1)} %get-tuple-element.971, pred[512,1024]{1,0:T(8,128)(4,1)S(1)} %fusion.216), kind=kOutput, calls=%fused_computation.25.clone.1 | convolution fusion | flops 1107296256 | bytes 37289984 | tf_op jit(solution)/shard_map/while/body/eval_jaxpr/hqk,khd->qhd/dot_general | solution.py:419
  366.4 13.3 %select_reduce_fusion.5 = (f32[16,512]{1,0:T(8,128)S(1)}, f32[16,512,1024]{2,1,0:T(8,128)}) fusion(pred[512,1024]{1,0:T(8,128)(4,1)S(1)} %fusion.216, bf16[512,16,64]{0,2,1:T(8,128)(2,1)S(1)} %bitcast.367, bf16[1024,16,64]{0,2,1:T(8,128)(2,1)S(1)} %get-tuple-element.1026), kind=kOutput, calls=%fused_computation.23.clone.1 | convolution fusion | flops 1090510848 | bytes 37257216 | tf_op jit(solution)/shard_map/while/body/eval_jaxpr/qhd,khd->hqk/dot_general | solution.py:413
  379.7 14.7 %fusion.217 = f32[16,512]{1,0:T(8,128)S(1)} fusion(f32[16,512,1024]{2,1,0:T(8,128)} %get-tuple-element.970, f32[16,512]{1,0:T(8,128)S(1)} %get-tuple-element.971, pred[512,1024]{1,0:T(8,128)(4,1)S(1)} %fusion.216), kind=kLoop, calls=%fused_computation.24.clone.1 | loop fusion | flops 25157632 | bytes 34144256 | tf_op jit(solution)/shard_map/while/body/eval_jaxpr/reduce_sum | solution.py:417
  394.4 14.8 %fusion.218 = bf16[16,512,64]{1,2,0:T(8,128)(2,1)} fusion(bf16[1024,16,64]{0,2,1:T(8,128)(2,1)S(1)} %copy-done.8, f32[16,512,1024]{2,1,0:T(8,128)} %get-tuple-element.970, f32[16,512]{1,0:T(8,128)S(1)} %fusion.217, f32[16,512]{1,0:T(8,128)S(1)} %get-tuple-element.971, pred[512,1024]{1,0:T(8,128)(4,1)S(1)} %fusion.216), kind=kOutput, calls=%fused_computation.25.clone.1 | convolution fusion | flops 1107296256 | bytes 37289984 | tf_op jit(solution)/shard_map/while/body/eval_jaxpr/hqk,khd->qhd/dot_general | solution.py:419
  427.9 24.3 %while.58 = (s32[]{:T(128)}, bf16[2,512,1024]{2,1,0:T(8,128)(2,1)}, f32[2,16,512,1]{2,1,3,0:T(8,128)S(1)}, s32[]{:T(128)}, s32[2]{0:T(128)S(1)}, /*index=5*/bf16...) while((s32[]{:T(128)}, bf16[2,512,1024]{2,1,0:T(8,128)(2,1)}, ...), condition=%wide.region_11.14_spmd.clone, body=%wide.region_8.13_spmd.clone.sunk | while | flops 555737344 | bytes 34866356 | solution.py:423
  471.6 25.0 %convert_reduce_fusion = (f32[4096]{0:T(1024)}, bf16[1024,4096]{1,0:T(8,128)(2,1)}) fusion(f32[1024,4096]{1,0:T(8,128)} %fusion.78, f32[4096]{0:T(1024)S(1)} %copy-done.85, bf16[1024,1024]{1,0:T(8,128)(2,1)S(1)} %bitcast.413, bf16[4096,1024]{1,0:T(8,128)(2,1)} %bitcast.445), kind=kOutput, calls=%fused_computation.80 | convolution fusion | flops 8686399488 | bytes 35684352 | tf_op jit(solution)/shard_map/dot_general | solution.py:395
  496.6 15.4 %multiply_reduce_fusion.2 = (f32[1024]{0:T(1024)S(1)}, f32[1024]{0:T(1024)S(1)}, f32[1024]{0:T(1024)S(1)}, f32[1024,1024]{1,0:T(8,128)S(1)}) fusion(f32[1024,1024]{1,0:T(8,128)} %copy-done.18, f32[1024]{0:T(1024)S(1)} %fusion.69, f32[1024]{0:T(1024)S(1)} %broadcast_multiply_fusion.4, f32[1024]{0:T(1024)S(1)} %copy-done.73, ...), kind=kOutput, calls=%fused_computation.106 | convolution fusion | flops 8598320128 | bytes 25190400 | tf_op jit(solution)/shard_map/dot_general | solution.py:395
  516.5 18.7 %fusion.60 = bf16[1,1024,1024]{2,1,0:T(8,128)(2,1)} fusion(f32[1024,1024]{1,0:T(8,128)} %copy-done.18, f32[1024]{0:T(1024)S(1)} %copy-done.65, f32[1024]{0:T(1024)S(1)} %copy-done.93, bf16[4096,1024]{1,0:T(8,128)(2,1)} %bitcast.446, f32[1024,4096]{1,0:T(8,128)} %fusion.78, f32[4096]{0:T(1024)S(1)} %copy-done.85), kind=kOutput, calls=%fused_computation.135 | convolution fusion | flops 8636071936 | bytes 31481856 | tf_op jit(solution)/shard_map/dot_general | solution.py:385
  543.1 46.0 %while.60 = (s32[]{:T(128)}, f32[256,16,64]{0,2,1:T(8,128)}, f32[256,16,64]{0,2,1:T(8,128)}, bf16[2,512,1024]{2,1,0:T(8,128)(2,1)}, s32[2]{0:T(128)S(1)}, /*inde...) while((s32[]{:T(128)}, f32[256,16,64]{0,2,1:T(8,128)}, ...), condition=%wide.region_19.22_spmd.clone, body=%wide.region_17.21_spmd.clone.sunk | while | flops 1368383744 | bytes 84640984 | solution.py:459
  617.5 227.5 %while.61 = (s32[]{:T(128)}, f32[1024,16,64]{0,2,1:T(8,128)}, f32[1024,16,64]{0,2,1:T(8,128)}, bf16[2,512,1024]{2,1,0:T(8,128)(2,1)}, s32[2]{0:T(128)S(1)}, /*in...) while((s32[]{:T(128)}, f32[1024,16,64]{0,2,1:T(8,128)}, ...), condition=%wide.region_24.27_spmd.clone.clone, body=%wide.region_22.26_spmd.clone.clone.sunk | while | flops 5474608640 | bytes 334731584 | solution.py:459
  639.2 16.2 %bitcast_add_fusion.6 = f32[1024,16,64]{0,2,1:T(8,128)} fusion(f32[1024,16,64]{0,2,1:T(8,128)} %get-tuple-element.1122, bf16[512,16,64]{0,2,1:T(8,128)(2,1)S(1)} %bitcast.357, f32[16,512,1024]{2,1,0:T(8,128)} %fusion.243, f32[16,512]{1,0:T(8,128)S(1)} %dynamic-slice_bitcast_fusion.5, pred[512,1024]{1,0:T(8,128)(4,1)S(1)} %fusion.244, pred[]{:T(512)S(6)} %compare.8), kind=kOutput, calls=%fused_computation.60.clone.1 | convolution fusion | flops 1101004800 | bytes 43548672 | tf_op jit(solution)/shard_map/while/body/eval_jaxpr/hqk,qhd->khd/dot_general | solution.py:443
  655.4 24.9 %multiply_reduce_fusion.12 = (f32[16,512]{1,0:T(8,128)S(1)}, f32[16,512,1024]{2,1,0:T(8,128)}) fusion(f32[16,512,1024]{2,1,0:T(8,128)} %fusion.243, f32[16,512]{1,0:T(8,128)S(1)} %dynamic-slice_bitcast_fusion.5, pred[512,1024]{1,0:T(8,128)(4,1)S(1)} %fusion.244, bf16[512,16,64]{0,2,1:T(8,128)(2,1)S(1)} %bitcast.358, ...), kind=kOutput, calls=%fused_computation.53.clone.1 | convolution fusion | flops 1107288064 | bytes 70844416 | tf_op jit(solution)/shard_map/while/body/eval_jaxpr/qhd,khd->hqk/dot_general | solution.py:446
  680.3 27.8 %multiply_convert_fusion.15 = bf16[16,512,1024]{2,1,0:T(8,128)(2,1)} fusion(f32[16,512,1024]{2,1,0:T(8,128)} %get-tuple-element.996, f32[16,512,1024]{2,1,0:T(8,128)} %fusion.243, f32[16,512]{1,0:T(8,128)S(1)} %get-tuple-element.997, f32[16,512]{1,0:T(8,128)S(1)} %dynamic-slice_bitcast_fusion.5, pred[512,1024]{1,0:T(8,128)(4,1)S(1)} %fusion.244), kind=kLoop, calls=%fused_computation.52.clone.1 | loop fusion | flops 41943040 | bytes 84475904 | tf_op jit(solution)/shard_map/while/body/eval_jaxpr/convert_element_type | solution.py:448
  751.9 17.4 %bitcast_add_fusion.6 = f32[1024,16,64]{0,2,1:T(8,128)} fusion(f32[1024,16,64]{0,2,1:T(8,128)} %get-tuple-element.1122, bf16[512,16,64]{0,2,1:T(8,128)(2,1)S(1)} %bitcast.357, f32[16,512,1024]{2,1,0:T(8,128)} %fusion.243, f32[16,512]{1,0:T(8,128)S(1)} %dynamic-slice_bitcast_fusion.5, pred[512,1024]{1,0:T(8,128)(4,1)S(1)} %fusion.244, pred[]{:T(512)S(6)} %compare.8), kind=kOutput, calls=%fused_computation.60.clone.1 | convolution fusion | flops 1101004800 | bytes 43548672 | tf_op jit(solution)/shard_map/while/body/eval_jaxpr/hqk,qhd->khd/dot_general | solution.py:443
  769.4 24.9 %multiply_reduce_fusion.12 = (f32[16,512]{1,0:T(8,128)S(1)}, f32[16,512,1024]{2,1,0:T(8,128)}) fusion(f32[16,512,1024]{2,1,0:T(8,128)} %fusion.243, f32[16,512]{1,0:T(8,128)S(1)} %dynamic-slice_bitcast_fusion.5, pred[512,1024]{1,0:T(8,128)(4,1)S(1)} %fusion.244, bf16[512,16,64]{0,2,1:T(8,128)(2,1)S(1)} %bitcast.358, ...), kind=kOutput, calls=%fused_computation.53.clone.1 | convolution fusion | flops 1107288064 | bytes 70844416 | tf_op jit(solution)/shard_map/while/body/eval_jaxpr/qhd,khd->hqk/dot_general | solution.py:446
  794.3 27.8 %multiply_convert_fusion.15 = bf16[16,512,1024]{2,1,0:T(8,128)(2,1)} fusion(f32[16,512,1024]{2,1,0:T(8,128)} %get-tuple-element.996, f32[16,512,1024]{2,1,0:T(8,128)} %fusion.243, f32[16,512]{1,0:T(8,128)S(1)} %get-tuple-element.997, f32[16,512]{1,0:T(8,128)S(1)} %dynamic-slice_bitcast_fusion.5, pred[512,1024]{1,0:T(8,128)(4,1)S(1)} %fusion.244), kind=kLoop, calls=%fused_computation.52.clone.1 | loop fusion | flops 41943040 | bytes 84475904 | tf_op jit(solution)/shard_map/while/body/eval_jaxpr/convert_element_type | solution.py:448
  955.1 14.1 %reduce.64 = bf16[1024,1024]{1,0:T(8,128)(2,1)} reduce(bf16[1024,1,1024]{2,1,0:T(2,128)(2,1)} %bitcast.372, bf16[]{:T(256)} %broadcast.542), dimensions={1}, to_apply=%bitcast.258.reduce_sub_computation | reduce | bytes 4194306
  1020.5 18.4 %convolution_convert_fusion = bf16[4096,1024]{1,0:T(8,128)(2,1)} fusion(bf16[1024,1024]{1,0:T(8,128)(2,1)S(1)} %copy-done.41, f32[1024,4096]{1,0:T(8,128)} %fusion.78, f32[4096]{0:T(1024)S(1)} %copy-done.86), kind=kOutput, calls=%fused_computation.82 | convolution fusion | flops 8636071936 | bytes 27279360 | tf_op jit(solution)/shard_map/dot_general | solution.py:389
  1038.9 158.3 %scatter_grads.1 = (f32[3,32,1024]{2,1,0:T(8,128)}, f32[1,32,1024]{2,1,0:T(8,128)}, f32[3,32,1024]{2,1,0:T(8,128)}, f32[1,32,1024]{2,1,0:T(8,128)}, f32[1,32,4096]{2,1,0:T(8,128)}, /*index=5*/f32[1,128,1024]{2,1,0:T(8,128)}) custom-call(bf16[3,4,2,4,32,1024]{5,4,3,2,1,0:T(8,128)(2,1)} %pad_maximum_fusion.refs_0_, bf16[1,4,2,4,32,1024]{5,4,3,2,1,0:T(8,128)(2,1)} %bitcast.412, ...), custom_call_target="tpu_custom_call" | custom-call | tf_op jit(solution)/shard_map/scatter_grads/pallas_call | solution.py:312
  (512 shorter events, 533.0 us)
Async XLA Ops:
  0.6 13.6 %copy-start = (bf16[32,32,1024]{2,1,0:T(8,128)(2,1)S(1)}, bf16[32,32,1024]{2,1,0:T(8,128)(2,1)}, u32[]{:S(2)}) copy-start(bf16[32,32,1024]{2,1,0:T(8,128)(2,1)} %param.31) | copy-start | bytes 6291460
  4.7 23.6 %all-to-all-start.1 = ((bf16[32,8,1024]{2,1,0:T(8,128)(2,1)}), bf16[32,8,1024]{2,1,0:T(8,128)(2,1)S(1)}, u32[]{:S(2)}, u32[]{:S(2)}) async-start(bf16[32,8,1024]{2,1,0:T(8,128)(2,1)} %broadcast_select_fusion.5), calls=%async_computation.1 | async-start | bytes 1048576 | tf_op jit(solution)/shard_map/all_to_all | solution.py:494
  28.2 205.0 %all-to-all-start = ((bf16[32,32,1024]{2,1,0:T(8,128)(2,1)}), bf16[32,32,1024]{2,1,0:T(8,128)(2,1)S(1)}, u32[]{:S(2)}, u32[]{:S(2)}) async-start(bf16[32,32,1024]{2,1,0:T(8,128)(2,1)} %get-tuple-element.736), calls=%async_computation | async-start | bytes 4194304 | tf_op jit(solution)/shard_map/all_to_all | solution.py:493
  233.2 58.2 %copy-start.9 = (bf16[32,32,1024]{2,1,0:T(8,128)(2,1)}, bf16[32,32,1024]{2,1,0:T(8,128)(2,1)S(1)}, u32[]{:S(2)}) copy-start(bf16[32,32,1024]{2,1,0:T(8,128)(2,1)S(1)} %all-to-all-done) | copy-start | bytes 6291460
  233.2 54.1 %all-to-all-start.3 = ((bf16[32,32,1024]{2,1,0:T(8,128)(2,1)}), bf16[32,32,1024]{2,1,0:T(8,128)(2,1)}, u32[]{:S(2)}, u32[]{:S(2)}) async-start(bf16[32,32,1024]{2,1,0:T(8,128)(2,1)} %get-tuple-element.735), calls=%async_computation.3 | async-start | bytes 4194304 | tf_op jit(solution)/shard_map/all_to_all | solution.py:495
  242.5 49.0 %copy-start.62 = (f32[1024]{0:T(1024)}, f32[1024]{0:T(1024)S(1)}, u32[]{:S(2)}) copy-start(f32[1024]{0:T(1024)S(1)} %mul.351) | copy-start | bytes 12292
  243.2 17.7 %copy-start.82 = (f32[1024]{0:T(1024)}, f32[1024]{0:T(1024)S(1)}, u32[]{:S(2)}) copy-start(f32[1024]{0:T(1024)S(1)} %mul.358) | copy-start | bytes 12292
  308.8 103.0 %copy-start.96 = (f32[1024]{0:T(1024)S(1)}, f32[1024]{0:T(1024)}, u32[]{:S(2)}) copy-start(f32[1024]{0:T(1024)} %add.313) | copy-start | bytes 12292
  328.3 14.7 %copy-start.8 = (bf16[1024,16,64]{0,2,1:T(8,128)(2,1)S(1)}, bf16[1024,16,64]{0,2,1:T(8,128)(2,1)}, u32[]{:S(2)}) copy-start(bf16[1024,16,64]{0,2,1:T(8,128)(2,1)} %get-tuple-element.1027) | copy-start | bytes 6291460 | tf_op jit(solution)/shard_map/while
  379.7 14.7 %copy-start.8 = (bf16[1024,16,64]{0,2,1:T(8,128)(2,1)S(1)}, bf16[1024,16,64]{0,2,1:T(8,128)(2,1)}, u32[]{:S(2)}) copy-start(bf16[1024,16,64]{0,2,1:T(8,128)(2,1)} %get-tuple-element.1027) | copy-start | bytes 6291460 | tf_op jit(solution)/shard_map/while
  427.9 24.3 %copy-start.94 = (f32[1024]{0:T(1024)S(1)}, f32[1024]{0:T(1024)}, u32[]{:S(2)}) copy-start(f32[1024]{0:T(1024)} %add.327) | copy-start | bytes 12292
  458.2 13.4 %copy-start.18 = (f32[1024,1024]{1,0:T(8,128)}, f32[1024,1024]{1,0:T(8,128)S(1)}, u32[]{:S(2)}) copy-start(f32[1024,1024]{1,0:T(8,128)S(1)} %get-tuple-element.740) | copy-start | bytes 12582916
  458.3 53.8 %copy-start.69 = (f32[1024]{0:T(1024)}, f32[1024]{0:T(1024)S(1)}, u32[]{:S(2)}) copy-start(f32[1024]{0:T(1024)S(1)} %broadcast_multiply_fusion.4) | copy-start | bytes 12292
  458.9 53.2 %copy-start.79 = (f32[1024]{0:T(1024)}, f32[1024]{0:T(1024)S(1)}, u32[]{:S(2)}) copy-start(f32[1024]{0:T(1024)S(1)} %fusion.69) | copy-start | bytes 12292
  458.9 12.7 %copy-start.43 = (bf16[32,32,1024]{2,1,0:T(8,128)(2,1)S(1)}, bf16[32,32,1024]{2,1,0:T(8,128)(2,1)}, u32[]{:S(2)}) copy-start(bf16[32,32,1024]{2,1,0:T(8,128)(2,1)} %get-tuple-element.695) | copy-start | bytes 6291460
  458.9 12.7 %copy-start.85 = (f32[4096]{0:T(1024)S(1)}, f32[4096]{0:T(1024)}, u32[]{:S(2)}) copy-start(f32[4096]{0:T(1024)} %fusion.66) | copy-start | bytes 49156
  496.6 15.5 %copy-start.19 = (f32[1024,1024]{1,0:T(8,128)S(1)}, f32[1024,1024]{1,0:T(8,128)}, u32[]{:S(2)}) copy-start(f32[1024,1024]{1,0:T(8,128)} %copy-done.18) | copy-start | bytes 12582916
  516.5 18.7 %copy-start.11 = (f32[1024,1024]{1,0:T(8,128)S(1)}, f32[1024,1024]{1,0:T(8,128)}, u32[]{:S(2)}) copy-start(f32[1024,1024]{1,0:T(8,128)} %get-tuple-element.709) | copy-start | bytes 12582916
  589.1 10.1 copy-start.81
  877.1 16.8 %all-to-all-start.6 = ((f32[32,1,544]{2,1,0:T(1,128)}), f32[32,1,544]{2,1,0:T(1,128)S(1)}, u32[]{:S(2)}, u32[]{:S(2)}) async-start(f32[32,1,544]{2,1,0:T(1,128)} %copy.132), calls=%async_computation.6 | async-start | bytes 163840 | tf_op jit(solution)/shard_map/all_to_all | solution.py:625
  893.9 42.3 %all-to-all-start.5 = ((bf16[32,2,4096]{2,1,0:T(2,128)(2,1)}), bf16[32,2,4096]{2,1,0:T(2,128)(2,1)}, u32[]{:S(2)}, u32[]{:S(2)}) async-start(bf16[32,2,4096]{2,1,0:T(2,128)(2,1)} %reshape.1030), calls=%async_computation.5 | async-start | bytes 1048576 | tf_op jit(solution)/shard_map/all_to_all | solution.py:638
  911.4 15.7 %copy-start.32 = (bf16[256,1024]{0,1:T(8,128)(2,1)S(1)}, bf16[256,1024]{0,1:T(8,128)(2,1)}, u32[]{:S(2)}) copy-start(bf16[256,1024]{0,1:T(8,128)(2,1)} %copy.129) | copy-start | bytes 1572868
  936.1 68.0 %all-to-all-start.2 = ((bf16[32,2,16384]{2,1,0:T(2,128)(2,1)}), bf16[32,2,16384]{2,1,0:T(2,128)(2,1)S(1)}, u32[]{:S(2)}, u32[]{:S(2)}) async-start(bf16[32,2,16384]{2,1,0:T(2,128)(2,1)} %reshape.1026), calls=%async_computation.2 | async-start | bytes 4194304 | tf_op jit(solution)/shard_map/all_to_all | solution.py:636
  1004.1 215.6 %all-to-all-start.4 = ((bf16[32,2,16384]{2,1,0:T(2,128)(2,1)}), bf16[32,2,16384]{2,1,0:T(2,128)(2,1)}, u32[]{:S(2)}, u32[]{:S(2)}) async-start(bf16[32,2,16384]{2,1,0:T(2,128)(2,1)} %reshape.1028), calls=%async_computation.4 | async-start | bytes 4194304 | tf_op jit(solution)/shard_map/all_to_all | solution.py:637
  (97 other events, 466.7 us)

commit v2 on v1

v2 whole, which is shorter than its diff:
```python
import functools

import jax
import jax.numpy as jnp
from jax import lax
from jax.experimental import pallas as pl
from jax.experimental.pallas import tpu as pltpu
from jax.sharding import PartitionSpec as P

HD = 64
EPSILON = 1e-05
SCALE = 0.125
NEGATIVE = -1e30
MESH = pl.DeviceIdType.MESH
ANY = pl.BlockSpec(memory_space=pl.ANY)


def ring_place(f, ring):
    half = ring // 2
    upper, rest = f // half, f % half
    return upper * half + rest + upper * (half - 1 - 2 * rest)


def position(depth, ring):
    d, f = lax.axis_index("dp"), lax.axis_index("fsdp")
    return d // 2, d % 2, ring_place(f, ring), f


def greet(z, c, right, left, depth, f):
    barrier = pltpu.get_barrier_semaphore()

    def hail(d, g):
        pl.semaphore_signal(barrier, inc=1, device_id=(d, g), device_id_type=MESH)

    for s in range(1, depth):
        hail((z + s) % depth * 2 + c, f)
    hail(z * 2 + c, right)
    hail(z * 2 + c, left)
    hail(z * 2 + 1 - c, f)
    pl.semaphore_wait(barrier, depth + 2)


def gather_kernel(depth, ring, units, n_in, *refs):
    shards, fulls = refs[:n_in], refs[n_in : 2 * n_in]
    local_sem, z_send, z_recv, r_send, r_recv, c_send, c_recv = refs[2 * n_in :]
    half = ring // 2
    z, c, place, f = position(depth, ring)
    right = ring_place((place + 1) % ring, ring)
    left = ring_place((place + ring - 1) % ring, ring)
    greet(z, c, right, left, depth, f)

    def own(u):
        which, lead, rows, cols = units[u]
        return shards[which].at[lead, rows, cols]

    def chunk(u, zs, cc, g):
        which, lead, rows, cols = units[u]
        return fulls[which].at[lead, zs, cc, g, rows, cols]

    def remote(src, dst, send, recv, d, g):
        return pltpu.make_async_remote_copy(
            src_ref=src, dst_ref=dst, send_sem=send, recv_sem=recv,
            device_id=(d, g), device_id_type=MESH,
        )

    def kept(u):
        return pltpu.make_async_copy(own(u), chunk(u, z, c, f), local_sem.at[u])

    def z_out(u, s):
        return remote(own(u), chunk(u, z, c, f), z_send.at[u, s], z_recv.at[u, s],
                      (z + s) % depth * 2 + c, f)

    def z_in(u, s):
        src = (z + depth - s) % depth
        return remote(own(u), chunk(u, src, c, f), z_send.at[u, s], z_recv.at[u, s],
                      (z + s) % depth * 2 + c, f)

    all_z, low_z, high_z = slice(0, depth), slice(0, depth // 2), slice(depth // 2, depth)

    def zs_of(t, way):
        return all_z if t < half else (low_z, high_z)[way]

    def ring_copy(u, t, way, incoming):
        back = t - 1 + incoming
        origin = (place + ring - back) % ring if way == 0 else (place + back) % ring
        piece = chunk(u, zs_of(t, way), c, ring_place(origin, ring))
        return remote(piece, piece, r_send.at[u, t - 1, way], r_recv.at[u, t - 1, way],
                      z * 2 + c, (right, left)[way])

    def core_copy(u, origin, slot, cc):
        piece = chunk(u, all_z, cc, ring_place(origin % ring, ring))
        return remote(piece, piece, c_send.at[u, slot], c_recv.at[u, slot], z * 2 + 1 - c, f)

    def start_z(u):
        kept(u).start()
        for s in range(1, depth):
            z_out(u, s).start()

    def end_z(u):
        kept(u).wait()
        for s in range(1, depth):
            z_in(u, s).wait_recv()

    def start_ring(u, t):
        for way in range(2):
            ring_copy(u, t, way, 0).start()

    def end_ring(u, t):
        for way in range(2):
            ring_copy(u, t, way, 1).wait_recv()

    def sets_after(t):
        if t == 0:
            return [0]
        return [t] if t == half else [ring - t, t]

    def start_core(u, t):
        for shift in sets_after(t):
            core_copy(u, place + shift, shift, c).start()

    count = len(units)
    ahead = 2
    for u in range(min(ahead, count)):
        start_z(u)
    for i in range(count + half):
        if i + ahead < count:
            start_z(i + ahead)
        if i < count:
            end_z(i)
            start_ring(i, 1)
            start_core(i, 0)
        for t in range(1, half + 1):
            u = i - t
            if 0 <= u < count:
                end_ring(u, t)
                if t < half:
                    start_ring(u, t + 1)
                start_core(u, t)
    for u in range(count):
        for s in range(1, depth):
            z_out(u, s).wait_send()
        for t in range(1, half + 1):
            for way in range(2):
                ring_copy(u, t, way, 0).wait_send()
        for shift in range(ring):
            core_copy(u, place + shift, shift, c).wait_send()
            core_copy(u, place + shift, shift, 1 - c).wait_recv()


def gather_weights(mesh, shards, units, ident):
    depth, ring = mesh.shape["dp"] // 2, mesh.shape["fsdp"]
    n = len(units)
    half = ring // 2
    dma = pltpu.SemaphoreType.DMA
    return pl.pallas_call(
        functools.partial(gather_kernel, depth, ring, units, len(shards)),
        out_shape=[
            jax.ShapeDtypeStruct((a.shape[0], depth, 2, ring) + a.shape[1:], a.dtype)
            for a in shards
        ],
        in_specs=[ANY] * len(shards),
        out_specs=[ANY] * len(shards),
        scratch_shapes=[
            dma((n,)),
            dma((n, depth)),
            dma((n, depth)),
            dma((n, half, 2)),
            dma((n, half, 2)),
            dma((n, ring)),
            dma((n, ring)),
        ],
        compiler_params=pltpu.CompilerParams(collective_id=ident, has_side_effects=True),
        cost_estimate=pl.CostEstimate(flops=120_000_000_000, bytes_accessed=2 * 33_554_432, transcendentals=0),
        name="gather_weights",
    )(*shards)


def scatter_kernel(depth, ring, units, n_in, *refs):
    fulls, outs = refs[:n_in], refs[n_in : 2 * n_in]
    mine, theirs, rhalf, rfull, zbuf = refs[2 * n_in : 2 * n_in + 5]
    l_sem, c_send, c_recv, r_send, r_recv, z_send, z_recv = refs[2 * n_in + 5 :]
    half = ring // 2
    hz = depth // 2
    z, c, place, f = position(depth, ring)
    right = ring_place((place + 1) % ring, ring)
    left = ring_place((place + ring - 1) % ring, ring)
    greet(z, c, right, left, depth, f)
    count = len(units)

    def chunk(u, cc):
        which, lead, rows, cols = units[u]
        return fulls[which].at[lead, slice(0, depth), cc, slice(0, ring), rows, cols]

    def remote(src, dst, send, recv, d, g):
        return pltpu.make_async_remote_copy(
            src_ref=src, dst_ref=dst, send_sem=send, recv_sem=recv,
            device_id=(d, g), device_id_type=MESH,
        )

    def load(u):
        return pltpu.make_async_copy(chunk(u, c), mine.at[u], l_sem.at[u])

    def core(u):
        return remote(chunk(u, 1 - c), theirs.at[u], c_send.at[u], c_recv.at[u], z * 2 + 1 - c, f)

    def dest(t, way):
        ahead = half - t + 1
        return ring_place((place + ahead) % ring if way == 0 else (place + ring - ahead) % ring, ring)

    def ring_copy(u, t, way):
        g = dest(t, way)
        if t == 1:
            src = mine.at[u, slice(0, hz) if way == 0 else slice(hz, depth), g]
            dst = rhalf.at[u, way]
        else:
            src = mine.at[u, slice(0, depth), g]
            dst = rfull.at[u, t - 2, way]
        return remote(src, dst, r_send.at[u, t - 1, way], r_recv.at[u, t - 1, way],
                      z * 2 + c, (right, left)[way])

    def z_copy(u, s):
        to = (z + s) % depth
        return remote(mine.at[u, to, f], zbuf.at[u, s - 1], z_send.at[u, s], z_recv.at[u, s],
                      to * 2 + c, f)

    def first_sum(u):
        core(u).wait_recv()
        load(u).wait()

        def body(i, carry):
            a, g = i // ring, i % ring
            mine[u, a, g] = (
                mine[u, a, g].astype(jnp.float32) + theirs[u, a, g].astype(jnp.float32)
            ).astype(mine.dtype)
            return carry

        lax.fori_loop(0, depth * ring, body, 0)
        for way in range(2):
            ring_copy(u, 1, way).start()

    def next_sum(u, t):
        for way in range(2):
            ring_copy(u, t, way).wait_recv()
        if t < half:
            for way in range(2):
                g = dest(t + 1, way)
                low = hz * way if t == 1 else 0
                many = hz if t == 1 else depth
                src = rhalf.at[u, way] if t == 1 else rfull.at[u, t - 2, way]

                def body(i, carry, g=g, low=low, src=src):
                    mine[u, low + i, g] = (
                        mine[u, low + i, g].astype(jnp.float32) + src[i].astype(jnp.float32)
                    ).astype(mine.dtype)
                    return carry

                lax.fori_loop(0, many, body, 0)
                ring_copy(u, t + 1, way).start()
        else:
            one, two = rfull.at[u, t - 2, 0], rfull.at[u, t - 2, 1]

            def body(i, carry):
                mine[u, i, f] = (
                    mine[u, i, f].astype(jnp.float32)
                    + one[i].astype(jnp.float32)
                    + two[i].astype(jnp.float32)
                ).astype(mine.dtype)
                return carry

            lax.fori_loop(0, depth, body, 0)
            for s in range(1, depth):
                z_copy(u, s).start()

    def last_sum(u):
        for s in range(1, depth):
            z_copy(u, s).wait_recv()
        which, lead, rows, cols = units[u]
        total = mine[u, z, f].astype(jnp.float32)
        for s in range(1, depth):
            total = total + zbuf[u, s - 1].astype(jnp.float32)
        outs[which][lead, rows, cols] = total

    for u in range(count):
        core(u).start()
        load(u).start()
    for i in range(count + half + 1):
        if i < count:
            first_sum(i)
        for t in range(1, half + 1):
            u = i - t
            if 0 <= u < count:
                next_sum(u, t)
        u = i - half - 1
        if 0 <= u < count:
            last_sum(u)
    for u in range(count):
        core(u).wait_send()
        for t in range(1, half + 1):
            for way in range(2):
                ring_copy(u, t, way).wait_send()
        for s in range(1, depth):
            z_copy(u, s).wait_send()


def scatter_grads(mesh, fulls, units, ident):
    depth, ring = mesh.shape["dp"] // 2, mesh.shape["fsdp"]
    n = len(units)
    half = ring // 2
    hz = depth // 2
    dma = pltpu.SemaphoreType.DMA
    low = fulls[0].dtype
    rows = fulls[0].shape[-2]
    cols = fulls[0].shape[-1]
    vm = pl.BlockSpec(memory_space=pltpu.VMEM)
    return pl.pallas_call(
        functools.partial(scatter_kernel, depth, ring, units, len(fulls)),
        out_shape=[jax.ShapeDtypeStruct((a.shape[0],) + a.shape[4:], jnp.float32) for a in fulls],
        in_specs=[ANY] * len(fulls),
        out_specs=[vm] * len(fulls),
        scratch_shapes=[
            pltpu.VMEM((n, depth, ring, rows, cols), low),
            pltpu.VMEM((n, depth, ring, rows, cols), low),
            pltpu.VMEM((n, 2, hz, rows, cols), low),
            pltpu.VMEM((n, half - 1, 2, depth, rows, cols), low),
            pltpu.VMEM((n, depth - 1, rows, cols), low),
            dma((n,)),
            dma((n,)),
            dma((n,)),
            dma((n, half, 2)),
            dma((n, half, 2)),
            dma((n, depth)),
            dma((n, depth)),
        ],
        compiler_params=pltpu.CompilerParams(
            collective_id=ident, has_side_effects=True, vmem_limit_bytes=60 * 2**20
        ),
        name="scatter_grads",
    )(*fulls)


NN = (((1,), (0,)), ((), ()))
NT = (((1,), (1,)), ((), ()))
TN = (((0,), (0,)), ((), ()))
LOW = jnp.bfloat16
FULL = jnp.float32
SMEM = pl.BlockSpec(memory_space=pltpu.SMEM)
VMEM = pl.BlockSpec(memory_space=pltpu.VMEM)
PAIR = 2 * HD
ROOM = 60 * 2**20


def dot(left, right, how):
    return lax.dot_general(left, right, how, preferred_element_type=FULL)


def calls(kernel, name, flops, moved, **kw):
    return pl.pallas_call(
        kernel,
        name=name,
        compiler_params=pltpu.CompilerParams(vmem_limit_bytes=ROOM),
        cost_estimate=pl.CostEstimate(flops=int(flops), bytes_accessed=int(moved), transcendentals=0),
        **kw,
    )


def whole(shape):
    return pl.BlockSpec(shape, lambda *_: (0,) * len(shape))


def normal(x):
    mean = jnp.mean(x, axis=-1, keepdims=True)
    centred = x - mean
    rstd = lax.rsqrt(jnp.mean(centred * centred, axis=-1, keepdims=True) + EPSILON)
    return centred * rstd, rstd


def normal_back(hat, rstd, grad, gain):
    scaled = grad * gain
    lean = jnp.mean(scaled, axis=-1, keepdims=True)
    tilt = jnp.mean(scaled * hat, axis=-1, keepdims=True)
    back = rstd * (scaled - lean - hat * tilt)
    return back, jnp.sum(grad * hat, axis=0, keepdims=True), jnp.sum(grad, axis=0, keepdims=True)


def add_row(ref, value, first):
    @pl.when(first)
    def _():
        ref[...] = value

    @pl.when(jnp.logical_not(first))
    def _():
        ref[...] += value


GAIN, SHIFT, DOWN = 6, 9, 12


def qkv_kernel(x_ref, w_ref, p_ref, a_ref, o_ref):
    j = pl.program_id(0)

    @pl.when(j == 0)
    def _():
        hat, _ = normal(x_ref[...].astype(FULL))
        a_ref[...] = (hat * p_ref[GAIN : GAIN + 1] + p_ref[SHIFT : SHIFT + 1]).astype(LOW)

    bias = jnp.where(j == 0, p_ref[0:1], jnp.where(j == 2, p_ref[1:2], 0.0))
    scale = jnp.where(j == 0, SCALE, 1.0)
    o_ref[0] = ((dot(a_ref[...], w_ref[0], NN) + bias) * scale).astype(LOW)


def project_qkv(x, w, p):
    rows, width = x.shape
    return calls(
        qkv_kernel,
        "project_qkv",
        6 * rows * width * width,
        2 * (5 * rows * width + 3 * width * width),
        grid=(3,),
        in_specs=[whole(x.shape), pl.BlockSpec((1, width, width), lambda j: (j, 0, 0)), whole(p.shape)],
        out_specs=[whole(x.shape), pl.BlockSpec((1, rows, width), lambda j: (j, 0, 0))],
        out_shape=[
            jax.ShapeDtypeStruct((rows, width), LOW),
            jax.ShapeDtypeStruct((3, rows, width), LOW),
        ],
    )(x, w, p)


def lanes(shape):
    return lax.broadcasted_iota(jnp.int32, shape, len(shape) - 1)


def rows_of(shape):
    return lax.broadcasted_iota(jnp.int32, shape, 0)


def head_mask(head):
    return jnp.where(lanes((1, PAIR)) // HD == head, 1.0, 0.0).astype(LOW)


def attend_kernel(causal, tile, n_ref, q_ref, k_ref, v_ref, o_ref, l_ref):
    h = pl.program_id(0)
    q, k, v = q_ref[0], k_ref[0], v_ref[0]
    queries, count = q.shape[0], k.shape[0]
    lane_k = lanes((count, PAIR))
    shut = jnp.where((lane_k == 0) & (rows_of((count, PAIR)) >= n_ref[0]), NEGATIVE, 0.0).astype(LOW)
    first = jnp.where(lanes((queries, PAIR)) == 0, 1.0, 0.0).astype(LOW)
    ones = jnp.ones((count, PAIR), LOW)
    wide_q = jnp.concatenate([q, first], axis=1)
    spots = lanes((tile, PAIR))
    keys = [jnp.concatenate([k * head_mask(head), shut], axis=1) for head in range(2)]
    values = [jnp.concatenate([v * head_mask(head), ones], axis=1) for head in range(2)]
    for i in range(queries // tile):
        at = slice(i * tile, (i + 1) * tile)
        seen = (i + 1) * tile if causal else count
        mixed = jnp.zeros((tile, PAIR), FULL)

        @pl.when(h == 0)
        def _():
            l_ref[at] = jnp.zeros((tile, PAIR), FULL)

        kept = l_ref[at]
        for head in range(2):
            scores = dot(wide_q[at], keys[head][:seen], NT)
            if causal:
                square = (tile, tile)
                last = jnp.where(lanes(square) <= rows_of(square), scores[:, seen - tile :], NEGATIVE)
                scores = last if seen == tile else jnp.concatenate([scores[:, : seen - tile], last], axis=1)
            top = jnp.max(scores, axis=1, keepdims=True)
            weights = jnp.exp(scores - top).astype(LOW)
            sums = dot(weights, values[head][:seen], NN)
            total = sums[:, PAIR:]
            mixed = mixed + sums[:, :PAIR] / total
            kept = jnp.where(spots == 2 * h + head, top + jnp.log(total), kept)
        o_ref[at] = mixed.astype(LOW)
        l_ref[at] = kept


def attend(length, q, k, v, causal, name):
    rows, width = q[0].shape[1:]
    count = k[0].shape[1]
    tile = 256

    def cut(pair):
        part = pair[1]
        return pl.BlockSpec((1, pair[0].shape[1], PAIR), lambda h: (part, 0, h))

    return calls(
        functools.partial(attend_kernel, causal, tile),
        name,
        4 * 4 * rows * count * width // (2 if causal else 1),
        2 * (2 * rows + 2 * count) * width,
        grid=(width // PAIR,),
        in_specs=[SMEM, cut(q), cut(k), cut(v)],
        out_specs=[pl.BlockSpec((rows, PAIR), lambda h: (0, h)), whole((rows, PAIR))],
        out_shape=[
            jax.ShapeDtypeStruct((rows, width), LOW),
            jax.ShapeDtypeStruct((rows, PAIR), FULL),
        ],
    )(length, q[0], k[0], v[0])


def thirds(x):
    one = x.astype(LOW).astype(FULL)
    two = (x - one).astype(LOW).astype(FULL)
    return one, two, x - one - two


def attend_back_kernel(causal, tile, n_ref, q_ref, k_ref, v_ref, o_ref, g_ref, l_ref, dq_ref, dkv_ref, acc_ref):
    h = pl.program_id(0)
    q, k, v, grad = q_ref[0], k_ref[0], v_ref[0], g_ref[...]
    queries, count = q.shape[0], k.shape[0]
    lane_k, lane_q = lanes((count, PAIR)), lanes((queries, PAIR))
    shut = jnp.where(rows_of((count, PAIR)) >= n_ref[0], NEGATIVE, 0.0)
    open_k = jnp.where(lane_k == 0, shut, jnp.where(lane_k < 4, 1.0, 0.0)).astype(LOW)
    open_v = jnp.where(lane_k < 3, 1.0, 0.0).astype(LOW)
    product = grad.astype(FULL) * o_ref[...].astype(FULL)
    acc_ref[...] = jnp.zeros_like(acc_ref)
    heads = []
    for head in range(2):
        mask = head_mask(head)
        level = jnp.sum(jnp.where(lane_q == 2 * h + head, l_ref[...], 0.0), axis=1, keepdims=True)
        one, two, three = thirds(-level)
        tail = jnp.where(lane_q == 0, 1.0, jnp.where(lane_q == 1, one, jnp.where(lane_q == 2, two, jnp.where(lane_q == 3, three, 0.0))))
        wide_q = jnp.concatenate([q, tail.astype(LOW)], axis=1)
        inner = jnp.sum(jnp.where(lane_q // HD == head, product, 0.0), axis=1, keepdims=True)
        one, two, three = thirds(-inner)
        tail = jnp.where(lane_q == 0, one, jnp.where(lane_q == 1, two, jnp.where(lane_q == 2, three, 0.0)))
        wide_g = jnp.concatenate([grad, tail.astype(LOW)], axis=1)
        heads.append(
            (
                wide_q,
                wide_g,
                jnp.concatenate([k * mask, open_k], axis=1),
                jnp.concatenate([v * mask, open_v], axis=1),
                q * mask,
                grad * mask,
                k * mask,
            )
        )
    for i in range(count // tile):
        at = slice(i * tile, (i + 1) * tile)
        low = i * tile if causal else 0
        grad_k = jnp.zeros((tile, PAIR), FULL)
        grad_v = jnp.zeros((tile, PAIR), FULL)
        for wide_q, wide_g, wide_k, wide_v, q_one, g_one, k_one in heads:
            scores = dot(wide_k[at], wide_q[low:], NT)
            if causal:
                square = (tile, tile)
                near = jnp.where(rows_of(square) <= lanes(square), scores[:, :tile], NEGATIVE)
                scores = near if low + tile == queries else jnp.concatenate([near, scores[:, tile:]], axis=1)
            probs = jnp.exp(scores)
            slope = (probs * dot(wide_v[at], wide_g[low:], NT)).astype(LOW)
            grad_v = grad_v + dot(probs.astype(LOW), g_one[low:], NN)
            grad_k = grad_k + dot(slope, q_one[low:], NN)
            acc_ref[low:] += dot(slope, k_one[at], TN)
        dkv_ref[0, at] = grad_k.astype(LOW)
        dkv_ref[1, at] = grad_v.astype(LOW)
    dq_ref[...] = acc_ref[...].astype(LOW)


def attend_back(length, q, k, v, mixed, grad, level, causal, name):
    rows, width = mixed.shape
    count = k[0].shape[1]
    tile = 256

    def cut(pair):
        part = pair[1]
        return pl.BlockSpec((1, pair[0].shape[1], PAIR), lambda h: (part, 0, h))

    column = pl.BlockSpec((rows, PAIR), lambda h: (0, h))
    return calls(
        functools.partial(attend_back_kernel, causal, tile),
        name,
        4 * 10 * rows * count * width // (2 if causal else 1),
        2 * (4 * rows + 4 * count) * width,
        grid=(width // PAIR,),
        in_specs=[SMEM, cut(q), cut(k), cut(v), column, column, whole((rows, PAIR))],
        out_specs=[column, pl.BlockSpec((2, count, PAIR), lambda h: (0, 0, h))],
        out_shape=[
            jax.ShapeDtypeStruct((rows, width), LOW),
            jax.ShapeDtypeStruct((2, count, width), LOW),
        ],
        scratch_shapes=[pltpu.VMEM((rows, PAIR), FULL)],
    )(length, q[0], k[0], v[0], mixed, grad, level)


def middle_kernel(x_ref, o_ref, wo_ref, wq_ref, p_ref, x1_ref, a_ref, q_ref):
    x1 = x_ref[...].astype(FULL) + (dot(o_ref[...], wo_ref[...], NN) + p_ref[2:3])
    x1_ref[...] = x1
    hat, _ = normal(x1)
    a = (hat * p_ref[GAIN + 1 : GAIN + 2] + p_ref[SHIFT + 1 : SHIFT + 2]).astype(LOW)
    a_ref[...] = a
    q_ref[0] = ((dot(a, wq_ref[0], NN) + p_ref[3:4]) * SCALE).astype(LOW)


def middle(x, mixed, w_out, w_cross, p, tile=256):
    rows, width = x.shape
    part = pl.BlockSpec((tile, width), lambda i: (i, 0))
    return calls(
        middle_kernel,
        "middle",
        4 * rows * width * width,
        12 * rows * width + 4 * width * width,
        grid=(rows // tile,),
        in_specs=[part, part, whole(w_out.shape), whole((1, width, width)), whole(p.shape)],
        out_specs=[part, part, pl.BlockSpec((1, tile, width), lambda i: (0, i, 0))],
        out_shape=[
            jax.ShapeDtypeStruct((rows, width), FULL),
            jax.ShapeDtypeStruct((rows, width), LOW),
            jax.ShapeDtypeStruct((1, rows, width), LOW),
        ],
    )(x, mixed, w_out, w_cross, p)


def memory_kernel(e_ref, w_ref, p_ref, o_ref):
    j = pl.program_id(0)
    o_ref[0] = (dot(e_ref[...], w_ref[0], NN) + jnp.where(j == 1, p_ref[4:5], 0.0)).astype(LOW)


def project_memory(memory, w_cross, p):
    count, width = memory.shape
    return calls(
        memory_kernel,
        "project_memory",
        4 * count * width * width,
        4 * width * width,
        grid=(2,),
        in_specs=[whole(memory.shape), pl.BlockSpec((1, width, width), lambda j: (j + 1, 0, 0)), whole(p.shape)],
        out_specs=pl.BlockSpec((1, count, width), lambda j: (j, 0, 0)),
        out_shape=jax.ShapeDtypeStruct((2, count, width), LOW),
    )(memory, w_cross, p)


CUBIC = 0.044715
ROOT = 0.7978845608028654


def feed_kernel(
    step_cols, n_ref, x1_ref, o_ref, g_ref, wc_hbm, wu_hbm, wd_hbm, p_ref, bu_ref,
    out_ref, r_ref, du_ref, a_ref, g3_ref, dx_ref, g2_ref, do_ref,
    sum_up, sum_down, sum_five, sum_gain, sum_shift,
    wc_ref, wu_ref, wd_ref, slope_ref, sems,
):
    i = pl.program_id(0)
    first = i == 0
    tile, width = x1_ref.shape
    inner = wu_ref.shape[1]
    loads = [
        pltpu.make_async_copy(a, b, sems.at[s])
        for s, (a, b) in enumerate(((wc_hbm, wc_ref), (wu_hbm, wu_ref), (wd_hbm, wd_ref)))
    ]

    @pl.when(first)
    def _():
        for load in loads:
            load.start()
        loads[0].wait()

    valid = jnp.where(i * tile + rows_of((tile, 1)) < n_ref[0], 1.0, 0.0)
    x2 = x1_ref[...] + (dot(o_ref[...], wc_ref[...], NN) + p_ref[5:6])
    hat, rstd = normal(x2)
    gain = p_ref[GAIN + 2 : GAIN + 3]
    a_ref[...] = (hat * gain + p_ref[SHIFT + 2 : SHIFT + 3]).astype(LOW)

    @pl.when(first)
    def _():
        loads[1].wait()
        loads[2].wait()

    total = x2 + p_ref[DOWN : DOWN + 1]
    for j in range(inner // step_cols):
        cols = slice(j * step_cols, (j + 1) * step_cols)
        u = dot(a_ref[...], wu_ref[:, cols], NN) + bu_ref[:, cols]
        square = u * u
        t = jnp.tanh(ROOT * (u * (1.0 + CUBIC * square)))
        half = 0.5 * (1.0 + t)
        r = (u * half).astype(LOW)
        r_ref[:, cols] = r
        slope = half + 0.5 * u * (1.0 - t * t) * (ROOT * (1.0 + 3.0 * CUBIC * square))
        slope_ref[:, cols] = slope.astype(LOW)
        total = total + dot(r, wd_ref[cols, :], NN)
    out_ref[...] = (total * valid).astype(LOW)
    grad_out = g_ref[...].astype(FULL) * valid
    g3 = grad_out.astype(LOW)
    g3_ref[...] = g3
    grad = jnp.zeros((tile, width), FULL)
    for j in range(inner // step_cols):
        cols = slice(j * step_cols, (j + 1) * step_cols)
        du = (dot(g3, wd_ref[cols, :], NT) * slope_ref[:, cols].astype(FULL)).astype(LOW)
        du_ref[:, cols] = du
        line = jnp.sum(du.astype(FULL), axis=0, keepdims=True)

        @pl.when(first)
        def _():
            sum_up[:, cols] = line

        @pl.when(jnp.logical_not(first))
        def _():
            sum_up[:, cols] += line

        grad = grad + dot(du, wu_ref[:, cols], NT)
    back, lines, shifts = normal_back(hat, rstd, grad, gain)
    dx2 = grad_out + back
    dx_ref[...] = dx2
    g2 = dx2.astype(LOW)
    g2_ref[...] = g2
    do_ref[...] = dot(g2, wc_ref[...], NT).astype(LOW)
    add_row(sum_down, jnp.sum(g3.astype(FULL), axis=0, keepdims=True), first)
    add_row(sum_five, jnp.sum(g2.astype(FULL), axis=0, keepdims=True), first)
    add_row(sum_gain, lines, first)
    add_row(sum_shift, shifts, first)


def feed(length, x1, mixed, cotangent, w_cross, w_up, w_down, p, bias_up, tile=256):
    rows, width = x1.shape
    inner = w_up.shape[1]
    part = pl.BlockSpec((tile, width), lambda i: (i, 0))
    broad = pl.BlockSpec((tile, inner), lambda i: (i, 0))
    low = jax.ShapeDtypeStruct((rows, width), LOW)
    wide = jax.ShapeDtypeStruct((rows, inner), LOW)
    line = jax.ShapeDtypeStruct((1, width), FULL)
    return calls(
        functools.partial(feed_kernel, min(1024, inner)),
        "feed",
        2 * rows * width * (4 * inner + 2 * width),
        2 * rows * (9 * width + 2 * inner) + 4 * inner * width,
        grid=(rows // tile,),
        in_specs=[SMEM, part, part, part, ANY, ANY, ANY, whole(p.shape), whole(bias_up.shape)],
        out_specs=[part, broad, broad, part, part, part, part, part, whole((1, inner))] + [whole((1, width))] * 4,
        out_shape=[low, wide, wide, low, low, jax.ShapeDtypeStruct((rows, width), FULL), low, low,
                   jax.ShapeDtypeStruct((1, inner), FULL), line, line, line, line],
        scratch_shapes=[
            pltpu.VMEM(w_cross.shape, LOW),
            pltpu.VMEM(w_up.shape, LOW),
            pltpu.VMEM(w_down.shape, LOW),
            pltpu.VMEM((tile, inner), LOW),
            pltpu.SemaphoreType.DMA((3,)),
        ],
    )(length, x1, mixed, cotangent, w_cross, w_up, w_down, p, bias_up)


def weight_kernel(scale, a_ref, b_ref, o_ref):
    value = dot(a_ref[...], b_ref[...], TN)
    o_ref[...] = (value if scale == 1.0 else value * scale).astype(LOW)


def weight_grad(a, b, name, scale=1.0):
    rows, n = a.shape
    m = b.shape[1]
    block = min(1024, n)
    cols = min(1024, m)
    return calls(
        functools.partial(weight_kernel, scale),
        name,
        2 * rows * n * m,
        2 * (rows * (n + m) + n * m),
        grid=(n // block, m // cols),
        in_specs=[pl.BlockSpec((rows, block), lambda i, j: (0, i)), pl.BlockSpec((rows, cols), lambda i, j: (0, j))],
        out_specs=pl.BlockSpec((block, cols), lambda i, j: (i, j)),
        out_shape=jax.ShapeDtypeStruct((n, m), LOW),
    )(a, b)


def cross_back_kernel(x1_ref, dq_ref, dx2_ref, wq_ref, wo_ref, p_ref, dx_ref, g1_ref, do_ref,
                      sum_q, sum_out, sum_gain, sum_shift):
    first = pl.program_id(0) == 0
    grad = dot(dq_ref[...], wq_ref[0], NT) * SCALE
    hat, rstd = normal(x1_ref[...])
    back, lines, shifts = normal_back(hat, rstd, grad, p_ref[GAIN + 1 : GAIN + 2])
    dx1 = dx2_ref[...] + back
    dx_ref[...] = dx1
    g1 = dx1.astype(LOW)
    g1_ref[...] = g1
    do_ref[...] = dot(g1, wo_ref[...], NT).astype(LOW)
    add_row(sum_q, jnp.sum(dq_ref[...].astype(FULL), axis=0, keepdims=True) * SCALE, first)
    add_row(sum_out, jnp.sum(g1.astype(FULL), axis=0, keepdims=True), first)
    add_row(sum_gain, lines, first)
    add_row(sum_shift, shifts, first)


def cross_back(x1, dq, dx2, w_cross, w_out, p, tile=256):
    rows, width = x1.shape
    part = pl.BlockSpec((tile, width), lambda i: (i, 0))
    low = jax.ShapeDtypeStruct((rows, width), LOW)
    line = jax.ShapeDtypeStruct((1, width), FULL)
    return calls(
        cross_back_kernel,
        "cross_back",
        4 * rows * width * width,
        16 * rows * width + 4 * width * width,
        grid=(rows // tile,),
        in_specs=[part, part, part, whole((1, width, width)), whole(w_out.shape), whole(p.shape)],
        out_specs=[part, part, part] + [whole((1, width))] * 4,
        out_shape=[jax.ShapeDtypeStruct((rows, width), FULL), low, low, line, line, line, line],
    )(x1, dq, dx2, w_cross, w_out, p)


def self_back_kernel(x_ref, dq_ref, dkv_ref, dx1_ref, w_ref, p_ref, dx_ref, sum_q, sum_v, sum_gain, sum_shift):
    first = pl.program_id(0) == 0
    dq = dq_ref[...]
    grad = dot(dq, w_ref[0], NT) * SCALE + dot(dkv_ref[0], w_ref[1], NT) + dot(dkv_ref[1], w_ref[2], NT)
    hat, rstd = normal(x_ref[...].astype(FULL))
    back, lines, shifts = normal_back(hat, rstd, grad, p_ref[GAIN : GAIN + 1])
    dx_ref[...] = (dx1_ref[...] + back).astype(LOW)
    add_row(sum_q, jnp.sum(dq.astype(FULL), axis=0, keepdims=True) * SCALE, first)
    add_row(sum_v, jnp.sum(dkv_ref[1].astype(FULL), axis=0, keepdims=True), first)
    add_row(sum_gain, lines, first)
    add_row(sum_shift, shifts, first)


def self_back(x, dq, dkv, dx1, w, p, tile=256):
    rows, width = x.shape
    part = pl.BlockSpec((tile, width), lambda i: (i, 0))
    line = jax.ShapeDtypeStruct((1, width), FULL)
    return calls(
        self_back_kernel,
        "self_back",
        6 * rows * width * width,
        14 * rows * width + 6 * width * width,
        grid=(rows // tile,),
        in_specs=[part, part, pl.BlockSpec((2, tile, width), lambda i: (0, i, 0)), part, whole(w.shape), whole(p.shape)],
        out_specs=[part] + [whole((1, width))] * 4,
        out_shape=[jax.ShapeDtypeStruct((rows, width), LOW), line, line, line, line],
    )(x, dq, dkv, dx1, w, p)


def qkv_grad_kernel(a_ref, q_ref, b_ref, o_ref):
    j = pl.program_id(0)

    @pl.when(j == 0)
    def _():
        o_ref[0] = (dot(a_ref[...], q_ref[...], TN) * SCALE).astype(LOW)

    @pl.when(j > 0)
    def _():
        o_ref[0] = dot(a_ref[...], b_ref[0], TN).astype(LOW)


def qkv_grad(a, dq, dkv):
    rows, width = a.shape
    return calls(
        qkv_grad_kernel,
        "qkv_grad",
        6 * rows * width * width,
        2 * (4 * rows * width + 3 * width * width),
        grid=(3,),
        in_specs=[
            whole(a.shape),
            whole(dq.shape),
            pl.BlockSpec((1, rows, width), lambda j: (jnp.maximum(j - 1, 0), 0, 0)),
        ],
        out_specs=pl.BlockSpec((1, width, width), lambda j: (j, 0, 0)),
        out_shape=jax.ShapeDtypeStruct((3, width, width), LOW),
    )(a, dq, dkv)


def cross_grad_kernel(a_ref, q_ref, e_ref, b_ref, w_ref, o_ref, de_ref, sum_v, acc_ref):
    j = pl.program_id(0)

    @pl.when(j == 0)
    def _():
        o_ref[0] = (dot(a_ref[...], q_ref[...], TN) * SCALE).astype(LOW)

    @pl.when(j > 0)
    def _():
        o_ref[0] = dot(e_ref[...], b_ref[0], TN).astype(LOW)

    @pl.when(j == 1)
    def _():
        acc_ref[...] = dot(b_ref[0], w_ref[0], NT)

    @pl.when(j == 2)
    def _():
        de_ref[...] = (acc_ref[...] + dot(b_ref[0], w_ref[0], NT)).astype(LOW)
        sum_v[...] = jnp.sum(b_ref[0].astype(FULL), axis=0, keepdims=True)


def cross_grad(a, dq, memory, dkv, w_cross):
    rows, width = a.shape
    count = memory.shape[0]
    return calls(
        cross_grad_kernel,
        "cross_grad",
        2 * rows * width * width + 8 * count * width * width,
        2 * (2 * rows * width + 5 * width * width),
        grid=(3,),
        in_specs=[
            whole(a.shape),
            whole(dq.shape),
            whole(memory.shape),
            pl.BlockSpec((1, count, width), lambda j: (jnp.maximum(j - 1, 0), 0, 0)),
            pl.BlockSpec((1, width, width), lambda j: (jnp.maximum(j, 1), 0, 0)),
        ],
        out_specs=[pl.BlockSpec((1, width, width), lambda j: (j, 0, 0)), whole(memory.shape), whole((1, width))],
        out_shape=[
            jax.ShapeDtypeStruct((3, width, width), LOW),
            jax.ShapeDtypeStruct((count, width), LOW),
            jax.ShapeDtypeStruct((1, width), FULL),
        ],
        scratch_shapes=[pltpu.VMEM((count, width), FULL)],
    )(a, dq, memory, dkv, w_cross)


def layer(slots, x, memory, cotangent, length, count, s_qkv, s_out, c_qkv, c_out, w_up, w_down, p, bias_up):
    a0, qkv = project_qkv(x, s_qkv, p)
    mixed0, level0 = attend(length, (qkv, 0), (qkv, 1), (qkv, 2), True, "self_attend")
    x1, a1, q1 = middle(x, mixed0, s_out, c_qkv, p)
    kv1 = project_memory(memory, c_qkv, p)
    mixed1, level1 = attend(count, (q1, 0), (kv1, 0), (kv1, 1), False, "cross_attend")
    (result, r, du, a2, g3, dx2, g2, grad_mixed1, bias_up_grad, bias_down_grad, bias_five, gain_two, shift_two) = feed(
        length, x1, mixed1, cotangent, c_out, w_up, w_down, p, bias_up
    )
    result = leave(result, slots)
    grad_down = weight_grad(r, g3, "down_grad")
    grad_up = weight_grad(a2, du, "up_grad")
    dq1, dkv1 = attend_back(count, (q1, 0), (kv1, 0), (kv1, 1), mixed1, grad_mixed1, level1, False, "cross_attend_back")
    grad_c_out = weight_grad(mixed1, g2, "cross_out_grad")
    dx1, g1, grad_mixed0, bias_three, bias_two, gain_one, shift_one = cross_back(x1, dq1, dx2, c_qkv, s_out, p)
    grad_c_qkv, grad_memory, bias_four = cross_grad(a1, dq1, memory, dkv1, c_qkv)
    grad_memory = leave(grad_memory, slots)
    grad_mixed0 = after(grad_mixed0, result)
    dq0, dkv0 = attend_back(length, (qkv, 0), (qkv, 1), (qkv, 2), mixed0, grad_mixed0, level0, True, "self_attend_back")
    grad_s_out = weight_grad(mixed0, g1, "self_out_grad")
    dx, bias_zero, bias_one, gain_zero, shift_zero = self_back(x, after(dq0, grad_memory), dkv0, dx1, s_qkv, p)
    dx = leave(dx, slots)
    grad_s_qkv = qkv_grad(a0, dq0, dkv0)
    bias_grads = jnp.concatenate([bias_zero, bias_one, bias_two, bias_three, bias_four, bias_five])
    gains = jnp.concatenate([gain_zero, gain_one, gain_two])
    shifts = jnp.concatenate([shift_zero, shift_one, shift_two])
    return (
        (result, dx, grad_memory),
        (grad_s_qkv, grad_s_out, grad_c_qkv, grad_c_out, grad_up, grad_down),
        (bias_grads, bias_up_grad[0], bias_down_grad[0], gains, shifts),
    )


def units_of(shards):
    base = shards[0].shape[1]
    wide = shards[0].shape[2]
    found = []
    for which, (lead, rows, cols) in enumerate(a.shape for a in shards):
        for l in range(lead):
            for r in range(rows // base):
                for k in range(cols // wide):
                    found.append((which, l, slice(r * base, (r + 1) * base), slice(k * wide, (k + 1) * wide)))
    return tuple(found)


AXES = ("dp", "fsdp")


def arrive(array, deal):
    return lax.all_to_all(jnp.take(array, deal, axis=0), AXES, split_axis=0, concat_axis=1, tiled=True)[0]


def leave(array, slots):
    return lax.all_to_all(array.reshape(slots, -1, array.shape[-1]), AXES, split_axis=0, concat_axis=0, tiled=True)


def after(value, *others):
    return lax.optimization_barrier((value, *others))[0]


def per_device(
    mesh,
    units,
    encoder,
    cotangent,
    deal,
    lengths,
    enc_counts,
    self_qkv,
    self_out,
    cross_qkv,
    cross_out,
    ffn_up,
    ffn_down,
    biases,
    ffn_bias_up,
    ffn_bias_down,
    norm_gain,
    norm_shift,
):
    slots = deal.shape[0]
    depth, ring = mesh.shape["dp"] // 2, mesh.shape["fsdp"]
    inverse = jnp.zeros((slots,), jnp.int32).at[deal].set(jnp.arange(slots, dtype=jnp.int32))
    place = lax.axis_index(AXES)
    length = lax.dynamic_slice_in_dim(lengths, place, 1)
    enc_count = lax.dynamic_slice_in_dim(enc_counts, place, 1)
    x = arrive(units, deal)

    big = [self_qkv, self_out[None], cross_qkv, cross_out[None], ffn_up[None], ffn_down[None]]
    pieces = units_of(big)
    rows = jnp.concatenate([biases, norm_gain, norm_shift, ffn_bias_down[None]])
    flat = jnp.concatenate([rows.reshape(-1), ffn_bias_up])
    size = -(-flat.shape[0] // 2048) * 2048
    little = jnp.pad(flat, (0, size - flat.shape[0])).reshape(1, size // 128, 128)
    little_piece = ((len(big), 0, slice(0, size // 128), slice(0, 128)),)
    gathered = gather_weights(mesh, big + [little], little_piece + pieces, 0)
    memory = arrive(after(encoder, x, gathered[-1]), deal)
    cot = arrive(after(cotangent, memory), deal)
    s_qkv, s_out, c_qkv, c_out, w_up, w_down = (
        g.reshape(g.shape[0], -1, g.shape[-1]) for g in gathered[:6]
    )
    flat = gathered[6].reshape(slots, size).astype(jnp.float32)
    p = flat[:, : rows.size].reshape((slots,) + rows.shape)
    p = jnp.moveaxis(p, 0, 1).reshape(rows.shape[0], -1)
    p = jnp.pad(p, ((0, 16 - rows.shape[0]), (0, 0)))
    bias_up = flat[:, rows.size : rows.size + ffn_bias_up.size].reshape(1, -1)

    leaving, grads, small_grads = layer(
        slots, x, memory, cot, length, enc_count, s_qkv, s_out[0], c_qkv, c_out[0], w_up[0], w_down[0], p, bias_up
    )

    def cut(g):
        g = g if g.ndim == 3 else g[None]
        return g.reshape(g.shape[0], depth, 2, ring, -1, g.shape[-1])

    sums = scatter_grads(mesh, [cut(g) for g in grads], pieces, 1)
    terms = jnp.concatenate(
        [
            jnp.moveaxis(g.reshape(g.shape[:-1] + (slots, -1)), -2, 0).reshape(slots, -1)
            for g in small_grads
        ],
        axis=1,
    )
    terms = lax.all_to_all(terms, AXES, split_axis=0, concat_axis=0, tiled=True)
    flat = jnp.sum(terms, axis=0)
    small_sums, at = [], 0
    for like in (biases, ffn_bias_up, ffn_bias_down, norm_gain, norm_shift):
        small_sums.append(flat[at : at + like.size].reshape(like.shape))
        at += like.size
    return (
        *(jnp.take(a, inverse, axis=0) for a in leaving),
        sums[0],
        sums[1][0],
        sums[2],
        sums[3][0],
        sums[4][0],
        sums[5][0],
        *small_sums,
    )


def solution(mesh):
    middle_rows = P(None, AXES, None)
    first_rows = P(AXES, None)
    last = P(None, AXES)
    weights = (middle_rows, first_rows, middle_rows, first_rows, first_rows, first_rows, last, P(AXES), P(AXES), last, last)
    return jax.shard_map(
        functools.partial(per_device, mesh),
        mesh=mesh,
        in_specs=(middle_rows,) * 3 + (P(),) * 3 + weights,
        out_specs=(middle_rows,) * 3 + weights,
        check_vma=False,
    )
```

time: 1250 us -> 757 us (0.61)
  matrix products: 436 us -> 0 us
  Pallas kernels: 360 us -> 649 us
  other arithmetic: 198 us -> 13.5 us
  local copies, waits for them, and re-layouts: 174 us -> 26.3 us
  blocking collectives: 0 us -> 35.5 us
  waiting for transfers between devices: 19.9 us -> 1.52 us
  loops' own time: 17.2 us -> 0 us
  starting transfers between devices: 38.3 us -> 24.8 us
    dot_general x58 -> x0, matrix products: 436 us -> none  [the longest x10 77.2 us: product_nt(): lax.dot_general(left, right, (((1,), (1,)), ((), ())), preferred_element_...]
    pallas_call x0 -> x16, Pallas kernels: none -> 294 us  [the longest x1 64.5 us: feed(): calls(functools.partial(feed_kernel, min(1024, inner)), 'feed', 2 * rows...]
    convert_element_type x13 -> x0, other arithmetic: 70.3 us -> none  [the longest x4 61.4 us: one_block(): grad_scores = (probs * (grad_probs - inner)).astype(jnp.bfloat16)]
    reduce_sum x18 -> x0, other arithmetic: 55.1 us -> none  [the longest x4 32.5 us: one_block(): total = jnp.sum(weights, axis=-1, keepdims=True)]
    unnamed x231 -> x69, local copies, waits for them, and re-layouts: 57.4 us -> 6.03 us
    all_to_all x0 -> x2, blocking collectives: none -> 35.5 us  [the longest x1 22 us: arrive(): lax.all_to_all(jnp.take(array, deal, axis=0), AXES, split_axis=0, concat_...]
    unnamed x9 -> x0, other arithmetic: 30.6 us -> none
    dynamic_slice x26 -> x2, local copies, waits for them, and re-layouts: 28.4 us -> 1.17 us  [the longest x1 0.59 us: per_device(): length = lax.dynamic_slice_in_dim(lengths, place, 1)]
  transfers between devices with their start and end apart: 7 -> 5, of which waited for: 2 -> 1; matrix products, arithmetic and copies ran while one was open for 17% -> 2% of each run, Pallas kernels for 29% -> 76%
where the time goes in v2:
time: 757 us; the launch traced here: 752 us
  Pallas kernels  649 us (86%)
  blocking collectives  35.5 us (5%)
  local copies, waits for them, and re-layouts  26.3 us (3%)
  starting transfers between devices  24.8 us (3%)
  other arithmetic  13.5 us (2%)
    pallas_call x1, Pallas kernels, gather_weights(): pl.pallas_call(functools.partial(gather_kernel, depth, ring, units, len(s...  200 us
    pallas_call x1, Pallas kernels, scatter_grads(): pl.pallas_call(functools.partial(scatter_kernel, depth, ring, units, len(...  154 us
    pallas_call x1, Pallas kernels, feed(): calls(functools.partial(feed_kernel, min(1024, inner)), 'feed', 2 * rows...  64.5 us
    pallas_call x2, Pallas kernels, attend_back(): calls(functools.partial(attend_back_kernel, causal, tile), name, 4 * 10 *...  62.2 us
    pallas_call x2, Pallas kernels, attend(): calls(functools.partial(attend_kernel, causal, tile), name, 4 * 4 * rows...  52.5 us
    pallas_call x4, Pallas kernels, weight_grad(): calls(functools.partial(weight_kernel, scale), name, 2 * rows * n * m, 2...  38.4 us
    all_to_all x1, blocking collectives, arrive(): lax.all_to_all(jnp.take(array, deal, axis=0), AXES, split_axis=0, concat_...  22 us
  transfers between devices with their start and end apart: 5, of which 1 were waited for; matrix products, arithmetic and copies ran while one was open for 2% of the time, Pallas kernels for 76%

profile of v2, /device:TPU:0, one launch (start us, length us, event | category | flops | bytes accessed | tf_op | source)
XLA Modules:
  0.0 751.6 jit_solution(18368555591395482504)
XLA Ops:
  7.4 7.3 all-to-all-start
  15.6 200.1 %gather_weights.1 = (bf16[3,4,2,4,32,1024]{5,4,3,2,1,0:T(8,128)(2,1)}, bf16[1,4,2,4,32,1024]{5,4,3,2,1,0:T(8,128)(2,1)}, bf16[3,4,2,4,32,1024]{5,4,3,2,1,0:T(8,1...) custom-call(bf16[3,32,1024]{2,1,0:T(8,128)(2,1)} %refs_0_.1, ...), custom_call_target="tpu_custom_call" | custom-call | flops 120000004096 | bytes 67108864 | tf_op jit(solution)/shard_map/gather_weights/pallas_call | solution.py:155
  216.5 22.0 %all_to_all.51 = bf16[32,8,1024]{2,1,0:T(8,128)(2,1)} all-to-all(bf16[32,8,1024]{2,1,0:T(8,128)(2,1)S(1)} %broadcast_select_fusion.5), channel_id=1, replica_groups=mesh['dp'=8,'fsdp'=4] {'dp','fsdp'}, dimensions={0} | all-to-all | bytes 1048576 | tf_op jit(solution)/shard_map/all_to_all | solution.py:953
  248.3 12.1 %project_qkv.1 = (bf16[1024,1024]{1,0:T(8,128)(2,1)}, bf16[3,1024,1024]{2,1,0:T(8,128)(2,1)}) custom-call(bf16[1024,1024]{1,0:T(8,128)(2,1)} %bitcast.60, bf16[3,1024,1024]{2,1,0:T(8,128)(2,1)} %bitcast.90, f32[16,1024]{1,0:T(8,128)} %pad.9.p_ref), custom_call_target="tpu_custom_call" | custom-call | flops 6442450944 | bytes 16777216 | tf_op jit(solution)/shard_map/project_qkv/pallas_call | solution.py:413
  260.4 30.6 %self_attend.1 = (bf16[1024,1024]{1,0:T(8,128)(2,1)}, f32[1024,128]{1,0:T(8,128)}) custom-call(s32[1]{0:T(128)} %dynamic_slice.6.n_ref, bf16[3,1024,1024]{2,1,0:T(8,128)(2,1)} %get-tuple-element.76.q_ref.k_ref.v_ref, bf16[3,1024,1024]{2,1,0:T(8,128)(2,1)} %get-tuple-element.76.q_ref.k_ref.v_ref, bf16[3,1024,1024]{2,1,0:T(8,128)(2,1)} %get-tuple-element.76.q_ref.k_ref.v_ref), custom_call_target="tpu_custom_call" | custom-call | flops 8589934592 | bytes 8388608 | tf_op jit(solution)/shard_map/self_attend/pallas_call | solution.py:487
  291.0 9.9 %middle.1 = (f32[1024,1024]{1,0:T(8,128)}, bf16[1024,1024]{1,0:T(8,128)(2,1)}, bf16[1,1024,1024]{2,1,0:T(8,128)(2,1)}) custom-call(bf16[1024,1024]{1,0:T(8,128)(2,1)} %bitcast.61, bf16[1024,1024]{1,0:T(8,128)(2,1)} %get-tuple-element.77.o_ref.a_ref, bf16[1024,1024]{1,0:T(8,128)(2,1)} %bitcast.56, bf16[3,1024,1024]{2,1,0:T(8,128)(2,1)} %bitcast.48, ...), custom_call_target="tpu_custom_call" | custom-call | flops 4294967296 | bytes 16777216 | tf_op jit(solution)/shard_map/middle/pallas_call | solution.py:599
  301.0 4.0 project_memory.1.k_ref.v_ref
  304.9 21.9 %cross_attend.1 = (bf16[1024,1024]{1,0:T(8,128)(2,1)}, f32[1024,128]{1,0:T(8,128)}) custom-call(s32[1]{0:T(128)} %dynamic_slice.7.n_ref, bf16[1,1024,1024]{2,1,0:T(8,128)(2,1)} %get-tuple-element.81.q_ref, bf16[2,256,1024]{2,1,0:T(8,128)(2,1)} %project_memory.1.k_ref.v_ref, bf16[2,256,1024]{2,1,0:T(8,128)(2,1)} %project_memory.1.k_ref.v_ref), custom_call_target="tpu_custom_call" | custom-call | flops 4294967296 | bytes 5242880 | tf_op jit(solution)/shard_map/cross_attend/pallas_call | solution.py:487
  328.2 64.5 %feed.1 = (bf16[1024,1024]{1,0:T(8,128)(2,1)}, bf16[1024,4096]{1,0:T(8,128)(2,1)}, bf16[1024,4096]{1,0:T(8,128)(2,1)}, bf16[1024,1024]{1,0:T(8,128)(2,1)}, bf16[...) custom-call(s32[1]{0:T(128)} %dynamic_slice.6.n_ref, ...), custom_call_target="tpu_custom_call" | custom-call | flops 38654705664 | bytes 52428800 | tf_op jit(solution)/shard_map/feed/pallas_call | solution.py:722
  392.8 6.4 all-to-all-start.3
  400.4 21.8 %cross_attend_back.1 = (bf16[1024,1024]{1,0:T(8,128)(2,1)}, bf16[2,256,1024]{2,1,0:T(8,128)(2,1)}) custom-call(s32[1]{0:T(128)} %dynamic_slice.7.n_ref, bf16[1,1024,1024]{2,1,0:T(8,128)(2,1)} %get-tuple-element.81.q_ref, bf16[2,256,1024]{2,1,0:T(8,128)(2,1)} %project_memory.1.k_ref.v_ref, bf16[2,256,1024]{2,1,0:T(8,128)(2,1)} %project_memory.1.k_ref.v_ref, ...), custom_call_target="tpu_custom_call" | custom-call | flops 10737418240 | bytes 10485760 | tf_op jit(solution)/shard_map/cross_attend_back/pallas_call | solution.py:571
  422.1 13.2 %cross_back.1 = (f32[1024,1024]{1,0:T(8,128)}, bf16[1024,1024]{1,0:T(8,128)(2,1)}, bf16[1024,1024]{1,0:T(8,128)(2,1)}, f32[1,1024]{1,0:T(1,128)}, f32[1,1024]{1,...) custom-call(f32[1024,1024]{1,0:T(8,128)} %get-tuple-element.80.x1_ref, ...), custom_call_target="tpu_custom_call" | custom-call | flops 4294967296 | bytes 20971520 | tf_op jit(solution)/shard_map/cross_back/pallas_call | solution.py:786
  435.4 11.0 %cross_grad.1 = (bf16[3,1024,1024]{2,1,0:T(8,128)(2,1)}, bf16[256,1024]{1,0:T(8,128)(2,1)}, f32[1,1024]{1,0:T(1,128)}) custom-call(bf16[1024,1024]{1,0:T(8,128)(2,1)} %get-tuple-element.97.a_ref, bf16[1024,1024]{1,0:T(8,128)(2,1)} %get-tuple-element.91.dq_ref.q_ref, bf16[256,1024]{1,0:T(8,128)(2,1)} %bitcast.67, ...), custom_call_target="tpu_custom_call" | custom-call | flops 4294967296 | bytes 14680064 | tf_op jit(solution)/shard_map/cross_grad/pallas_call | solution.py:881
  447.8 4.6 all-to-all-start.4
  452.5 40.4 %self_attend_back.1 = (bf16[1024,1024]{1,0:T(8,128)(2,1)}, bf16[2,1024,1024]{2,1,0:T(8,128)(2,1)}) custom-call(s32[1]{0:T(128)} %dynamic_slice.6.n_ref, bf16[3,1024,1024]{2,1,0:T(8,128)(2,1)} %get-tuple-element.76.q_ref.k_ref.v_ref, bf16[3,1024,1024]{2,1,0:T(8,128)(2,1)} %get-tuple-element.76.q_ref.k_ref.v_ref, ...), custom_call_target="tpu_custom_call" | custom-call | flops 21474836480 | bytes 16777216 | tf_op jit(solution)/shard_map/self_attend_back/pallas_call | solution.py:571
  493.0 14.7 %self_back.1 = (bf16[1024,1024]{1,0:T(8,128)(2,1)}, f32[1,1024]{1,0:T(1,128)}, f32[1,1024]{1,0:T(1,128)}, f32[1,1024]{1,0:T(1,128)}, f32[1,1024]{1,0:T(1,128)}) custom-call(bf16[1024,1024]{1,0:T(8,128)(2,1)} %bitcast.62, bf16[1024,1024]{1,0:T(8,128)(2,1)} %get-tuple-element.100.dq_ref.q_ref, bf16[2,1024,1024]{2,1,0:T(8,128)(2,1)} %get-tuple-element.101.dkv_ref.b_ref, ...), custom_call_target="tpu_custom_call" | custom-call | flops 6442450944 | bytes 20971520 | tf_op jit(solution)/shard_map/self_back/pallas_call | solution.py:815
  510.2 13.5 %all_to_all.52 = f32[32,1,544]{2,1,0:T(1,128)S(1)} all-to-all(f32[32,1,544]{2,1,0:T(1,128)S(1)} %copy.39), channel_id=1, replica_groups=mesh['dp'=8,'fsdp'=4] {'dp','fsdp'}, dimensions={0} | all-to-all | bytes 139264 | tf_op jit(solution)/shard_map/all_to_all | solution.py:1027
  528.0 5.9 cross_out_grad.1
  533.9 5.9 self_out_grad.1
  539.8 13.4 %down_grad.1 = bf16[4096,1024]{1,0:T(8,128)(2,1)} custom-call(bf16[1024,4096]{1,0:T(8,128)(2,1)} %get-tuple-element.110.a_ref, bf16[1024,1024]{1,0:T(8,128)(2,1)} %get-tuple-element.111.b_ref), custom_call_target="tpu_custom_call" | custom-call | flops 8589934592 | bytes 18874368 | tf_op jit(solution)/shard_map/down_grad/pallas_call | solution.py:752
  553.2 13.2 %up_grad.1 = bf16[1024,4096]{1,0:T(8,128)(2,1)} custom-call(bf16[1024,1024]{1,0:T(8,128)(2,1)} %get-tuple-element.108.a_ref, bf16[1024,4096]{1,0:T(8,128)(2,1)} %get-tuple-element.109.b_ref), custom_call_target="tpu_custom_call" | custom-call | flops 8589934592 | bytes 18874368 | tf_op jit(solution)/shard_map/up_grad/pallas_call | solution.py:752
  567.9 11.4 %qkv_grad.1 = bf16[3,1024,1024]{2,1,0:T(8,128)(2,1)} custom-call(bf16[1024,1024]{1,0:T(8,128)(2,1)} %get-tuple-element.104.a_ref, bf16[1024,1024]{1,0:T(8,128)(2,1)} %get-tuple-element.100.dq_ref.q_ref, bf16[2,1024,1024]{2,1,0:T(8,128)(2,1)} %get-tuple-element.101.dkv_ref.b_ref), custom_call_target="tpu_custom_call" | custom-call | flops 6442450944 | bytes 14680064 | tf_op jit(solution)/shard_map/qkv_grad/pallas_call | solution.py:841
  579.2 154.5 %scatter_grads.1 = (f32[3,32,1024]{2,1,0:T(8,128)}, f32[1,32,1024]{2,1,0:T(8,128)}, f32[3,32,1024]{2,1,0:T(8,128)}, f32[1,32,1024]{2,1,0:T(8,128)}, f32[1,32,4096]{2,1,0:T(8,128)}, /*index=5*/f32[1,128,1024]{2,1,0:T(8,128)}) custom-call(bf16[3,4,2,4,32,1024]{5,4,3,2,1,0:T(8,128)(2,1)} %bitcast.55, bf16[1,4,2,4,32,1024]{5,4,3,2,1,0:T(8,128)(2,1)} %bitcast.59, ...), custom_call_target="tpu_custom_call" | custom-call | tf_op jit(solution)/shard_map/scatter_grads/pallas_call | solution.py:315
  742.8 4.1 broadcast_select_fusion
  (129 shorter events, 43.7 us)
Async XLA Ops:
  7.4 7.3 copy-start.23
  7.4 7.3 copy-start.24
  7.4 7.4 copy-start.25
  7.4 7.4 copy-start.26
  7.4 7.5 copy-start.28
  7.4 208.3 %all-to-all-start = ((bf16[32,32,1024]{2,1,0:T(8,128)(2,1)}), bf16[32,32,1024]{2,1,0:T(8,128)(2,1)S(1)}, u32[]{:S(2)}, u32[]{:S(2)}) async-start(bf16[32,32,1024]{2,1,0:T(8,128)(2,1)} %broadcast_select_fusion.3), calls=%async_computation | async-start | bytes 4194304 | tf_op jit(solution)/shard_map/all_to_all | solution.py:953
  15.6 200.2 %copy-start.7 = (bf16[32,8,1024]{2,1,0:T(8,128)(2,1)S(1)}, bf16[32,8,1024]{2,1,0:T(8,128)(2,1)}, u32[]{:S(2)}) copy-start(bf16[32,8,1024]{2,1,0:T(8,128)(2,1)} %param.22) | copy-start | bytes 1572868
  215.7 22.8 %copy-start.3 = (bf16[32,32,1024]{2,1,0:T(8,128)(2,1)}, bf16[32,32,1024]{2,1,0:T(8,128)(2,1)S(1)}, u32[]{:S(2)}) copy-start(bf16[32,32,1024]{2,1,0:T(8,128)(2,1)S(1)} %all-to-all-done) | copy-start | bytes 6291460
  242.4 84.5 %all-to-all-start.2 = ((bf16[32,32,1024]{2,1,0:T(8,128)(2,1)}), bf16[32,32,1024]{2,1,0:T(8,128)(2,1)S(1)}, u32[]{:S(2)}, u32[]{:S(2)}) async-start(bf16[32,32,1024]{2,1,0:T(8,128)(2,1)} %broadcast_select_fusion.2), calls=%async_computation.2 | async-start | bytes 4194304 | tf_op jit(solution)/shard_map/all_to_all | solution.py:953
  392.8 6.9 copy-start.22
  392.8 55.1 %all-to-all-start.3 = ((bf16[32,32,1024]{2,1,0:T(8,128)(2,1)}), bf16[32,32,1024]{2,1,0:T(8,128)(2,1)S(1)}, u32[]{:S(2)}, u32[]{:S(2)}) async-start(bf16[32,32,1024]{2,1,0:T(8,128)(2,1)} %bitcast.65), calls=%async_computation.3 | async-start | bytes 4194304 | tf_op jit(solution)/shard_map/all_to_all | solution.py:957
  447.8 45.1 %all-to-all-start.4 = ((bf16[32,8,1024]{2,1,0:T(8,128)(2,1)}), bf16[32,8,1024]{2,1,0:T(8,128)(2,1)S(1)}, u32[]{:S(2)}, u32[]{:S(2)}) async-start(bf16[32,8,1024]{2,1,0:T(8,128)(2,1)} %bitcast.72), calls=%async_computation.4 | async-start | bytes 1048576 | tf_op jit(solution)/shard_map/all_to_all | solution.py:957
  492.9 14.8 %copy-start.15 = (f32[1,1024]{1,0:T(1,128)S(1)}, f32[1,1024]{1,0:T(1,128)}, u32[]{:S(2)}) copy-start(f32[1,1024]{1,0:T(1,128)} %get-tuple-element.128) | copy-start | bytes 12292
  492.9 14.8 %copy-start.16 = (f32[1,1024]{1,0:T(1,128)S(1)}, f32[1,1024]{1,0:T(1,128)}, u32[]{:S(2)}) copy-start(f32[1,1024]{1,0:T(1,128)} %get-tuple-element.131) | copy-start | bytes 12292
  492.9 14.8 %copy-start.20 = (f32[1,1024]{1,0:T(1,128)S(1)}, f32[1,1024]{1,0:T(1,128)}, u32[]{:S(2)}) copy-start(f32[1,1024]{1,0:T(1,128)} %get-tuple-element.127) | copy-start | bytes 12292
  492.9 14.8 %copy-start.21 = (f32[1,1024]{1,0:T(1,128)S(1)}, f32[1,1024]{1,0:T(1,128)}, u32[]{:S(2)}) copy-start(f32[1,1024]{1,0:T(1,128)} %get-tuple-element.130) | copy-start | bytes 12292
  493.0 16.0 %copy-start.14 = (f32[1,1024]{1,0:T(1,128)S(1)}, f32[1,1024]{1,0:T(1,128)}, u32[]{:S(2)}) copy-start(f32[1,1024]{1,0:T(1,128)} %get-tuple-element.123) | copy-start | bytes 12292
  493.0 16.0 %copy-start.17 = (f32[1,1024]{1,0:T(1,128)S(1)}, f32[1,1024]{1,0:T(1,128)}, u32[]{:S(2)}) copy-start(f32[1,1024]{1,0:T(1,128)} %get-tuple-element.121) | copy-start | bytes 12292
  493.0 16.0 %copy-start.18 = (f32[1,1024]{1,0:T(1,128)S(1)}, f32[1,1024]{1,0:T(1,128)}, u32[]{:S(2)}) copy-start(f32[1,1024]{1,0:T(1,128)} %get-tuple-element.120) | copy-start | bytes 12292
  493.0 16.0 %copy-start.19 = (f32[1,1024]{1,0:T(1,128)S(1)}, f32[1,1024]{1,0:T(1,128)}, u32[]{:S(2)}) copy-start(f32[1,1024]{1,0:T(1,128)} %get-tuple-element.122) | copy-start | bytes 12292
  493.0 17.0 %copy-start.13 = (f32[1,4096]{1,0:T(1,128)S(1)}, f32[1,4096]{1,0:T(1,128)}, u32[]{:S(2)}) copy-start(f32[1,4096]{1,0:T(1,128)} %get-tuple-element.124) | copy-start | bytes 49156
  523.6 215.4 %all-to-all-start.5 = ((bf16[32,32,1024]{2,1,0:T(8,128)(2,1)}), bf16[32,32,1024]{2,1,0:T(8,128)(2,1)}, u32[]{:S(2)}, u32[]{:S(2)}) async-start(bf16[32,32,1024]{2,1,0:T(8,128)(2,1)} %bitcast.63), calls=%async_computation.5 | async-start | bytes 4194304 | tf_op jit(solution)/shard_map/all_to_all | solution.py:957
  742.8 5.6 copy-start.8
  742.8 6.3 copy-start.11
  (12 other events, 39.2 us)

commit v3 on v0

v3 whole, which is shorter than its diff:
```python
import functools

import jax
import jax.numpy as jnp
from jax import lax
from jax.experimental import pallas as pl
from jax.experimental.pallas import tpu as pltpu
from jax.sharding import PartitionSpec as P

HD = 64
EPSILON = 1e-05
SCALE = 0.125
NEGATIVE = -1e30
MESH = pl.DeviceIdType.MESH
ANY = pl.BlockSpec(memory_space=pl.ANY)
DMA = pltpu.SemaphoreType.DMA


def ring_place(f, ring):
    half = ring // 2
    upper, rest = f // half, f % half
    return upper * half + rest + upper * (half - 1 - 2 * rest)


class Place:
    def __init__(self, depth, ring):
        self.depth, self.ring, self.half = depth, ring, ring // 2
        d, f = lax.axis_index("dp"), lax.axis_index("fsdp")
        self.z, self.c, self.f = d // 2, d % 2, f
        self.at = ring_place(f, ring)
        self.right = ring_place((self.at + 1) % ring, ring)
        self.left = ring_place((self.at + ring - 1) % ring, ring)

    def greet(self):
        barrier = pltpu.get_barrier_semaphore()

        def hail(d, g):
            pl.semaphore_signal(barrier, inc=1, device_id=(d, g), device_id_type=MESH)

        for s in range(1, self.depth):
            hail((self.z + s) % self.depth * 2 + self.c, self.f)
        hail(self.z * 2 + self.c, self.right)
        hail(self.z * 2 + self.c, self.left)
        hail(self.z * 2 + 1 - self.c, self.f)
        pl.semaphore_wait(barrier, self.depth + 2)

    def to_z(self, src, dst, send, recv, s):
        return self.remote(src, dst, send, recv, (self.z + s) % self.depth * 2 + self.c, self.f)

    def to_side(self, src, dst, send, recv, way):
        return self.remote(src, dst, send, recv, self.z * 2 + self.c, (self.right, self.left)[way])

    def to_core(self, src, dst, send, recv):
        return self.remote(src, dst, send, recv, self.z * 2 + 1 - self.c, self.f)

    @staticmethod
    def remote(src, dst, send, recv, d, g):
        return pltpu.make_async_remote_copy(
            src_ref=src, dst_ref=dst, send_sem=send, recv_sem=recv,
            device_id=(d, g), device_id_type=MESH,
        )


def when(flag, run):
    if isinstance(flag, bool):
        if flag:
            run()
    else:
        pl.when(flag)(run)


def both(one, two):
    if isinstance(one, bool) and isinstance(two, bool):
        return one and two
    return jnp.logical_and(one, two)


def loop(count, run):
    def body(i, carry):
        run(i)
        return carry

    lax.fori_loop(0, count, body, 0)


class Gather:
    def __init__(self, place, count, shards, fulls, sems, ahead=2):
        self.place, self.count, self.shards, self.fulls = place, count, shards, fulls
        self.local, self.z_send, self.z_recv, self.r_send, self.r_recv, self.c_send, self.c_recv = sems
        self.ahead = min(ahead, count)

    @staticmethod
    def sems(mesh, n):
        depth, ring = mesh.shape["dp"] // 2, mesh.shape["fsdp"]
        half = ring // 2
        return [DMA((n,)), DMA((n, depth)), DMA((n, depth)), DMA((n, half, 2)), DMA((n, half, 2)), DMA((n, ring)), DMA((n, ring))]

    def chunk(self, u, zs, c, g):
        return self.fulls.at[u, zs, c, g]

    def kept(self, u):
        p = self.place
        return pltpu.make_async_copy(self.shards.at[u], self.chunk(u, p.z, p.c, p.f), self.local.at[u])

    def z_copy(self, u, s, incoming):
        p = self.place
        origin = (p.z + p.depth - s) % p.depth if incoming else p.z
        return p.to_z(self.shards.at[u], self.chunk(u, origin, p.c, p.f), self.z_send.at[u, s], self.z_recv.at[u, s], s)

    def ring_copy(self, u, t, way, incoming):
        p = self.place
        back = t - 1 + incoming
        origin = (p.at + p.ring - back) % p.ring if way == 0 else (p.at + back) % p.ring
        cut = p.depth // 2
        zs = slice(0, p.depth) if t < p.half else (slice(0, cut), slice(cut, p.depth))[way]
        piece = self.chunk(u, zs, p.c, ring_place(origin, p.ring))
        return p.to_side(piece, piece, self.r_send.at[u, t - 1, way], self.r_recv.at[u, t - 1, way], way)

    def core_copy(self, u, shift, incoming):
        p = self.place
        c = 1 - p.c if incoming else p.c
        piece = self.chunk(u, slice(0, p.depth), c, ring_place((p.at + shift) % p.ring, p.ring))
        return p.to_core(piece, piece, self.c_send.at[u, shift], self.c_recv.at[u, shift])

    def start_z(self, u):
        self.kept(u).start()
        for s in range(1, self.place.depth):
            self.z_copy(u, s, False).start()

    def start_ring(self, u, t):
        for way in range(2):
            self.ring_copy(u, t, way, 0).start()

    def start_core(self, u, t):
        half, ring = self.place.half, self.place.ring
        for shift in [0] if t == 0 else [t] if t == half else [ring - t, t]:
            self.core_copy(u, shift, False).start()

    def begin(self):
        for u in range(self.ahead):
            self.start_z(u)

    def steps(self):
        return self.count + self.place.half

    def step(self, i):
        place = self.place

        def first():
            self.kept(i).wait()
            for s in range(1, place.depth):
                self.z_copy(i, s, True).wait_recv()
            self.start_ring(i, 1)
            self.start_core(i, 0)

        def later(u, t):
            for way in range(2):
                self.ring_copy(u, t, way, 1).wait_recv()
            if t < place.half:
                self.start_ring(u, t + 1)
            self.start_core(u, t)

        when(i + self.ahead < self.count, lambda: self.start_z(i + self.ahead))
        when(i < self.count, first)
        for t in range(1, place.half + 1):
            u = i - t
            when(both(0 <= u, u < self.count), functools.partial(later, u, t))

    def finish(self):
        place = self.place

        def one(u):
            for s in range(1, place.depth):
                self.z_copy(u, s, False).wait_send()
            for t in range(1, place.half + 1):
                for way in range(2):
                    self.ring_copy(u, t, way, 0).wait_send()
            for shift in range(place.ring):
                self.core_copy(u, shift, False).wait_send()
                self.core_copy(u, shift, True).wait_recv()

        loop(self.count, one)


class Scatter:
    def __init__(self, place, count, rows, held, outs, refs, sems):
        self.place, self.count, self.rows, self.held, self.outs = place, count, rows, held, outs
        self.mine, self.theirs, self.rhalf, self.rfull, self.zbuf = refs
        self.c_send, self.c_recv, self.r_send, self.r_recv, self.z_send, self.z_recv = sems
        self.slots = held.shape[0]

    @staticmethod
    def refs(mesh, n, rows, cols, low):
        depth, ring = mesh.shape["dp"] // 2, mesh.shape["fsdp"]
        half, cut = ring // 2, depth // 2
        return [
            pltpu.VMEM((n, depth, ring, rows, cols), low),
            pltpu.VMEM((n, depth, ring * rows, cols), low),
            pltpu.VMEM((n, 2, cut, rows, cols), low),
            pltpu.VMEM((n, half - 1, 2, depth, rows, cols), low),
            pltpu.VMEM((n, depth - 1, rows, cols), low),
        ]

    @staticmethod
    def sems(mesh, n):
        depth, ring = mesh.shape["dp"] // 2, mesh.shape["fsdp"]
        half = ring // 2
        return [DMA((n,)), DMA((n,)), DMA((n, half, 2)), DMA((n, half, 2)), DMA((n, depth)), DMA((n, depth))]

    def core(self, u):
        p = self.place
        return p.to_core(self.held.at[u % self.slots, slice(0, p.depth), 1 - p.c], self.theirs.at[u], self.c_send.at[u], self.c_recv.at[u])

    def dest(self, t, way):
        p = self.place
        ahead = p.half - t + 1
        return ring_place((p.at + ahead) % p.ring if way == 0 else (p.at + p.ring - ahead) % p.ring, p.ring)

    def ring_copy(self, u, t, way):
        p = self.place
        g, cut = self.dest(t, way), p.depth // 2
        if t == 1:
            src = self.mine.at[u, slice(0, cut) if way == 0 else slice(cut, p.depth), g]
            dst = self.rhalf.at[u, way]
        else:
            src = self.mine.at[u, slice(0, p.depth), g]
            dst = self.rfull.at[u, t - 2, way]
        return p.to_side(src, dst, self.r_send.at[u, t - 1, way], self.r_recv.at[u, t - 1, way], way)

    def z_copy(self, u, s):
        p = self.place
        to = (p.z + s) % p.depth
        return p.to_z(self.mine.at[u, to, p.f], self.zbuf.at[u, s - 1], self.z_send.at[u, s], self.z_recv.at[u, s], s)

    def first_sum(self, u):
        p, full = self.place, jnp.float32
        self.core(u).wait_recv()

        def one(a):
            total = self.held[u % self.slots, a, p.c].astype(full) + self.theirs[u, a].astype(full)
            for g in range(p.ring):
                self.mine[u, a, g] = total[g * self.rows : (g + 1) * self.rows].astype(self.mine.dtype)

        loop(p.depth, one)
        for way in range(2):
            self.ring_copy(u, 1, way).start()

    def next_sum(self, u, t):
        p, full, mine = self.place, jnp.float32, self.mine
        for way in range(2):
            self.ring_copy(u, t, way).wait_recv()
        cut = p.depth // 2
        if t < p.half:
            for way in range(2):
                g = self.dest(t + 1, way)
                low = cut * way if t == 1 else 0
                src = self.rhalf.at[u, way] if t == 1 else self.rfull.at[u, t - 2, way]

                def one(a, g=g, low=low, src=src):
                    mine[u, low + a, g] = (mine[u, low + a, g].astype(full) + src[a].astype(full)).astype(mine.dtype)

                loop(cut if t == 1 else p.depth, one)
                self.ring_copy(u, t + 1, way).start()
        else:
            left, right = self.rfull.at[u, t - 2, 0], self.rfull.at[u, t - 2, 1]

            def one(a):
                mine[u, a, p.f] = (
                    mine[u, a, p.f].astype(full) + left[a].astype(full) + right[a].astype(full)
                ).astype(mine.dtype)

            loop(p.depth, one)
            for s in range(1, p.depth):
                self.z_copy(u, s).start()

    def last_sum(self, u):
        p, full = self.place, jnp.float32
        for s in range(1, p.depth):
            self.z_copy(u, s).wait_recv()
        total = self.mine[u, p.z, p.f].astype(full)
        for s in range(1, p.depth):
            total = total + self.zbuf[u, s - 1].astype(full)
        self.outs[u] = total

    def finish(self):
        p = self.place

        def one(u):
            for t in range(1, p.half + 1):
                for way in range(2):
                    self.ring_copy(u, t, way).wait_send()
            for s in range(1, p.depth):
                self.z_copy(u, s).wait_send()

        loop(self.count, one)
        for u in range(max(0, self.count - self.slots), self.count):
            self.core(u).wait_send()

    def steps(self):
        return self.count + self.place.half // 2 + 1

    def early(self, i):
        for t in range(1, self.place.half + 1, 2):
            u = i - (t + 1) // 2
            when(both(0 <= u, u < self.count), functools.partial(self.next_sum, u, t))

    def late(self, i):
        when(i < self.count, lambda: self.first_sum(i))
        for t in range(2, self.place.half + 1, 2):
            u = i - t // 2
            when(both(0 <= u, u < self.count), functools.partial(self.next_sum, u, t))
        u = i - self.place.half // 2 - 1
        when(both(0 <= u, u < self.count), lambda: self.last_sum(u))


def remote_params(ident):
    return pltpu.CompilerParams(collective_id=ident, has_side_effects=True, vmem_limit_bytes=60 * 2**20)


def first_gather_kernel(depth, ring, count, shard, little, full, little_full, *sems):
    place = Place(depth, ring)
    place.greet()
    small = Gather(place, 1, little, little_full, sems[:7])
    big = Gather(place, count, shard, full, sems[7:])
    small.begin()
    big.begin()
    for i in range(big.steps()):
        if i < small.steps():
            small.step(i)
        big.step(i)
    small.finish()
    big.finish()


def first_gather(mesh, shards, little, ident):
    depth, ring = mesh.shape["dp"] // 2, mesh.shape["fsdp"]
    count = shards.shape[0]

    def full(a):
        return jax.ShapeDtypeStruct((a.shape[0], depth, 2, ring) + a.shape[1:], a.dtype)

    return pl.pallas_call(
        functools.partial(first_gather_kernel, depth, ring, count),
        out_shape=[full(shards), full(little)],
        in_specs=[ANY] * 2,
        out_specs=[ANY] * 2,
        scratch_shapes=Gather.sems(mesh, 1) + Gather.sems(mesh, count),
        compiler_params=remote_params(ident),
        cost_estimate=pl.CostEstimate(flops=60_000_000_000, bytes_accessed=2 * 33_554_432, transcendentals=0),
        name="first_gather",
    )(shards, little)


NN = (((1,), (0,)), ((), ()))
NT = (((1,), (1,)), ((), ()))
TN = (((0,), (0,)), ((), ()))
LOW = jnp.bfloat16
FULL = jnp.float32
SMEM = pl.BlockSpec(memory_space=pltpu.SMEM)
VMEM = pl.BlockSpec(memory_space=pltpu.VMEM)
PAIR = 2 * HD
ROOM = 60 * 2**20


def dot(left, right, how):
    return lax.dot_general(left, right, how, preferred_element_type=FULL)


def calls(kernel, name, flops, moved, **kw):
    return pl.pallas_call(
        kernel,
        name=name,
        compiler_params=pltpu.CompilerParams(vmem_limit_bytes=ROOM),
        cost_estimate=pl.CostEstimate(flops=int(flops), bytes_accessed=int(moved), transcendentals=0),
        **kw,
    )


def whole(shape):
    return pl.BlockSpec(shape, lambda *_: (0,) * len(shape))


def normal(x):
    mean = jnp.mean(x, axis=-1, keepdims=True)
    centred = x - mean
    rstd = lax.rsqrt(jnp.mean(centred * centred, axis=-1, keepdims=True) + EPSILON)
    return centred * rstd, rstd


def normal_back(hat, rstd, grad, gain):
    scaled = grad * gain
    lean = jnp.mean(scaled, axis=-1, keepdims=True)
    tilt = jnp.mean(scaled * hat, axis=-1, keepdims=True)
    back = rstd * (scaled - lean - hat * tilt)
    return back, jnp.sum(grad * hat, axis=0, keepdims=True), jnp.sum(grad, axis=0, keepdims=True)


def add_row(ref, value, first):
    @pl.when(first)
    def _():
        ref[...] = value

    @pl.when(jnp.logical_not(first))
    def _():
        ref[...] += value


GAIN, SHIFT, DOWN = 6, 9, 12


def lanes(shape):
    return lax.broadcasted_iota(jnp.int32, shape, len(shape) - 1)


def rows_of(shape):
    return lax.broadcasted_iota(jnp.int32, shape, 0)


def head_mask(head):
    return jnp.where(lanes((1, PAIR)) // HD == head, 1.0, 0.0).astype(LOW)


def thirds(x):
    one = x.astype(LOW).astype(FULL)
    two = (x - one).astype(LOW).astype(FULL)
    return one, two, x - one - two


def wide_keys(k, v, n):
    count = k.shape[0]
    shut = jnp.where((lanes((count, PAIR)) == 0) & (rows_of((count, PAIR)) >= n), NEGATIVE, 0.0).astype(LOW)
    ones = jnp.ones((count, PAIR), LOW)
    return [
        (jnp.concatenate([k * head_mask(h), shut], axis=1), jnp.concatenate([v * head_mask(h), ones], axis=1))
        for h in range(2)
    ]


def attend_pair(causal, tile, h, n, q, k, v, store, l_ref):
    queries, count = q.shape[0], k.shape[0]
    first = jnp.where(lanes((queries, PAIR)) == 0, 1.0, 0.0).astype(LOW)
    wide_q = jnp.concatenate([q, first], axis=1)
    spots = lanes((tile, PAIR))
    heads = wide_keys(k, v, n)
    for i in range(queries // tile):
        at = slice(i * tile, (i + 1) * tile)
        seen = (i + 1) * tile if causal else count
        mixed = jnp.zeros((tile, PAIR), FULL)
        kept = l_ref[at]
        for head, (keys, values) in enumerate(heads):
            scores = dot(wide_q[at], keys[:seen], NT)
            if causal:
                square = (tile, tile)
                last = jnp.where(lanes(square) <= rows_of(square), scores[:, seen - tile :], NEGATIVE)
                scores = last if seen == tile else jnp.concatenate([scores[:, : seen - tile], last], axis=1)
            top = jnp.max(scores, axis=1, keepdims=True)
            weights = jnp.exp(scores - top).astype(LOW)
            sums = dot(weights, values[:seen], NN)
            total = sums[:, PAIR:]
            mixed = mixed + sums[:, :PAIR] / total
            kept = jnp.where(spots == 2 * h + head, top + jnp.log(total), kept)
        store(at, mixed.astype(LOW))
        l_ref[at] = kept


def forward_kernel(
    depth, ring, count, n_ref, m_ref, x_hbm, e_hbm, w_hbm, p_ref, shard,
    full, a0_hbm, qkv_hbm, o0_hbm, l0_hbm, x1_hbm, a1_hbm, q1_hbm, kv_hbm, o1_hbm, l1_hbm,
    x_ref, e_ref, w_ref, a_ref, qkv_ref, o_ref, l0_ref, x1_ref, q1_ref, kv_ref, l1_ref, a1_ref,
    w_sem, in_sem, out_sem, *sems,
):
    place = Place(depth, ring)
    place.greet()
    gather = Gather(place, count, shard, full, sems)
    gather.begin()
    rows, width = x_ref.shape
    tile = 256
    load_x = pltpu.make_async_copy(x_hbm, x_ref, in_sem.at[0])
    load_e = pltpu.make_async_copy(e_hbm, e_ref, in_sem.at[1])
    load_x.start()
    parts = w_ref.shape[0]
    loads = [pltpu.make_async_copy(w_hbm.at[u], w_ref.at[u], w_sem.at[u]) for u in range(parts)]
    for load in loads[:3]:
        load.start()
    load_e.start()
    for load in loads[3:]:
        load.start()
    leaving = []

    def send(src, dst):
        copy = pltpu.make_async_copy(src, dst, out_sem.at[len(leaving)])
        copy.start()
        leaving.append(copy)

    l0_ref[...] = jnp.zeros_like(l0_ref)
    l1_ref[...] = jnp.zeros_like(l1_ref)
    load_x.wait()
    gather.step(0)
    for i in range(rows // tile):
        at = slice(i * tile, (i + 1) * tile)
        hat, _ = normal(x_ref[at].astype(FULL))
        a_ref[at] = (hat * p_ref[GAIN : GAIN + 1] + p_ref[SHIFT : SHIFT + 1]).astype(LOW)
    send(a_ref, a0_hbm)
    for j in range(3):
        loads[j].wait()
        bias = (p_ref[0:1], None, p_ref[1:2])[j]

        def project(i, j=j, bias=bias):
            at = pl.ds(pl.multiple_of(i * 2 * tile, 2 * tile), 2 * tile)
            y = dot(a_ref[at], w_ref[j], NN)
            if bias is not None:
                y = y + bias
            qkv_ref[j, at] = (y * SCALE if j == 0 else y).astype(LOW)

        loop(rows // (2 * tile), project)
        send(qkv_ref.at[j], qkv_hbm.at[j])
        if j == 1:
            gather.step(1)

    pairs = width // PAIR

    def self_pair(h):
        cols = pl.ds(pl.multiple_of(h * PAIR, PAIR), PAIR)

        def store(at, value):
            o_ref[at, cols] = value

        attend_pair(True, tile, h, n_ref[0], qkv_ref[0, :, cols], qkv_ref[1, :, cols], qkv_ref[2, :, cols], store, l0_ref)
        when(h % 2 == 0, lambda: gather.step(2 + h // 2))

    loop(pairs, self_pair)
    send(o_ref, o0_hbm)
    send(l0_ref, l0_hbm)
    done = 2 + (pairs + 1) // 2
    loads[3].wait()
    loads[4].wait()

    def middle_part(i):
        at = pl.ds(pl.multiple_of(i * tile, tile), tile)
        x1 = x_ref[at].astype(FULL) + (dot(o_ref[at], w_ref[3], NN) + p_ref[2:3])
        x1_ref[at] = x1
        hat, _ = normal(x1)
        a = (hat * p_ref[GAIN + 1 : GAIN + 2] + p_ref[SHIFT + 1 : SHIFT + 2]).astype(LOW)
        a1_ref[at] = a
        q1_ref[at] = ((dot(a, w_ref[4], NN) + p_ref[3:4]) * SCALE).astype(LOW)
        when(i % 2 == 1, lambda: gather.step(done + i // 2))

    loop(rows // tile, middle_part)
    done = done + rows // tile // 2
    send(x1_ref, x1_hbm)
    send(a1_ref, a1_hbm)
    send(q1_ref, q1_hbm.at[0])
    load_e.wait()
    for j in range(2):
        loads[5 + j].wait()
        y = dot(e_ref[...], w_ref[5 + j], NN)
        kv_ref[j] = (y + p_ref[4:5] if j == 1 else y).astype(LOW)
    send(kv_ref, kv_hbm)
    leaving[4].wait()

    def cross_pair(h):
        cols = pl.ds(pl.multiple_of(h * PAIR, PAIR), PAIR)

        def store(at, value):
            o_ref[at, cols] = value

        attend_pair(False, tile, h, m_ref[0], q1_ref[:, cols], kv_ref[0, :, cols], kv_ref[1, :, cols], store, l1_ref)
        when(h % 2 == 0, lambda: gather.step(done + h // 2))

    loop(pairs, cross_pair)
    done = done + (pairs + 1) // 2
    send(o_ref, o1_hbm)
    send(l1_ref, l1_hbm)
    for i in range(done, gather.steps()):
        gather.step(i)
    gather.finish()
    for k, copy in enumerate(leaving):
        if k != 4:
            copy.wait()


def forward(mesh, length, enc_count, x, memory, w, p, shards, ident):
    depth, ring = mesh.shape["dp"] // 2, mesh.shape["fsdp"]
    count = shards.shape[0]
    rows, width = x.shape
    enc = memory.shape[0]
    low = jax.ShapeDtypeStruct((rows, width), LOW)
    level = jax.ShapeDtypeStruct((rows, PAIR), FULL)
    out_shape = [
        jax.ShapeDtypeStruct((count, depth, 2, ring) + shards.shape[1:], LOW),
        low,
        jax.ShapeDtypeStruct((3, rows, width), LOW),
        low,
        level,
        jax.ShapeDtypeStruct((rows, width), FULL),
        low,
        jax.ShapeDtypeStruct((1, rows, width), LOW),
        jax.ShapeDtypeStruct((2, enc, width), LOW),
        low,
        level,
    ]
    big = pltpu.VMEM((rows, width), LOW)
    return pl.pallas_call(
        functools.partial(forward_kernel, depth, ring, count),
        out_shape=out_shape,
        in_specs=[SMEM, SMEM, ANY, ANY, ANY, VMEM, ANY],
        out_specs=[ANY] * len(out_shape),
        scratch_shapes=[
            big,
            pltpu.VMEM((enc, width), LOW),
            pltpu.VMEM(w.shape, LOW),
            big,
            pltpu.VMEM((3, rows, width), LOW),
            big,
            pltpu.VMEM((rows, PAIR), FULL),
            pltpu.VMEM((rows, width), FULL),
            big,
            pltpu.VMEM((2, enc, width), LOW),
            pltpu.VMEM((rows, PAIR), FULL),
            big,
            DMA((w.shape[0],)),
            DMA((2,)),
            DMA((12,)),
        ]
        + Gather.sems(mesh, count),
        compiler_params=remote_params(ident),
        cost_estimate=pl.CostEstimate(flops=70_000_000_000, bytes_accessed=2 * 33_554_432, transcendentals=0),
        name="forward_gather",
    )(length, enc_count, x, memory, w, p, shards)


def back_pair(causal, tile, h, n, q, k, v, mixed, grad, level, acc_ref, store):
    queries, count = q.shape[0], k.shape[0]
    lane_k, lane_q = lanes((count, PAIR)), lanes((queries, PAIR))
    shut = jnp.where(rows_of((count, PAIR)) >= n, NEGATIVE, 0.0)
    open_k = jnp.where(lane_k == 0, shut, jnp.where(lane_k < 4, 1.0, 0.0)).astype(LOW)
    open_v = jnp.where(lane_k < 3, 1.0, 0.0).astype(LOW)
    product = grad.astype(FULL) * mixed.astype(FULL)
    acc_ref[...] = jnp.zeros_like(acc_ref)
    heads = []
    for head in range(2):
        mask = head_mask(head)
        lse = jnp.sum(jnp.where(lane_q == 2 * h + head, level, 0.0), axis=1, keepdims=True)
        one, two, three = thirds(-lse)
        tail = jnp.where(lane_q == 0, 1.0, jnp.where(lane_q == 1, one, jnp.where(lane_q == 2, two, jnp.where(lane_q == 3, three, 0.0))))
        wide_q = jnp.concatenate([q, tail.astype(LOW)], axis=1)
        inner = jnp.sum(jnp.where(lane_q // HD == head, product, 0.0), axis=1, keepdims=True)
        one, two, three = thirds(-inner)
        tail = jnp.where(lane_q == 0, one, jnp.where(lane_q == 1, two, jnp.where(lane_q == 2, three, 0.0)))
        wide_g = jnp.concatenate([grad, tail.astype(LOW)], axis=1)
        wide_k = jnp.concatenate([k * mask, open_k], axis=1)
        wide_v = jnp.concatenate([v * mask, open_v], axis=1)
        heads.append((wide_q, wide_g, wide_k, wide_v, q * mask, grad * mask, k * mask))
    for i in range(count // tile):
        at = slice(i * tile, (i + 1) * tile)
        low = i * tile if causal else 0
        grad_k = jnp.zeros((tile, PAIR), FULL)
        grad_v = jnp.zeros((tile, PAIR), FULL)
        for wide_q, wide_g, wide_k, wide_v, q_one, g_one, k_one in heads:
            scores = dot(wide_k[at], wide_q[low:], NT)
            if causal:
                square = (tile, tile)
                near = jnp.where(rows_of(square) <= lanes(square), scores[:, :tile], NEGATIVE)
                scores = near if low + tile == queries else jnp.concatenate([near, scores[:, tile:]], axis=1)
            probs = jnp.exp(scores)
            slope = (probs * dot(wide_v[at], wide_g[low:], NT)).astype(LOW)
            grad_v = grad_v + dot(probs.astype(LOW), g_one[low:], NN)
            grad_k = grad_k + dot(slope, q_one[low:], NN)
            acc_ref[low:] += dot(slope, k_one[at], TN)
        store(at, grad_k.astype(LOW), grad_v.astype(LOW))


def unit_grad(place, held, slot, a_ref, b_ref, scale):
    depth, part = held.shape[1], held.shape[3]
    width = a_ref.shape[1]
    piece = width // 2
    for m in range(2):
        value = dot(a_ref[:, m * piece : (m + 1) * piece], b_ref[...], TN)
        if scale is not None:
            value = value * scale
        value = value.astype(LOW)
        for k in range(piece // part):
            at = m * (piece // part) + k
            held[slot, at // 2, at % 2] = value[k * part : (k + 1) * part]


def feed_scatter_kernel(
    depth, ring, n_ref, a2_hbm, g3_hbm, du_hbm, r_hbm, qkv_hbm, mixed_hbm, grad_hbm, l_ref,
    outs, dq_hbm, dkv_hbm,
    a2_ref, g3_ref, moving, held, q_buf, acc_ref, dq_buf, dkv_buf, in_sem, move_sem, q_sem, out_sem, *rest,
):
    place = Place(depth, ring)
    place.greet()
    blocks = du_hbm.shape[0]
    count = 2 * blocks
    sums = Scatter(place, count, outs.shape[1], held, outs, rest[:5], rest[5:])
    pairs = mixed_hbm.shape[1] // PAIR
    slots = held.shape[0]
    load_a = pltpu.make_async_copy(a2_hbm, a2_ref, in_sem.at[0])
    load_g = pltpu.make_async_copy(g3_hbm, g3_ref, in_sem.at[1])

    def move(u, array, j):
        return pltpu.make_async_copy(array.at[j], moving.at[u % 2], move_sem.at[u % 2])

    def start_move(u):
        when(u < blocks, lambda: move(u, du_hbm, u).start())
        when(u >= blocks, lambda: move(u, r_hbm, jnp.maximum(u - blocks, 0)).start())

    def fetch(h):
        cols = pl.ds(pl.multiple_of(h * PAIR, PAIR), PAIR)
        sources = [qkv_hbm.at[0, :, cols], qkv_hbm.at[1, :, cols], qkv_hbm.at[2, :, cols], mixed_hbm.at[:, cols], grad_hbm.at[:, cols]]
        return [pltpu.make_async_copy(s, q_buf.at[h % 2, k], q_sem.at[h % 2, k]) for k, s in enumerate(sources)]

    def put(h):
        cols = pl.ds(pl.multiple_of(h * PAIR, PAIR), PAIR)
        return [
            pltpu.make_async_copy(dq_buf.at[h % 2], dq_hbm.at[:, cols], out_sem.at[h % 2, 0]),
            pltpu.make_async_copy(dkv_buf.at[h % 2], dkv_hbm.at[:, :, cols], out_sem.at[h % 2, 1]),
        ]

    load_a.start()
    start_move(0)
    for copy in fetch(0):
        copy.start()
    load_g.start()
    load_a.wait()

    def weights(i):
        when(i + 1 < count, lambda: start_move(i + 1))
        when(i == blocks, load_g.wait)
        move(i, du_hbm, 0).wait()
        when(i >= slots, lambda: sums.core(i - slots).wait_send())
        slot = i % slots
        when(i < blocks, lambda: unit_grad(place, held, slot, a2_ref, moving.at[i % 2], None))
        when(i >= blocks, lambda: unit_grad(place, held, slot, moving.at[i % 2], g3_ref, None))
        sums.core(i).start()

    def heads(h):
        def next_fetch():
            for copy in fetch(h + 1):
                copy.start()

        when(h + 1 < pairs, next_fetch)
        for copy in fetch(h):
            copy.wait()

        def free():
            for copy in put(h - 2):
                copy.wait()

        when(h >= 2, free)
        b = h % 2

        def store(at, grad_k, grad_v):
            dkv_buf[b, 0, at] = grad_k
            dkv_buf[b, 1, at] = grad_v

        back_pair(True, 256, h, n_ref[0], q_buf[b, 0], q_buf[b, 1], q_buf[b, 2], q_buf[b, 3], q_buf[b, 4], l_ref[...], acc_ref, store)
        dq_buf[b] = acc_ref[...].astype(LOW)
        for copy in put(h):
            copy.start()

    def step(i):
        when(i < count, lambda: weights(i))
        sums.early(i)
        when(i < pairs, lambda: heads(i))
        sums.late(i)

    loop(max(sums.steps(), pairs), step)
    for h in range(max(0, pairs - 2), pairs):
        for copy in put(h):
            copy.wait()
    sums.finish()


def feed_scatter(mesh, length, a2, g3, du, r, qkv, mixed, grad, level, ident):
    depth, ring = mesh.shape["dp"] // 2, mesh.shape["fsdp"]
    blocks, rows, width = du.shape
    own = width // (2 * depth * ring)
    count = 2 * blocks
    big = pltpu.VMEM((rows, width), LOW)
    return pl.pallas_call(
        functools.partial(feed_scatter_kernel, depth, ring),
        out_shape=[
            jax.ShapeDtypeStruct((count, own, width), FULL),
            jax.ShapeDtypeStruct((rows, width), LOW),
            jax.ShapeDtypeStruct((2, rows, width), LOW),
        ],
        in_specs=[SMEM] + [ANY] * 7 + [VMEM],
        out_specs=[VMEM, ANY, ANY],
        scratch_shapes=[
            big,
            big,
            pltpu.VMEM((2, rows, width), LOW),
            pltpu.VMEM((3, depth, 2, ring * own, width), LOW),
            pltpu.VMEM((2, 5, rows, PAIR), LOW),
            pltpu.VMEM((rows, PAIR), FULL),
            pltpu.VMEM((2, rows, PAIR), LOW),
            pltpu.VMEM((2, 2, rows, PAIR), LOW),
            DMA((2,)),
            DMA((2,)),
            DMA((2, 5)),
            DMA((2, 2)),
        ]
        + Scatter.refs(mesh, count, own, width, LOW)
        + Scatter.sems(mesh, count),
        compiler_params=remote_params(ident),
        cost_estimate=pl.CostEstimate(flops=60_000_000_000, bytes_accessed=2 * 33_554_432, transcendentals=0),
        name="feed_scatter",
    )(length, a2, g3, du, r, qkv, mixed, grad, level)


def last_scatter_kernel(
    depth, ring, made_hbm, o1_hbm, g2_hbm, a1_hbm, dq1_hbm, o0_hbm, g1_hbm, a0_hbm, dq0_hbm, dkv_hbm, tiny_ref,
    outs, tiny_out, left, right, held, tiny_held, left_sem, right_sem, made_sem, *rest,
):
    place = Place(depth, ring)
    place.greet()
    made = made_hbm.shape[0]
    pairs = [(a1_hbm, dq1_hbm), (o1_hbm, g2_hbm), (o0_hbm, g1_hbm), (a0_hbm, dq0_hbm), (a0_hbm, dkv_hbm.at[0]), (a0_hbm, dkv_hbm.at[1])]
    scaled = (0, 3)
    count = made + len(pairs)
    small = Scatter(place, 1, tiny_out.shape[1], tiny_held, tiny_out, rest[:5], rest[5:11])
    sums = Scatter(place, count, outs.shape[1], held, outs, rest[11:16], rest[16:])
    slots = held.shape[0]

    def load(k):
        a, b = pairs[k]
        return [
            pltpu.make_async_copy(a, left.at[k % 2], left_sem.at[k % 2]),
            pltpu.make_async_copy(b, right.at[k % 2], right_sem.at[k % 2]),
        ]

    given = [pltpu.make_async_copy(made_hbm.at[u], held.at[u], made_sem.at[u]) for u in range(made)]
    for copy in given:
        copy.start()
    for k in range(2):
        for copy in load(k):
            copy.start()
    tiny_held[0] = tiny_ref[...]
    small.core(0).start()
    for i in range(sums.steps()):
        if i < count:
            k = i - made
            if i < made:
                given[i].wait()
            else:
                for copy in load(k):
                    copy.wait()
                if i >= slots:
                    sums.core(i - slots).wait_send()
                unit_grad(place, held, i % slots, left.at[k % 2], right.at[k % 2], SCALE if k in scaled else None)
                if k + 2 < len(pairs):
                    for copy in load(k + 2):
                        copy.start()
            sums.core(i).start()
        if i < small.steps():
            small.early(i)
        sums.early(i)
        if i < small.steps():
            small.late(i)
        sums.late(i)
    small.finish()
    sums.finish()


def last_scatter(mesh, made, pairs, tiny, ident):
    depth, ring = mesh.shape["dp"] // 2, mesh.shape["fsdp"]
    n, width = made.shape[0], made.shape[-1]
    rows = pairs[0].shape[0]
    own = made.shape[3] // ring
    count = n + 6
    tiny_rows = tiny.shape[2] // ring
    return pl.pallas_call(
        functools.partial(last_scatter_kernel, depth, ring),
        out_shape=[
            jax.ShapeDtypeStruct((count, own, width), FULL),
            jax.ShapeDtypeStruct((1, tiny_rows, tiny.shape[3]), FULL),
        ],
        in_specs=[ANY] * (1 + len(pairs)) + [VMEM],
        out_specs=[VMEM, VMEM],
        scratch_shapes=[
            pltpu.VMEM((2, rows, width), LOW),
            pltpu.VMEM((2, rows, width), LOW),
            pltpu.VMEM((3,) + made.shape[1:], LOW),
            pltpu.VMEM((1,) + tiny.shape, FULL),
            DMA((2,)),
            DMA((2,)),
            DMA((n,)),
        ]
        + Scatter.refs(mesh, 1, tiny_rows, tiny.shape[3], FULL)
        + Scatter.sems(mesh, 1)
        + Scatter.refs(mesh, count, own, width, LOW)
        + Scatter.sems(mesh, count),
        compiler_params=remote_params(ident),
        cost_estimate=pl.CostEstimate(flops=60_000_000_000, bytes_accessed=2 * 33_554_432, transcendentals=0),
        name="last_scatter",
    )(made, *pairs, tiny)


CUBIC = 0.044715
ROOT = 0.7978845608028654


def feed_kernel(
    n_ref, x1_ref, o_ref, g_ref, w_hbm, p_ref, bu_ref,
    out_ref, r_ref, du_ref, a_ref, g3_ref, dx_ref, g2_ref, do_ref,
    sum_up, sum_down, sum_five, sum_gain, sum_shift,
    w_ref, slope_ref, sems,
):
    i = pl.program_id(0)
    first = i == 0
    tile, width = x1_ref.shape
    blocks = (w_hbm.shape[0] - 1) // 2
    order = [0] + [k * blocks + j + 1 for j in range(blocks) for k in range(2)]
    loads = {u: pltpu.make_async_copy(w_hbm.at[u], w_ref.at[u], sems.at[u]) for u in order}

    def ready(u):
        pl.when(first)(loads[u].wait)

    @pl.when(first)
    def _():
        for u in order:
            loads[u].start()
        loads[0].wait()

    valid = jnp.where(i * tile + rows_of((tile, 1)) < n_ref[0], 1.0, 0.0)
    x2 = x1_ref[...] + (dot(o_ref[...], w_ref[0], NN) + p_ref[5:6])
    hat, rstd = normal(x2)
    gain = p_ref[GAIN + 2 : GAIN + 3]
    a_ref[...] = (hat * gain + p_ref[SHIFT + 2 : SHIFT + 3]).astype(LOW)

    total = x2 + p_ref[DOWN : DOWN + 1]
    for j in range(blocks):
        cols = slice(j * width, (j + 1) * width)
        ready(1 + j)
        u = dot(a_ref[...], w_ref[1 + j], NN) + bu_ref[:, cols]
        square = u * u
        t = jnp.tanh(ROOT * (u * (1.0 + CUBIC * square)))
        half = 0.5 * (1.0 + t)
        r = (u * half).astype(LOW)
        r_ref[j] = r
        slope = half + 0.5 * u * (1.0 - t * t) * (ROOT * (1.0 + 3.0 * CUBIC * square))
        slope_ref[:, cols] = slope.astype(LOW)
        ready(1 + blocks + j)
        total = total + dot(r, w_ref[1 + blocks + j], NN)
    out_ref[...] = (total * valid).astype(LOW)
    grad_out = g_ref[...].astype(FULL) * valid
    g3 = grad_out.astype(LOW)
    g3_ref[...] = g3
    grad = jnp.zeros((tile, width), FULL)
    for j in range(blocks):
        cols = slice(j * width, (j + 1) * width)
        du = (dot(g3, w_ref[1 + blocks + j], NT) * slope_ref[:, cols].astype(FULL)).astype(LOW)
        du_ref[j] = du
        line = jnp.sum(du.astype(FULL), axis=0, keepdims=True)

        @pl.when(first)
        def _():
            sum_up[:, cols] = line

        @pl.when(jnp.logical_not(first))
        def _():
            sum_up[:, cols] += line

        grad = grad + dot(du, w_ref[1 + j], NT)
    back, lines, shifts = normal_back(hat, rstd, grad, gain)
    dx2 = grad_out + back
    dx_ref[...] = dx2
    g2 = dx2.astype(LOW)
    g2_ref[...] = g2
    do_ref[...] = dot(g2, w_ref[0], NT).astype(LOW)
    add_row(sum_down, jnp.sum(g3.astype(FULL), axis=0, keepdims=True), first)
    add_row(sum_five, jnp.sum(g2.astype(FULL), axis=0, keepdims=True), first)
    add_row(sum_gain, lines, first)
    add_row(sum_shift, shifts, first)


def feed(length, x1, mixed, cotangent, w, p, bias_up, tile=256):
    rows, width = x1.shape
    blocks = (w.shape[0] - 1) // 2
    inner = blocks * width
    part = pl.BlockSpec((tile, width), lambda i: (i, 0))
    broad = pl.BlockSpec((blocks, tile, width), lambda i: (0, i, 0))
    low = jax.ShapeDtypeStruct((rows, width), LOW)
    wide = jax.ShapeDtypeStruct((blocks, rows, width), LOW)
    line = jax.ShapeDtypeStruct((1, width), FULL)
    return calls(
        feed_kernel,
        "feed",
        2 * rows * width * (4 * inner + 2 * width),
        2 * rows * (9 * width + 2 * inner) + 4 * inner * width,
        grid=(rows // tile,),
        in_specs=[SMEM, part, part, part, ANY, whole(p.shape), whole(bias_up.shape)],
        out_specs=[part, broad, broad, part, part, part, part, part, whole((1, inner))] + [whole((1, width))] * 4,
        out_shape=[low, wide, wide, low, low, jax.ShapeDtypeStruct((rows, width), FULL), low, low,
                   jax.ShapeDtypeStruct((1, inner), FULL), line, line, line, line],
        scratch_shapes=[pltpu.VMEM(w.shape, LOW), pltpu.VMEM((tile, inner), LOW), DMA((w.shape[0],))],
    )(length, x1, mixed, cotangent, w, p, bias_up)


def unit_of(w, u):
    return pl.BlockSpec((1,) + w.shape[1:], lambda *_: (u, 0, 0))


def cross_attend_back_kernel(n_ref, q_ref, k_ref, v_ref, o_ref, g_ref, l_ref, dq_ref, dkv_ref, acc_ref):
    def store(at, grad_k, grad_v):
        dkv_ref[0, at] = grad_k
        dkv_ref[1, at] = grad_v

    h = pl.program_id(0)
    back_pair(False, k_ref.shape[1], h, n_ref[0], q_ref[0], k_ref[0], v_ref[0], o_ref[...], g_ref[...], l_ref[...], acc_ref, store)
    dq_ref[...] = acc_ref[...].astype(LOW)


def cross_attend_back(count, q, kv, mixed, grad, level):
    rows, width = mixed.shape
    enc = kv.shape[1]

    def cut(part, n):
        return pl.BlockSpec((1, n, PAIR), lambda h: (part, 0, h))

    column = pl.BlockSpec((rows, PAIR), lambda h: (0, h))
    return calls(
        cross_attend_back_kernel,
        "cross_attend_back",
        4 * 10 * rows * enc * width,
        2 * (4 * rows + 4 * enc) * width,
        grid=(width // PAIR,),
        in_specs=[SMEM, cut(0, rows), cut(0, enc), cut(1, enc), column, column, whole((rows, PAIR))],
        out_specs=[column, pl.BlockSpec((2, enc, PAIR), lambda h: (0, 0, h))],
        out_shape=[jax.ShapeDtypeStruct((rows, width), LOW), jax.ShapeDtypeStruct((2, enc, width), LOW)],
        scratch_shapes=[pltpu.VMEM((rows, PAIR), FULL)],
    )(count, q, kv, kv, mixed, grad, level)


def memory_grad_kernel(e_ref, b_ref, w_ref, o_ref, de_ref, sum_v, acc_ref):
    j = pl.program_id(0)
    o_ref[0] = dot(e_ref[...], b_ref[0], TN).astype(LOW)

    @pl.when(j == 0)
    def _():
        acc_ref[...] = dot(b_ref[0], w_ref[0], NT)

    @pl.when(j == 1)
    def _():
        de_ref[...] = (acc_ref[...] + dot(b_ref[0], w_ref[0], NT)).astype(LOW)
        sum_v[...] = jnp.sum(b_ref[0].astype(FULL), axis=0, keepdims=True)


def memory_grad(memory, dkv, w):
    count, width = memory.shape
    return calls(
        memory_grad_kernel,
        "memory_grad",
        8 * count * width * width,
        8 * width * width,
        grid=(2,),
        in_specs=[
            whole(memory.shape),
            pl.BlockSpec((1, count, width), lambda j: (j, 0, 0)),
            pl.BlockSpec((1, width, width), lambda j: (5 + j, 0, 0)),
        ],
        out_specs=[pl.BlockSpec((1, width, width), lambda j: (j, 0, 0)), whole(memory.shape), whole((1, width))],
        out_shape=[
            jax.ShapeDtypeStruct((2, width, width), LOW),
            jax.ShapeDtypeStruct((count, width), LOW),
            jax.ShapeDtypeStruct((1, width), FULL),
        ],
        scratch_shapes=[pltpu.VMEM((count, width), FULL)],
    )(memory, dkv, w)


def cross_back_kernel(x1_ref, dq_ref, dx2_ref, wq_ref, wo_ref, p_ref, dx_ref, g1_ref, do_ref,
                      sum_q, sum_out, sum_gain, sum_shift):
    first = pl.program_id(0) == 0
    grad = dot(dq_ref[...], wq_ref[0], NT) * SCALE
    hat, rstd = normal(x1_ref[...])
    back, lines, shifts = normal_back(hat, rstd, grad, p_ref[GAIN + 1 : GAIN + 2])
    dx1 = dx2_ref[...] + back
    dx_ref[...] = dx1
    g1 = dx1.astype(LOW)
    g1_ref[...] = g1
    do_ref[...] = dot(g1, wo_ref[0], NT).astype(LOW)
    add_row(sum_q, jnp.sum(dq_ref[...].astype(FULL), axis=0, keepdims=True) * SCALE, first)
    add_row(sum_out, jnp.sum(g1.astype(FULL), axis=0, keepdims=True), first)
    add_row(sum_gain, lines, first)
    add_row(sum_shift, shifts, first)


def cross_back(x1, dq, dx2, w, p, tile=256):
    rows, width = x1.shape
    part = pl.BlockSpec((tile, width), lambda i: (i, 0))
    low = jax.ShapeDtypeStruct((rows, width), LOW)
    line = jax.ShapeDtypeStruct((1, width), FULL)
    return calls(
        cross_back_kernel,
        "cross_back",
        4 * rows * width * width,
        16 * rows * width + 4 * width * width,
        grid=(rows // tile,),
        in_specs=[part, part, part, unit_of(w, 4), unit_of(w, 3), whole(p.shape)],
        out_specs=[part, part, part] + [whole((1, width))] * 4,
        out_shape=[jax.ShapeDtypeStruct((rows, width), FULL), low, low, line, line, line, line],
    )(x1, dq, dx2, w, w, p)


def self_back_kernel(x_ref, dq_ref, dkv_ref, dx1_ref, w_ref, p_ref, dx_ref, sum_q, sum_v, sum_gain, sum_shift):
    first = pl.program_id(0) == 0
    dq = dq_ref[...]
    grad = dot(dq, w_ref[0], NT) * SCALE + dot(dkv_ref[0], w_ref[1], NT) + dot(dkv_ref[1], w_ref[2], NT)
    hat, rstd = normal(x_ref[...].astype(FULL))
    back, lines, shifts = normal_back(hat, rstd, grad, p_ref[GAIN : GAIN + 1])
    dx_ref[...] = (dx1_ref[...] + back).astype(LOW)
    add_row(sum_q, jnp.sum(dq.astype(FULL), axis=0, keepdims=True) * SCALE, first)
    add_row(sum_v, jnp.sum(dkv_ref[1].astype(FULL), axis=0, keepdims=True), first)
    add_row(sum_gain, lines, first)
    add_row(sum_shift, shifts, first)


def self_back(x, dq, dkv, dx1, w, p, tile=256):
    rows, width = x.shape
    part = pl.BlockSpec((tile, width), lambda i: (i, 0))
    line = jax.ShapeDtypeStruct((1, width), FULL)
    return calls(
        self_back_kernel,
        "self_back",
        6 * rows * width * width,
        14 * rows * width + 6 * width * width,
        grid=(rows // tile,),
        in_specs=[part, part, pl.BlockSpec((2, tile, width), lambda i: (0, i, 0)), part, whole((3, width, width)), whole(p.shape)],
        out_specs=[part] + [whole((1, width))] * 4,
        out_shape=[jax.ShapeDtypeStruct((rows, width), LOW), line, line, line, line],
    )(x, dq, dkv, dx1, w, p)


AXES = ("dp", "fsdp")


def exchange(array):
    return lax.all_to_all(array, AXES, split_axis=0, concat_axis=0, tiled=True)


def leave(array, slots):
    return exchange(array.reshape(slots, -1, array.shape[-1]))


def after(value, *others):
    return lax.optimization_barrier((value, *others))[0]


def per_device(
    mesh,
    units,
    encoder,
    cotangent,
    deal,
    lengths,
    enc_counts,
    self_qkv,
    self_out,
    cross_qkv,
    cross_out,
    ffn_up,
    ffn_down,
    biases,
    ffn_bias_up,
    ffn_bias_down,
    norm_gain,
    norm_shift,
):
    slots = deal.shape[0]
    depth, ring = mesh.shape["dp"] // 2, mesh.shape["fsdp"]
    own, width = self_out.shape
    blocks = ffn_up.shape[1] // width
    inverse = jnp.zeros((slots,), jnp.int32).at[deal].set(jnp.arange(slots, dtype=jnp.int32))
    place = lax.axis_index(AXES)
    length = lax.dynamic_slice_in_dim(lengths, place, 1)
    enc_count = lax.dynamic_slice_in_dim(enc_counts, place, 1)
    tokens = units.shape[1]
    arrived = exchange(jnp.take(jnp.concatenate([units, encoder], axis=1), deal, axis=0))
    x = arrived[:, :tokens].reshape(-1, width)
    memory = arrived[:, tokens:].reshape(-1, width)

    up = ffn_up.reshape(own, slots, blocks, own).transpose(2, 0, 1, 3).reshape(blocks, own, width)
    early = jnp.concatenate([self_qkv, self_out[None], cross_qkv])
    late = jnp.concatenate([cross_out[None], up, ffn_down.reshape(blocks, own, width)])
    rows = jnp.concatenate([biases, norm_gain, norm_shift, ffn_bias_down[None]])
    flat = jnp.concatenate([rows.reshape(-1), ffn_bias_up])
    size = -(-flat.shape[0] // 2048) * 2048
    little = jnp.pad(flat, (0, size - flat.shape[0])).reshape(1, size // 128, 128)
    w_one, little = first_gather(mesh, early, little, 0)
    w_one = w_one.reshape(early.shape[0], width, width)
    flat = little.reshape(slots, size).astype(FULL)
    p = flat[:, : rows.size].reshape((slots,) + rows.shape)
    p = jnp.moveaxis(p, 0, 1).reshape(rows.shape[0], -1)
    p = jnp.pad(p, ((0, 16 - rows.shape[0]), (0, 0)))
    bias_up = flat[:, rows.size : rows.size + ffn_bias_up.size].reshape(slots, blocks, own)
    bias_up = bias_up.transpose(1, 0, 2).reshape(1, -1)

    cot = exchange(jnp.take(after(cotangent, arrived), deal, axis=0)).reshape(-1, width)
    w_two, a0, qkv, mixed0, level0, x1, a1, q1, kv1, mixed1, level1 = forward(
        mesh, length, enc_count, x, memory, w_one, p, late, 1
    )
    w_two = w_two.reshape(late.shape[0], width, width)
    (result, r, du, a2, g3, dx2, g2, grad_mixed1, bias_up_grad, bias_down_grad, bias_five, gain_two, shift_two) = feed(
        length, x1, mixed1, cot, w_two, p, bias_up
    )
    result = leave(result, slots)
    dq1, dkv1 = cross_attend_back(enc_count, q1, kv1, mixed1, grad_mixed1, level1)
    dx1, g1, grad_mixed0, bias_three, bias_two, gain_one, shift_one = cross_back(x1, dq1, dx2, w_one, p)
    made, grad_memory, bias_four = memory_grad(memory, dkv1, w_one)
    grad_memory = leave(after(grad_memory, result), slots)
    sums_one, dq0, dkv0 = feed_scatter(mesh, length, a2, g3, du, r, qkv, mixed0, grad_mixed0, level0, 2)
    dx, bias_zero, bias_one, gain_zero, shift_zero = self_back(x, dq0, dkv0, dx1, w_one, p)
    dx = leave(after(dx, grad_memory), slots)

    bias_up_grad = bias_up_grad.reshape(blocks, slots, own).transpose(1, 0, 2).reshape(slots, -1)

    def by_owner(*lines):
        return jnp.concatenate(lines).reshape(len(lines), slots, own).transpose(1, 0, 2).reshape(slots, -1)

    terms = jnp.concatenate(
        [
            by_owner(
                bias_zero, bias_one, bias_two, bias_three, bias_four, bias_five, bias_down_grad,
                gain_zero, gain_one, gain_two, shift_zero, shift_one, shift_two,
            ),
            bias_up_grad,
        ],
        axis=1,
    )
    tiny = -(-terms.shape[1] // 1024) * 8
    terms = jnp.pad(terms, ((0, 0), (0, tiny * 128 - terms.shape[1]))).reshape(depth, 2, ring * tiny, 128)
    part = ring * own
    pairs = (mixed1, g2, a1, dq1, mixed0, g1, a0, dq0, dkv0)
    sums_two, tiny_sums = last_scatter(mesh, made.reshape(2, depth, 2, part, width), pairs, terms, 3)
    flat = tiny_sums.reshape(-1)
    lines = flat[: 13 * own].reshape(13, own)
    up_sum = sums_one[:blocks].reshape(blocks, own, slots, own).transpose(1, 2, 0, 3).reshape(own, -1)
    return (
        jnp.take(result, inverse, axis=0),
        jnp.take(dx, inverse, axis=0),
        jnp.take(grad_memory, inverse, axis=0),
        sums_two[5:8],
        sums_two[4],
        jnp.concatenate([sums_two[2:3], sums_two[0:2]]),
        sums_two[3],
        up_sum,
        sums_one[blocks:].reshape(blocks * own, width),
        lines[:6],
        flat[13 * own : 13 * own + ffn_bias_up.size],
        lines[6],
        lines[7:10],
        lines[10:13],
    )


def solution(mesh):
    middle_rows = P(None, AXES, None)
    first_rows = P(AXES, None)
    last = P(None, AXES)
    weights = (middle_rows, first_rows, middle_rows, first_rows, first_rows, first_rows, last, P(AXES), P(AXES), last, last)
    return jax.shard_map(
        functools.partial(per_device, mesh),
        mesh=mesh,
        in_specs=(middle_rows,) * 3 + (P(),) * 3 + weights,
        out_specs=(middle_rows,) * 3 + weights,
        check_vma=False,
    )
```

time: 2960 us -> 736 us (0.25)
  waiting for transfers between devices: 1620 us -> 5.47 us
  Pallas kernels: 0 us -> 619 us
  blocking collectives: 487 us -> 0 us
  matrix products: 441 us -> 0 us
  other arithmetic: 195 us -> 23.6 us
  local copies, waits for them, and re-layouts: 153 us -> 49.9 us
    reduce_scatter x6 -> x0, waiting for transfers between devices: 1510 us -> none  [the longest x1 362 us: per_device(): lax.psum_scatter(grad_down, ('dp', 'fsdp'), scatter_dimension=0, tiled=True)]
    pallas_call x0 -> x9, Pallas kernels: none -> 619 us  [the longest x1 141 us: forward(): pl.pallas_call(functools.partial(forward_kernel, depth, ring, count), out...]
    dot_general x58 -> x0, matrix products: 441 us -> none  [the longest x10 71.6 us: product(): return jnp.dot(left, right, preferred_element_type=jnp.float32)]
    all_gather x4 -> x0, blocking collectives: 297 us -> none  [the longest x1 102 us: per_device(): lax.all_gather(ffn_bias_up, ('dp', 'fsdp'), axis=0, tiled=True)]
    unnamed x2 -> x0, blocking collectives: 107 us -> none
    unnamed x18 -> x0, waiting for transfers between devices: 92.5 us -> none
    all_to_all x1 -> x0, blocking collectives: 82.9 us -> none  [per_device(): lax.all_to_all(dealt_units, ('dp', 'fsdp'), split_axis=0, concat_axis=1,...]
    convert_element_type x15 -> x0, other arithmetic: 72.7 us -> none  [the longest x4 61.3 us: one_block(): grad_scores = (probs * (grad_probs - inner)).astype(jnp.bfloat16)]
  transfers between devices with their start and end apart: 20 -> 5, of which waited for: 8 -> 1; matrix products, arithmetic and copies ran while one was open for 14% -> 6% of each run, Pallas kernels for 0% -> 75%
where the time goes in v3:
time: 736 us; the launch traced here: 730 us
  Pallas kernels  619 us (84%)
  local copies, waits for them, and re-layouts  49.9 us (7%)
  starting transfers between devices  30.7 us (4%)
  other arithmetic  23.6 us (3%)
    pallas_call x1, Pallas kernels, forward(): pl.pallas_call(functools.partial(forward_kernel, depth, ring, count), out...  141 us
    pallas_call x1, Pallas kernels, first_gather(): pl.pallas_call(functools.partial(first_gather_kernel, depth, ring, count)...  132 us
    pallas_call x1, Pallas kernels, last_scatter(): pl.pallas_call(functools.partial(last_scatter_kernel, depth, ring), out_s...  121 us
    pallas_call x1, Pallas kernels, feed_scatter(): pl.pallas_call(functools.partial(feed_scatter_kernel, depth, ring), out_s...  100 us
    pallas_call x1, Pallas kernels, feed(): calls(feed_kernel, 'feed', 2 * rows * width * (4 * inner + 2 * width), 2...  69.1 us
    all_to_all x5, starting transfers between devices, exchange(): return lax.all_to_all(array, AXES, split_axis=0, concat_axis=0, tiled=True)  30.7 us
    pallas_call x1, Pallas kernels, cross_attend_back(): calls(cross_attend_back_kernel, 'cross_attend_back', 4 * 10 * rows * enc...  21.7 us
    pallas_call x1, Pallas kernels, self_back(): calls(self_back_kernel, 'self_back', 6 * rows * width * width, 14 * rows...  14.7 us
  transfers between devices with their start and end apart: 5, of which 1 were waited for; matrix products, arithmetic and copies ran while one was open for 6% of the time, Pallas kernels for 75%

profile of v3, /device:TPU:0, one launch (start us, length us, event | category | flops | bytes accessed | tf_op | source)
XLA Modules:
  0.0 730.5 jit_solution(1132731579367029599)
XLA Ops:
  2.2 3.6 pad_maximum_fusion
  5.8 4.0 gather_fusion
  9.8 3.6 broadcast_select_fusion
  13.4 7.4 %all-to-all-start = ((bf16[32,40,1024]{2,1,0:T(8,128)(2,1)}), bf16[32,40,1024]{2,1,0:T(8,128)(2,1)}, u32[]{:S(2)}, u32[]{:S(2)}) async-start(bf16[32,40,1024]{2,1,0:T(8,128)(2,1)} %broadcast_select_fusion), calls=%async_computation | async-start | bytes 5242880 | tf_op jit(solution)/shard_map/all_to_all | solution.py:1141
  22.5 131.9 %first_gather.1 = (bf16[7,4,2,4,32,1024]{5,4,3,2,1,0:T(8,128)(2,1)}, bf16[1,4,2,4,16,128]{5,4,3,2,1,0:T(8,128)(2,1)}) custom-call(bf16[7,32,1024]{2,1,0:T(8,128)(2,1)} %pad_maximum_fusion.2.shard, bf16[1,16,128]{2,1,0:T(8,128)(2,1)} %fusion.3.little), custom_call_target="tpu_custom_call" | custom-call | flops 60000002048 | bytes 67108864 | tf_op jit(solution)/shard_map/first_gather/pallas_call | solution.py:342
  166.7 3.2 broadcast_select_fusion.3
  169.9 8.2 %all-to-all-start.1 = ((bf16[32,32,1024]{2,1,0:T(8,128)(2,1)}), bf16[32,32,1024]{2,1,0:T(8,128)(2,1)S(1)}, u32[]{:S(2)}, u32[]{:S(2)}) async-start(bf16[32,32,1024]{2,1,0:T(8,128)(2,1)} %broadcast_select_fusion.3), calls=%async_computation.1 | async-start | bytes 4194304 | tf_op jit(solution)/shard_map/all_to_all | solution.py:1141
  178.0 3.2 slice.92
  183.1 141.2 %forward_gather.1 = (bf16[9,4,2,4,32,1024]{5,4,3,2,1,0:T(8,128)(2,1)}, bf16[1024,1024]{1,0:T(8,128)(2,1)}, bf16[3,1024,1024]{2,1,0:T(8,128)(2,1)}, bf16[1024,102...) custom-call(s32[1]{0:T(128)} %dynamic_slice.6.n_ref, ...), custom_call_target="tpu_custom_call" | custom-call | flops 70000001024 | bytes 67108864 | tf_op jit(solution)/shard_map/forward_gather/pallas_call | solution.py:603
  325.6 69.1 %feed.1 = (bf16[1024,1024]{1,0:T(8,128)(2,1)}, bf16[4,1024,1024]{2,1,0:T(8,128)(2,1)}, bf16[4,1024,1024]{2,1,0:T(8,128)(2,1)}, bf16[1024,1024]{1,0:T(8,128)(2,1)...) custom-call(s32[1]{0:T(128)} %dynamic_slice.6.n_ref, ...), custom_call_target="tpu_custom_call" | custom-call | flops 38654705664 | bytes 52428800 | tf_op jit(solution)/shard_map/feed/pallas_call | solution.py:988
  394.8 4.4 all-to-all-start.2
  401.2 21.7 %cross_attend_back.1 = (bf16[1024,1024]{1,0:T(8,128)(2,1)}, bf16[2,256,1024]{2,1,0:T(8,128)(2,1)}) custom-call(s32[1]{0:T(128)} %dynamic_slice.7.m_ref.n_ref, bf16[1,1024,1024]{2,1,0:T(8,128)(2,1)} %get-tuple-element.79.q_ref, bf16[2,256,1024]{2,1,0:T(8,128)(2,1)} %get-tuple-element.80.k_ref.v_ref, bf16[2,256,1024]{2,1,0:T(8,128)(2,1)} %get-tuple-element.80.k_ref.v_ref, ...), custom_call_target="tpu_custom_call" | custom-call | flops 10737418240 | bytes 10485760 | tf_op jit(solution)/shard_map/cross_attend_back/pallas_call | solution.py:1024
  422.9 6.4 memory_grad.1
  429.3 13.2 %cross_back.1 = (f32[1024,1024]{1,0:T(8,128)}, bf16[1024,1024]{1,0:T(8,128)(2,1)}, bf16[1024,1024]{1,0:T(8,128)(2,1)}, f32[1,1024]{1,0:T(1,128)}, f32[1,1024]{1,...) custom-call(f32[1024,1024]{1,0:T(8,128)} %get-tuple-element.68.x1_ref, ...), custom_call_target="tpu_custom_call" | custom-call | flops 4294967296 | bytes 20971520 | tf_op jit(solution)/shard_map/cross_back/pallas_call | solution.py:1096
  442.5 5.5 all-to-all-done.2
  447.9 4.4 all-to-all-start.3
  452.3 100.0 %feed_scatter.1 = (f32[8,32,1024]{2,1,0:T(8,128)}, bf16[1024,1024]{1,0:T(8,128)(2,1)}, bf16[2,1024,1024]{2,1,0:T(8,128)(2,1)}) custom-call(s32[1]{0:T(128)} %dynamic_slice.6.n_ref, bf16[1024,1024]{1,0:T(8,128)(2,1)} %get-tuple-element.73.a2_hbm, bf16[1024,1024]{1,0:T(8,128)(2,1)} %get-tuple-element.74.g3_hbm, ...), custom_call_target="tpu_custom_call" | custom-call | flops 60000002048 | bytes 67108864 | tf_op jit(solution)/shard_map/feed_scatter/pallas_call | solution.py:782
  552.4 14.7 %self_back.1 = (bf16[1024,1024]{1,0:T(8,128)(2,1)}, f32[1,1024]{1,0:T(1,128)}, f32[1,1024]{1,0:T(1,128)}, f32[1,1024]{1,0:T(1,128)}, f32[1,1024]{1,0:T(1,128)}) custom-call(bf16[1024,1024]{1,0:T(8,128)(2,1)} %bitcast.47, bf16[1024,1024]{1,0:T(8,128)(2,1)} %get-tuple-element.87.dq_ref.dq0_hbm, bf16[2,1024,1024]{2,1,0:T(8,128)(2,1)} %get-tuple-element.88.dkv_ref.dkv_hbm, ...), custom_call_target="tpu_custom_call" | custom-call | flops 6442450944 | bytes 20971520 | tf_op jit(solution)/shard_map/self_back/pallas_call | solution.py:1125
  571.3 6.4 all-to-all-start.4
  577.7 121.2 %last_scatter.1 = (f32[8,32,1024]{2,1,0:T(8,128)}, f32[1,8,128]{2,1,0:T(8,128)}) custom-call(bf16[2,4,2,128,1024]{4,3,2,1,0:T(8,128)(2,1)} %bitcast.66, bf16[1024,1024]{1,0:T(8,128)(2,1)} %get-tuple-element.69.o_ref.o1_hbm, bf16[1024,1024]{1,0:T(8,128)(2,1)} %get-tuple-element.96.g2_hbm, bf16[1024,1024]{1,0:T(8,128)(2,1)} %get-tuple-element.97.a1_hbm, ...), custom_call_target="tpu_custom_call" | custom-call | flops 60000002048 | bytes 67108864 | tf_op jit(solution)/shard_map/last_scatter/pallas_call | solution.py:874
  707.1 3.1 copy.40
  710.2 4.6 reshape.166
  721.8 3.7 gather_fusion.4
  725.5 4.8 broadcast_select_fusion.1
  (125 shorter events, 39.8 us)
Async XLA Ops:
  0.6 163.8 %copy-start = (bf16[32,32,1024]{2,1,0:T(8,128)(2,1)S(1)}, bf16[32,32,1024]{2,1,0:T(8,128)(2,1)}, u32[]{:S(2)}) copy-start(bf16[32,32,1024]{2,1,0:T(8,128)(2,1)} %param.21) | copy-start | bytes 6291460
  13.3 8.3 %copy-start.7 = (bf16[3,32,1024]{2,1,0:T(8,128)(2,1)S(1)}, bf16[3,32,1024]{2,1,0:T(8,128)(2,1)}, u32[]{:S(2)}) copy-start(bf16[3,32,1024]{2,1,0:T(8,128)(2,1)} %param.27) | copy-start | bytes 589828
  13.4 8.3 %copy-start.8 = (bf16[3,32,1024]{2,1,0:T(8,128)(2,1)S(1)}, bf16[3,32,1024]{2,1,0:T(8,128)(2,1)}, u32[]{:S(2)}) copy-start(bf16[3,32,1024]{2,1,0:T(8,128)(2,1)} %param.25) | copy-start | bytes 589828
  13.4 8.3 %copy-start.9 = (bf16[32,1024]{1,0:T(8,128)(2,1)S(1)}, bf16[32,1024]{1,0:T(8,128)(2,1)}, u32[]{:S(2)}) copy-start(bf16[32,1024]{1,0:T(8,128)(2,1)} %param.26) | copy-start | bytes 196612
  13.4 151.1 %all-to-all-start = ((bf16[32,40,1024]{2,1,0:T(8,128)(2,1)}), bf16[32,40,1024]{2,1,0:T(8,128)(2,1)}, u32[]{:S(2)}, u32[]{:S(2)}) async-start(bf16[32,40,1024]{2,1,0:T(8,128)(2,1)} %broadcast_select_fusion), calls=%async_computation | async-start | bytes 5242880 | tf_op jit(solution)/shard_map/all_to_all | solution.py:1141
  22.5 132.9 %copy-start.31 = (s32[32]{0:T(128)S(1)}, s32[32]{0:T(128)}, u32[]{:S(2)}) copy-start(s32[32]{0:T(128)} %param.23) | copy-start | bytes 388
  22.5 133.5 %copy-start.32 = (s32[32]{0:T(128)S(1)}, s32[32]{0:T(128)}, u32[]{:S(2)}) copy-start(s32[32]{0:T(128)} %param.24) | copy-start | bytes 388
  22.5 134.4 %copy-start.6 = (bf16[32,4096]{1,0:T(8,128)(2,1)S(1)}, bf16[32,4096]{1,0:T(8,128)(2,1)}, u32[]{:S(2)}) copy-start(bf16[32,4096]{1,0:T(8,128)(2,1)} %param.29) | copy-start | bytes 786436
  169.9 154.5 %all-to-all-start.1 = ((bf16[32,32,1024]{2,1,0:T(8,128)(2,1)}), bf16[32,32,1024]{2,1,0:T(8,128)(2,1)S(1)}, u32[]{:S(2)}, u32[]{:S(2)}) async-start(bf16[32,32,1024]{2,1,0:T(8,128)(2,1)} %broadcast_select_fusion.3), calls=%async_computation.1 | async-start | bytes 4194304 | tf_op jit(solution)/shard_map/all_to_all | solution.py:1141
  394.8 53.1 %all-to-all-start.2 = ((bf16[32,32,1024]{2,1,0:T(8,128)(2,1)}), bf16[32,32,1024]{2,1,0:T(8,128)(2,1)S(1)}, u32[]{:S(2)}, u32[]{:S(2)}) async-start(bf16[32,32,1024]{2,1,0:T(8,128)(2,1)} %bitcast.50), calls=%async_computation.2 | async-start | bytes 4194304 | tf_op jit(solution)/shard_map/all_to_all | solution.py:1141
  447.9 104.4 %copy-start.2 = (bf16[32,32,1024]{2,1,0:T(8,128)(2,1)}, bf16[32,32,1024]{2,1,0:T(8,128)(2,1)S(1)}, u32[]{:S(2)}) copy-start(bf16[32,32,1024]{2,1,0:T(8,128)(2,1)S(1)} %all-to-all-done.2) | copy-start | bytes 6291460
  447.9 123.4 %all-to-all-start.3 = ((bf16[32,8,1024]{2,1,0:T(8,128)(2,1)}), bf16[32,8,1024]{2,1,0:T(8,128)(2,1)S(1)}, u32[]{:S(2)}, u32[]{:S(2)}) async-start(bf16[32,8,1024]{2,1,0:T(8,128)(2,1)} %bitcast.14), calls=%async_computation.3 | async-start | bytes 1048576 | tf_op jit(solution)/shard_map/all_to_all | solution.py:1141
  552.3 14.9 %copy-start.13 = (f32[1,1024]{1,0:T(1,128)S(1)}, f32[1,1024]{1,0:T(1,128)}, u32[]{:S(2)}) copy-start(f32[1,1024]{1,0:T(1,128)} %get-tuple-element.106) | copy-start | bytes 12292
  552.3 14.9 %copy-start.14 = (f32[1,1024]{1,0:T(1,128)S(1)}, f32[1,1024]{1,0:T(1,128)}, u32[]{:S(2)}) copy-start(f32[1,1024]{1,0:T(1,128)} %get-tuple-element.105) | copy-start | bytes 12292
  552.3 14.9 %copy-start.15 = (f32[1,1024]{1,0:T(1,128)S(1)}, f32[1,1024]{1,0:T(1,128)}, u32[]{:S(2)}) copy-start(f32[1,1024]{1,0:T(1,128)} %get-tuple-element.109) | copy-start | bytes 12292
  552.4 14.9 %copy-start.16 = (f32[1,1024]{1,0:T(1,128)S(1)}, f32[1,1024]{1,0:T(1,128)}, u32[]{:S(2)}) copy-start(f32[1,1024]{1,0:T(1,128)} %get-tuple-element.112) | copy-start | bytes 12292
  552.4 14.9 %copy-start.17 = (f32[1,1024]{1,0:T(1,128)S(1)}, f32[1,1024]{1,0:T(1,128)}, u32[]{:S(2)}) copy-start(f32[1,1024]{1,0:T(1,128)} %get-tuple-element.104) | copy-start | bytes 12292
  552.4 14.9 %copy-start.18 = (f32[1,1024]{1,0:T(1,128)S(1)}, f32[1,1024]{1,0:T(1,128)}, u32[]{:S(2)}) copy-start(f32[1,1024]{1,0:T(1,128)} %get-tuple-element.103) | copy-start | bytes 12292
  552.4 14.8 %copy-start.19 = (f32[1,1024]{1,0:T(1,128)S(1)}, f32[1,1024]{1,0:T(1,128)}, u32[]{:S(2)}) copy-start(f32[1,1024]{1,0:T(1,128)} %get-tuple-element.102) | copy-start | bytes 12292
  552.4 14.8 %copy-start.20 = (f32[1,1024]{1,0:T(1,128)S(1)}, f32[1,1024]{1,0:T(1,128)}, u32[]{:S(2)}) copy-start(f32[1,1024]{1,0:T(1,128)} %get-tuple-element.108) | copy-start | bytes 12292
  552.4 14.8 %copy-start.21 = (f32[1,1024]{1,0:T(1,128)S(1)}, f32[1,1024]{1,0:T(1,128)}, u32[]{:S(2)}) copy-start(f32[1,1024]{1,0:T(1,128)} %get-tuple-element.111) | copy-start | bytes 12292
  552.4 17.2 %copy-start.11 = (f32[1,4096]{1,0:T(1,128)S(1)}, f32[1,4096]{1,0:T(1,128)}, u32[]{:S(2)}) copy-start(f32[1,4096]{1,0:T(1,128)} %get-tuple-element.113) | copy-start | bytes 49156
  571.3 150.5 %all-to-all-start.4 = ((bf16[32,32,1024]{2,1,0:T(8,128)(2,1)}), bf16[32,32,1024]{2,1,0:T(8,128)(2,1)}, u32[]{:S(2)}, u32[]{:S(2)}) async-start(bf16[32,32,1024]{2,1,0:T(8,128)(2,1)} %bitcast.49), calls=%async_computation.4 | async-start | bytes 4194304 | tf_op jit(solution)/shard_map/all_to_all | solution.py:1141
  577.7 127.8 %copy-start.5 = (f32[8,32,1024]{2,1,0:T(8,128)S(1)}, f32[8,32,1024]{2,1,0:T(8,128)}, u32[]{:S(2)}) copy-start(f32[8,32,1024]{2,1,0:T(8,128)} %get-tuple-element.115) | copy-start | bytes 3145732
  (14 other events, 72.5 us)

commit v4 on v3

--- a/solution.py
+++ b/solution.py
@@ -44,6 +44,24 @@
         hail(self.z * 2 + 1 - self.c, self.f)
         pl.semaphore_wait(barrier, self.depth + 2)
 
+    def peers(self):
+        return 2 * self.depth * self.ring
+
+    def peer(self, k, sign):
+        dz, dc, df = k % self.depth, k // self.depth % 2, k // self.depth // 2
+        z = (self.z + sign * dz + self.depth) % self.depth
+        f = (self.f + sign * df + self.ring) % self.ring
+        return z * 2 + (self.c + dc) % 2, f
+
+    def greet_all(self):
+        barrier = pltpu.get_barrier_semaphore()
+
+        def hail(k):
+            pl.semaphore_signal(barrier, inc=1, device_id=self.peer(k + 1, 1), device_id_type=MESH)
+
+        loop(self.peers() - 1, hail)
+        pl.semaphore_wait(barrier, self.peers() - 1)
+
     def to_z(self, src, dst, send, recv, s):
         return self.remote(src, dst, send, recv, (self.z + s) % self.depth * 2 + self.c, self.f)
 
@@ -98,14 +116,19 @@
     def chunk(self, u, zs, c, g):
         return self.fulls.at[u, zs, c, g]
 
+    def shard(self, u):
+        if callable(self.shards):
+            return self.shards(u if isinstance(u, int) else 0)
+        return self.shards.at[u]
+
     def kept(self, u):
         p = self.place
-        return pltpu.make_async_copy(self.shards.at[u], self.chunk(u, p.z, p.c, p.f), self.local.at[u])
+        return pltpu.make_async_copy(self.shard(u), self.chunk(u, p.z, p.c, p.f), self.local.at[u])
 
     def z_copy(self, u, s, incoming):
         p = self.place
         origin = (p.z + p.depth - s) % p.depth if incoming else p.z
-        return p.to_z(self.shards.at[u], self.chunk(u, origin, p.c, p.f), self.z_send.at[u, s], self.z_recv.at[u, s], s)
+        return p.to_z(self.shard(u), self.chunk(u, origin, p.c, p.f), self.z_send.at[u, s], self.z_recv.at[u, s], s)
 
     def ring_copy(self, u, t, way, incoming):
         p = self.place
@@ -182,9 +205,60 @@
         loop(self.count, one)
 
 
+class Exchange:
+    def __init__(self, place, arrays, steps, sems):
+        self.place, self.arrays = place, arrays
+        self.send, self.recv, self.local = sems
+        self.each = -(-(place.peers() - 1) // steps)
+
+    @staticmethod
+    def sems(mesh, n):
+        peers = 2 * (mesh.shape["dp"] // 2) * mesh.shape["fsdp"]
+        return [DMA((n, peers)), DMA((n, peers)), DMA((n,))]
+
+    def block(self, d, f):
+        return d * self.place.ring + f
+
+    def own(self, a):
+        p = self.place
+        src, dst = self.arrays[a]
+        me = self.block(p.z * 2 + p.c, p.f)
+        return pltpu.make_async_copy(src.at[me], dst.at[me], self.local.at[a])
+
+    def copy(self, a, k, incoming):
+        p = self.place
+        src, dst = self.arrays[a]
+        d, f = p.peer(k, 1)
+        at, g = p.peer(k, -1) if incoming else (p.z * 2 + p.c, p.f)
+        return p.remote(src.at[self.block(d, f)], dst.at[self.block(at, g)], self.send.at[a, k], self.recv.at[a, k], d, f)
+
+    def begin(self):
+        for a in range(len(self.arrays)):
+            self.own(a).start()
+
+    def start(self, k):
+        for a in range(len(self.arrays)):
+            self.copy(a, k, False).start()
+
+    def step(self, i):
+        for j in range(self.each):
+            k = 1 + i * self.each + j
+            when(k < self.place.peers(), functools.partial(self.start, k))
+
+    def finish(self):
+        def one(k):
+            for a in range(len(self.arrays)):
+                self.copy(a, k + 1, False).wait_send()
+                self.copy(a, k + 1, True).wait_recv()
+
+        loop(self.place.peers() - 1, one)
+        for a in range(len(self.arrays)):
+            self.own(a).wait()
+
+
 class Scatter:
-    def __init__(self, place, count, rows, held, outs, refs, sems):
-        self.place, self.count, self.rows, self.held, self.outs = place, count, rows, held, outs
+    def __init__(self, place, count, rows, held, put, refs, sems):
+        self.place, self.count, self.rows, self.held, self.put = place, count, rows, held, put
         self.mine, self.theirs, self.rhalf, self.rfull, self.zbuf = refs
         self.c_send, self.c_recv, self.r_send, self.r_recv, self.z_send, self.z_recv = sems
         self.slots = held.shape[0]
@@ -280,7 +354,7 @@
         total = self.mine[u, p.z, p.f].astype(full)
         for s in range(1, p.depth):
             total = total + self.zbuf[u, s - 1].astype(full)
-        self.outs[u] = total
+        self.put(u, total)
 
     def finish(self):
         p = self.place
@@ -317,38 +391,96 @@
     return pltpu.CompilerParams(collective_id=ident, has_side_effects=True, vmem_limit_bytes=60 * 2**20)
 
 
-def first_gather_kernel(depth, ring, count, shard, little, full, little_full, *sems):
+def first_gather_kernel(depth, ring, where, n_w, n_x, *refs):
+    weights, little, sent = refs[:n_w], refs[n_w], refs[n_w + 1 : n_w + 1 + n_x]
+    full, little_full, arrived = refs[n_w + 1 + n_x], refs[n_w + 2 + n_x], refs[n_w + 3 + n_x : n_w + 3 + 2 * n_x]
+    sems = refs[n_w + 3 + 2 * n_x :]
     place = Place(depth, ring)
-    place.greet()
+    place.greet_all()
+    count = len(where)
+
+    def shard(u):
+        which, lead = where[u]
+        return weights[which] if lead is None else weights[which].at[lead]
+
     small = Gather(place, 1, little, little_full, sems[:7])
-    big = Gather(place, count, shard, full, sems[7:])
+    big = Gather(place, count, shard, full, sems[7:14], ahead=count)
+    swap = Exchange(place, tuple(zip(sent, arrived, strict=True)), max(1, big.steps() - 3), sems[14:])
     small.begin()
     big.begin()
+    swap.begin()
     for i in range(big.steps()):
+        swap.step(i)
         if i < small.steps():
             small.step(i)
         big.step(i)
     small.finish()
     big.finish()
-
-
-def first_gather(mesh, shards, little, ident):
+    swap.finish()
+
+
+def first_gather(mesh, weights, little, sent, ident):
     depth, ring = mesh.shape["dp"] // 2, mesh.shape["fsdp"]
-    count = shards.shape[0]
-
-    def full(a):
-        return jax.ShapeDtypeStruct((a.shape[0], depth, 2, ring) + a.shape[1:], a.dtype)
-
+    where = []
+    for which, a in enumerate(weights):
+        where += [(which, None)] if a.ndim == 2 else [(which, lead) for lead in range(a.shape[0])]
+    count = len(where)
+
+    def full(n, a):
+        return jax.ShapeDtypeStruct((n, depth, 2, ring) + a.shape[-2:], a.dtype)
+
+    same = [jax.ShapeDtypeStruct(a.shape, a.dtype) for a in sent]
     return pl.pallas_call(
-        functools.partial(first_gather_kernel, depth, ring, count),
-        out_shape=[full(shards), full(little)],
-        in_specs=[ANY] * 2,
-        out_specs=[ANY] * 2,
-        scratch_shapes=Gather.sems(mesh, 1) + Gather.sems(mesh, count),
+        functools.partial(first_gather_kernel, depth, ring, tuple(where), len(weights), len(sent)),
+        out_shape=[full(count, weights[0]), full(1, little)] + same,
+        in_specs=[pl.BlockSpec(memory_space=pltpu.VMEM)] * (len(weights) + 1) + [ANY] * len(sent),
+        out_specs=[ANY] * (2 + len(sent)),
+        scratch_shapes=Gather.sems(mesh, 1) + Gather.sems(mesh, count) + Exchange.sems(mesh, len(sent)),
         compiler_params=remote_params(ident),
         cost_estimate=pl.CostEstimate(flops=60_000_000_000, bytes_accessed=2 * 33_554_432, transcendentals=0),
         name="first_gather",
-    )(shards, little)
+    )(*weights, little, *sent)
+
+
+def deal_kernel(out_of, n, deal_ref, *refs):
+    sources, dests, held, sem = refs[:n], refs[n : 2 * n], refs[2 * n : 3 * n], refs[3 * n]
+    slots = deal_ref.shape[0]
+
+    def load(a, i):
+        return pltpu.make_async_copy(sources[a].at[i if out_of else deal_ref[i]], held[a].at[i], sem.at[0, a, i])
+
+    def store(a, i):
+        return pltpu.make_async_copy(held[a].at[i], dests[a].at[deal_ref[i] if out_of else i], sem.at[1, a, i])
+
+    def begin(i):
+        for a in range(n):
+            load(a, i).start()
+
+    def turn(i):
+        for a in range(n):
+            load(a, i).wait()
+            store(a, i).start()
+
+    def end(i):
+        for a in range(n):
+            store(a, i).wait()
+
+    loop(slots, begin)
+    loop(slots, turn)
+    loop(slots, end)
+
+
+def deal_blocks(deal, arrays, out_of, name):
+    n = len(arrays)
+    return pl.pallas_call(
+        functools.partial(deal_kernel, out_of, n),
+        out_shape=[jax.ShapeDtypeStruct(a.shape, a.dtype) for a in arrays],
+        in_specs=[pl.BlockSpec(memory_space=pltpu.SMEM)] + [ANY] * n,
+        out_specs=[ANY] * n,
+        scratch_shapes=[pltpu.VMEM(a.shape, a.dtype) for a in arrays] + [DMA((2, n, deal.shape[0]))],
+        compiler_params=pltpu.CompilerParams(vmem_limit_bytes=60 * 2**20),
+        name=name,
+    )(deal, *arrays)
 
 
 NN = (((1,), (0,)), ((), ()))
@@ -393,16 +525,6 @@
     tilt = jnp.mean(scaled * hat, axis=-1, keepdims=True)
     back = rstd * (scaled - lean - hat * tilt)
     return back, jnp.sum(grad * hat, axis=0, keepdims=True), jnp.sum(grad, axis=0, keepdims=True)
-
-
-def add_row(ref, value, first):
-    @pl.when(first)
-    def _():
-        ref[...] = value
-
-    @pl.when(jnp.logical_not(first))
-    def _():
-        ref[...] += value
 
 
 GAIN, SHIFT, DOWN = 6, 9, 12
@@ -463,16 +585,37 @@
         l_ref[at] = kept
 
 
+def parts_of(value, heads, spare):
+    lane = lanes(value.shape)
+    shown = jnp.where(lane < heads, value, 0.0)
+    shown = shown + pltpu.roll(shown, heads, 1) + pltpu.roll(shown, 2 * heads, 1)
+    one, two, three = thirds(-shown)
+    part = jnp.where(lane < heads, one, jnp.where(lane < 2 * heads, two, three))
+    return jnp.where(lane == 3 * heads, spare, part).astype(LOW)
+
+
+def take_part(head, heads):
+    lane = lanes((1, PAIR))
+    return jnp.where((lane < 3 * heads) & (lane % heads == head), 1.0, 0.0)
+
+
 def forward_kernel(
-    depth, ring, count, n_ref, m_ref, x_hbm, e_hbm, w_hbm, p_ref, shard,
-    full, a0_hbm, qkv_hbm, o0_hbm, l0_hbm, x1_hbm, a1_hbm, q1_hbm, kv_hbm, o1_hbm, l1_hbm,
-    x_ref, e_ref, w_ref, a_ref, qkv_ref, o_ref, l0_ref, x1_ref, q1_ref, kv_ref, l1_ref, a1_ref,
+    depth, ring, count, n_ref, m_ref, x_hbm, e_hbm, w_hbm, p_ref, shard, sent,
+    full, arrived, a0_hbm, qkv_hbm, o0_hbm, l0_hbm, x1_hbm, a1_hbm, q1_hbm, kv_hbm, o1_hbm, l1_hbm,
+    x_ref, e_ref, w_ref, a_ref, qkv_ref, o_ref, l0_ref, x1_ref, q1_ref, kv_ref, l1_ref, a1_ref, lp_ref,
     w_sem, in_sem, out_sem, *sems,
 ):
     place = Place(depth, ring)
-    place.greet()
-    gather = Gather(place, count, shard, full, sems)
+    place.greet_all()
+    gather = Gather(place, count, shard, full, sems[:7], ahead=count)
+    swap = Exchange(place, ((sent, arrived),), gather.steps() - 2, sems[7:])
     gather.begin()
+    swap.begin()
+
+    def advance(i):
+        swap.step(i)
+        gather.step(i)
+
     rows, width = x_ref.shape
     tile = 256
     load_x = pltpu.make_async_copy(x_hbm, x_ref, in_sem.at[0])
@@ -495,7 +638,7 @@
     l0_ref[...] = jnp.zeros_like(l0_ref)
     l1_ref[...] = jnp.zeros_like(l1_ref)
     load_x.wait()
-    gather.step(0)
+    advance(0)
     for i in range(rows // tile):
         at = slice(i * tile, (i + 1) * tile)
         hat, _ = normal(x_ref[at].astype(FULL))
@@ -515,7 +658,7 @@
         loop(rows // (2 * tile), project)
         send(qkv_ref.at[j], qkv_hbm.at[j])
         if j == 1:
-            gather.step(1)
+            advance(1)
 
     pairs = width // PAIR
 
@@ -526,11 +669,13 @@
             o_ref[at, cols] = value
 
         attend_pair(True, tile, h, n_ref[0], qkv_ref[0, :, cols], qkv_ref[1, :, cols], qkv_ref[2, :, cols], store, l0_ref)
-        when(h % 2 == 0, lambda: gather.step(2 + h // 2))
+        when(h % 2 == 0, lambda: advance(2 + h // 2))
 
     loop(pairs, self_pair)
     send(o_ref, o0_hbm)
-    send(l0_ref, l0_hbm)
+    heads = 2 * pairs
+    lp_ref[0] = parts_of(l0_ref[...], heads, 1.0)
+    send(lp_ref.at[0], l0_hbm)
     done = 2 + (pairs + 1) // 2
     loads[3].wait()
     loads[4].wait()
@@ -543,7 +688,7 @@
         a = (hat * p_ref[GAIN + 1 : GAIN + 2] + p_ref[SHIFT + 1 : SHIFT + 2]).astype(LOW)
         a1_ref[at] = a
         q1_ref[at] = ((dot(a, w_ref[4], NN) + p_ref[3:4]) * SCALE).astype(LOW)
-        when(i % 2 == 1, lambda: gather.step(done + i // 2))
+        when(i % 2 == 1, lambda: advance(done + i // 2))
 
     loop(rows // tile, middle_part)
     done = done + rows // tile // 2
@@ -565,29 +710,32 @@
             o_ref[at, cols] = value
 
         attend_pair(False, tile, h, m_ref[0], q1_ref[:, cols], kv_ref[0, :, cols], kv_ref[1, :, cols], store, l1_ref)
-        when(h % 2 == 0, lambda: gather.step(done + h // 2))
+        when(h % 2 == 0, lambda: advance(done + h // 2))
 
     loop(pairs, cross_pair)
     done = done + (pairs + 1) // 2
     send(o_ref, o1_hbm)
-    send(l1_ref, l1_hbm)
+    lp_ref[1] = parts_of(l1_ref[...], heads, 1.0)
+    send(lp_ref.at[1], l1_hbm)
     for i in range(done, gather.steps()):
-        gather.step(i)
+        advance(i)
     gather.finish()
+    swap.finish()
     for k, copy in enumerate(leaving):
         if k != 4:
             copy.wait()
 
 
-def forward(mesh, length, enc_count, x, memory, w, p, shards, ident):
+def forward(mesh, length, enc_count, x, memory, w, p, shards, sent, ident):
     depth, ring = mesh.shape["dp"] // 2, mesh.shape["fsdp"]
     count = shards.shape[0]
     rows, width = x.shape
     enc = memory.shape[0]
     low = jax.ShapeDtypeStruct((rows, width), LOW)
-    level = jax.ShapeDtypeStruct((rows, PAIR), FULL)
+    level = jax.ShapeDtypeStruct((rows, PAIR), LOW)
     out_shape = [
         jax.ShapeDtypeStruct((count, depth, 2, ring) + shards.shape[1:], LOW),
+        jax.ShapeDtypeStruct(sent.shape, sent.dtype),
         low,
         jax.ShapeDtypeStruct((3, rows, width), LOW),
         low,
@@ -603,7 +751,7 @@
     return pl.pallas_call(
         functools.partial(forward_kernel, depth, ring, count),
         out_shape=out_shape,
-        in_specs=[SMEM, SMEM, ANY, ANY, ANY, VMEM, ANY],
+        in_specs=[SMEM, SMEM, ANY, ANY, ANY, VMEM, VMEM, ANY],
         out_specs=[ANY] * len(out_shape),
         scratch_shapes=[
             big,
@@ -618,45 +766,40 @@
             pltpu.VMEM((2, enc, width), LOW),
             pltpu.VMEM((rows, PAIR), FULL),
             big,
+            pltpu.VMEM((2, rows, PAIR), LOW),
             DMA((w.shape[0],)),
             DMA((2,)),
             DMA((12,)),
         ]
-        + Gather.sems(mesh, count),
+        + Gather.sems(mesh, count)
+        + Exchange.sems(mesh, 1),
         compiler_params=remote_params(ident),
         cost_estimate=pl.CostEstimate(flops=70_000_000_000, bytes_accessed=2 * 33_554_432, transcendentals=0),
         name="forward_gather",
-    )(length, enc_count, x, memory, w, p, shards)
-
-
-def back_pair(causal, tile, h, n, q, k, v, mixed, grad, level, acc_ref, store):
+    )(length, enc_count, x, memory, w, p, shards, sent)
+
+
+def back_pair(causal, tile, h, heads, n, q, k, v, grad, level, inner, acc_ref, store):
     queries, count = q.shape[0], k.shape[0]
-    lane_k, lane_q = lanes((count, PAIR)), lanes((queries, PAIR))
+    acc_ref[...] = jnp.zeros_like(acc_ref)
+    wide_q = jnp.concatenate([q, level], axis=1)
+    wide_g = jnp.concatenate([grad, inner], axis=1)
     shut = jnp.where(rows_of((count, PAIR)) >= n, NEGATIVE, 0.0)
-    open_k = jnp.where(lane_k == 0, shut, jnp.where(lane_k < 4, 1.0, 0.0)).astype(LOW)
-    open_v = jnp.where(lane_k < 3, 1.0, 0.0).astype(LOW)
-    product = grad.astype(FULL) * mixed.astype(FULL)
-    acc_ref[...] = jnp.zeros_like(acc_ref)
-    heads = []
+    both_heads = []
     for head in range(2):
         mask = head_mask(head)
-        lse = jnp.sum(jnp.where(lane_q == 2 * h + head, level, 0.0), axis=1, keepdims=True)
-        one, two, three = thirds(-lse)
-        tail = jnp.where(lane_q == 0, 1.0, jnp.where(lane_q == 1, one, jnp.where(lane_q == 2, two, jnp.where(lane_q == 3, three, 0.0))))
-        wide_q = jnp.concatenate([q, tail.astype(LOW)], axis=1)
-        inner = jnp.sum(jnp.where(lane_q // HD == head, product, 0.0), axis=1, keepdims=True)
-        one, two, three = thirds(-inner)
-        tail = jnp.where(lane_q == 0, one, jnp.where(lane_q == 1, two, jnp.where(lane_q == 2, three, 0.0)))
-        wide_g = jnp.concatenate([grad, tail.astype(LOW)], axis=1)
+        mine = take_part(2 * h + head, heads)
+        open_k = jnp.where(lanes((count, PAIR)) == 3 * heads, shut, mine).astype(LOW)
+        open_v = jnp.broadcast_to(mine, (count, PAIR)).astype(LOW)
         wide_k = jnp.concatenate([k * mask, open_k], axis=1)
         wide_v = jnp.concatenate([v * mask, open_v], axis=1)
-        heads.append((wide_q, wide_g, wide_k, wide_v, q * mask, grad * mask, k * mask))
+        both_heads.append((wide_k, wide_v, q * mask, grad * mask, k * mask))
     for i in range(count // tile):
         at = slice(i * tile, (i + 1) * tile)
         low = i * tile if causal else 0
         grad_k = jnp.zeros((tile, PAIR), FULL)
         grad_v = jnp.zeros((tile, PAIR), FULL)
-        for wide_q, wide_g, wide_k, wide_v, q_one, g_one, k_one in heads:
+        for wide_k, wide_v, q_one, g_one, k_one in both_heads:
             scores = dot(wide_k[at], wide_q[low:], NT)
             if causal:
                 square = (tile, tile)
@@ -668,6 +811,15 @@
             grad_k = grad_k + dot(slope, q_one[low:], NN)
             acc_ref[low:] += dot(slope, k_one[at], TN)
         store(at, grad_k.astype(LOW), grad_v.astype(LOW))
+
+
+def inner_parts(grad, mixed, heads):
+    width = grad.shape[1]
+    product = grad.astype(FULL) * mixed.astype(FULL)
+    head = (rows_of((width, PAIR)) // HD == lanes((width, PAIR))).astype(FULL).astype(LOW)
+    high = product.astype(LOW)
+    rest = product - high.astype(FULL)
+    return parts_of(dot(high, head, NN) + dot(rest.astype(LOW), head, NN), heads, 0.0)
 
 
 def unit_grad(place, held, slot, a_ref, b_ref, scale):
@@ -685,16 +837,22 @@
 
 
 def feed_scatter_kernel(
-    depth, ring, n_ref, a2_hbm, g3_hbm, du_hbm, r_hbm, qkv_hbm, mixed_hbm, grad_hbm, l_ref,
-    outs, dq_hbm, dkv_hbm,
+    depth, ring, n_ref, a2_hbm, g3_hbm, du_hbm, r_hbm, qkv_hbm, grad_hbm, l_ref, i_ref, sent,
+    outs, dq_hbm, dkv_hbm, arrived,
     a2_ref, g3_ref, moving, held, q_buf, acc_ref, dq_buf, dkv_buf, in_sem, move_sem, q_sem, out_sem, *rest,
 ):
     place = Place(depth, ring)
-    place.greet()
+    place.greet_all()
     blocks = du_hbm.shape[0]
     count = 2 * blocks
-    sums = Scatter(place, count, outs.shape[1], held, outs, rest[:5], rest[5:])
-    pairs = mixed_hbm.shape[1] // PAIR
+
+    def put_sum(u, total):
+        outs[u] = total
+
+    sums = Scatter(place, count, outs.shape[1], held, put_sum, rest[:5], rest[5:11])
+    swap = Exchange(place, ((sent, arrived),), count, rest[11:])
+    pairs = grad_hbm.shape[1] // PAIR
+    swap.begin()
     slots = held.shape[0]
     load_a = pltpu.make_async_copy(a2_hbm, a2_ref, in_sem.at[0])
     load_g = pltpu.make_async_copy(g3_hbm, g3_ref, in_sem.at[1])
@@ -708,7 +866,7 @@
 
     def fetch(h):
         cols = pl.ds(pl.multiple_of(h * PAIR, PAIR), PAIR)
-        sources = [qkv_hbm.at[0, :, cols], qkv_hbm.at[1, :, cols], qkv_hbm.at[2, :, cols], mixed_hbm.at[:, cols], grad_hbm.at[:, cols]]
+        sources = [qkv_hbm.at[0, :, cols], qkv_hbm.at[1, :, cols], qkv_hbm.at[2, :, cols], grad_hbm.at[:, cols]]
         return [pltpu.make_async_copy(s, q_buf.at[h % 2, k], q_sem.at[h % 2, k]) for k, s in enumerate(sources)]
 
     def put(h):
@@ -755,7 +913,7 @@
             dkv_buf[b, 0, at] = grad_k
             dkv_buf[b, 1, at] = grad_v
 
-        back_pair(True, 256, h, n_ref[0], q_buf[b, 0], q_buf[b, 1], q_buf[b, 2], q_buf[b, 3], q_buf[b, 4], l_ref[...], acc_ref, store)
+        back_pair(True, 256, h, 2 * pairs, n_ref[0], q_buf[b, 0], q_buf[b, 1], q_buf[b, 2], q_buf[b, 3], l_ref[...], i_ref[...], acc_ref, store)
         dq_buf[b] = acc_ref[...].astype(LOW)
         for copy in put(h):
             copy.start()
@@ -765,15 +923,17 @@
         sums.early(i)
         when(i < pairs, lambda: heads(i))
         sums.late(i)
+        swap.step(i)
 
     loop(max(sums.steps(), pairs), step)
     for h in range(max(0, pairs - 2), pairs):
         for copy in put(h):
             copy.wait()
     sums.finish()
-
-
-def feed_scatter(mesh, length, a2, g3, du, r, qkv, mixed, grad, level, ident):
+    swap.finish()
+
+
+def feed_scatter(mesh, length, a2, g3, du, r, qkv, grad, level, inner, sent, ident):
     depth, ring = mesh.shape["dp"] // 2, mesh.shape["fsdp"]
     blocks, rows, width = du.shape
     own = width // (2 * depth * ring)
@@ -785,43 +945,55 @@
             jax.ShapeDtypeStruct((count, own, width), FULL),
             jax.ShapeDtypeStruct((rows, width), LOW),
             jax.ShapeDtypeStruct((2, rows, width), LOW),
+            jax.ShapeDtypeStruct(sent.shape, sent.dtype),
         ],
-        in_specs=[SMEM] + [ANY] * 7 + [VMEM],
-        out_specs=[VMEM, ANY, ANY],
+        in_specs=[SMEM] + [ANY] * 6 + [VMEM, VMEM, ANY],
+        out_specs=[VMEM, ANY, ANY, ANY],
         scratch_shapes=[
             big,
             big,
             pltpu.VMEM((2, rows, width), LOW),
             pltpu.VMEM((3, depth, 2, ring * own, width), LOW),
-            pltpu.VMEM((2, 5, rows, PAIR), LOW),
+            pltpu.VMEM((2, 4, rows, PAIR), LOW),
             pltpu.VMEM((rows, PAIR), FULL),
             pltpu.VMEM((2, rows, PAIR), LOW),
             pltpu.VMEM((2, 2, rows, PAIR), LOW),
             DMA((2,)),
             DMA((2,)),
-            DMA((2, 5)),
+            DMA((2, 4)),
             DMA((2, 2)),
         ]
         + Scatter.refs(mesh, count, own, width, LOW)
-        + Scatter.sems(mesh, count),
+        + Scatter.sems(mesh, count)
+        + Exchange.sems(mesh, 1),
         compiler_params=remote_params(ident),
         cost_estimate=pl.CostEstimate(flops=60_000_000_000, bytes_accessed=2 * 33_554_432, transcendentals=0),
         name="feed_scatter",
-    )(length, a2, g3, du, r, qkv, mixed, grad, level)
+    )(length, a2, g3, du, r, qkv, grad, level, inner, sent)
 
 
 def last_scatter_kernel(
-    depth, ring, made_hbm, o1_hbm, g2_hbm, a1_hbm, dq1_hbm, o0_hbm, g1_hbm, a0_hbm, dq0_hbm, dkv_hbm, tiny_ref,
-    outs, tiny_out, left, right, held, tiny_held, left_sem, right_sem, made_sem, *rest,
+    depth, ring, made_hbm, o1_hbm, g2_hbm, a1_hbm, dq1_hbm, o0_hbm, g1_hbm, a0_hbm, dq0_hbm, dkv_hbm, tiny_ref, sent,
+    s_qkv, s_out, c_qkv, c_out, tiny_out, arrived, left, right, held, tiny_held, left_sem, right_sem, made_sem, *rest,
 ):
     place = Place(depth, ring)
-    place.greet()
+    place.greet_all()
     made = made_hbm.shape[0]
+    spots = [c_qkv.at[1], c_qkv.at[2], c_qkv.at[0], c_out, s_out, s_qkv.at[0], s_qkv.at[1], s_qkv.at[2]]
+
+    def put_sum(u, total):
+        spots[u][...] = total
+
+    def put_tiny(u, total):
+        tiny_out[u] = total
+
     pairs = [(a1_hbm, dq1_hbm), (o1_hbm, g2_hbm), (o0_hbm, g1_hbm), (a0_hbm, dq0_hbm), (a0_hbm, dkv_hbm.at[0]), (a0_hbm, dkv_hbm.at[1])]
     scaled = (0, 3)
     count = made + len(pairs)
-    small = Scatter(place, 1, tiny_out.shape[1], tiny_held, tiny_out, rest[:5], rest[5:11])
-    sums = Scatter(place, count, outs.shape[1], held, outs, rest[11:16], rest[16:])
+    small = Scatter(place, 1, tiny_out.shape[1], tiny_held, put_tiny, rest[:5], rest[5:11])
+    sums = Scatter(place, count, s_out.shape[0], held, put_sum, rest[11:16], rest[16:22])
+    swap = Exchange(place, ((sent, arrived),), count, rest[22:])
+    swap.begin()
     slots = held.shape[0]
 
     def load(k):
@@ -860,11 +1032,13 @@
         if i < small.steps():
             small.late(i)
         sums.late(i)
+        swap.step(i)
     small.finish()
     sums.finish()
-
-
-def last_scatter(mesh, made, pairs, tiny, ident):
+    swap.finish()
+
+
+def last_scatter(mesh, made, pairs, tiny, sent, ident):
     depth, ring = mesh.shape["dp"] // 2, mesh.shape["fsdp"]
     n, width = made.shape[0], made.shape[-1]
     rows = pairs[0].shape[0]
@@ -874,11 +1048,15 @@
     return pl.pallas_call(
         functools.partial(last_scatter_kernel, depth, ring),
         out_shape=[
-            jax.ShapeDtypeStruct((count, own, width), FULL),
+            jax.ShapeDtypeStruct((3, own, width), FULL),
+            jax.ShapeDtypeStruct((own, width), FULL),
+            jax.ShapeDtypeStruct((3, own, width), FULL),
+            jax.ShapeDtypeStruct((own, width), FULL),
             jax.ShapeDtypeStruct((1, tiny_rows, tiny.shape[3]), FULL),
+            jax.ShapeDtypeStruct(sent.shape, sent.dtype),
         ],
-        in_specs=[ANY] * (1 + len(pairs)) + [VMEM],
-        out_specs=[VMEM, VMEM],
+        in_specs=[ANY] * (1 + len(pairs)) + [VMEM, ANY],
+        out_specs=[VMEM] * 5 + [ANY],
         scratch_shapes=[
             pltpu.VMEM((2, rows, width), LOW),
             pltpu.VMEM((2, rows, width), LOW),
@@ -891,11 +1069,12 @@
         + Scatter.refs(mesh, 1, tiny_rows, tiny.shape[3], FULL)
         + Scatter.sems(mesh, 1)
         + Scatter.refs(mesh, count, own, width, LOW)
-        + Scatter.sems(mesh, count),
+        + Scatter.sems(mesh, count)
+        + Exchange.sems(mesh, 1),
         compiler_params=remote_params(ident),
         cost_estimate=pl.CostEstimate(flops=60_000_000_000, bytes_accessed=2 * 33_554_432, transcendentals=0),
         name="last_scatter",
-    )(made, *pairs, tiny)
+    )(made, *pairs, tiny, sent)
 
 
 CUBIC = 0.044715
@@ -904,7 +1083,7 @@
 
 def feed_kernel(
     n_ref, x1_ref, o_ref, g_ref, w_hbm, p_ref, bu_ref,
-    out_ref, r_ref, du_ref, a_ref, g3_ref, dx_ref, g2_ref, do_ref,
+    out_ref, r_ref, du_ref, a_ref, g3_ref, dx_ref, g2_ref, do_ref, inner_ref,
     sum_up, sum_down, sum_five, sum_gain, sum_shift,
     w_ref, slope_ref, sems,
 ):
@@ -915,13 +1094,12 @@
     order = [0] + [k * blocks + j + 1 for j in range(blocks) for k in range(2)]
     loads = {u: pltpu.make_async_copy(w_hbm.at[u], w_ref.at[u], sems.at[u]) for u in order}
 
-    def ready(u):
-        pl.when(first)(loads[u].wait)
-
     @pl.when(first)
     def _():
         for u in order:
             loads[u].start()
+        for ref in (sum_up, sum_down, sum_five, sum_gain, sum_shift):
+            ref[...] = jnp.zeros_like(ref)
         loads[0].wait()
 
     valid = jnp.where(i * tile + rows_of((tile, 1)) < n_ref[0], 1.0, 0.0)
@@ -930,10 +1108,14 @@
     gain = p_ref[GAIN + 2 : GAIN + 3]
     a_ref[...] = (hat * gain + p_ref[SHIFT + 2 : SHIFT + 3]).astype(LOW)
 
+    @pl.when(first)
+    def _():
+        for u in order[1:]:
+            loads[u].wait()
+
     total = x2 + p_ref[DOWN : DOWN + 1]
     for j in range(blocks):
         cols = slice(j * width, (j + 1) * width)
-        ready(1 + j)
         u = dot(a_ref[...], w_ref[1 + j], NN) + bu_ref[:, cols]
         square = u * u
         t = jnp.tanh(ROOT * (u * (1.0 + CUBIC * square)))
@@ -942,7 +1124,6 @@
         r_ref[j] = r
         slope = half + 0.5 * u * (1.0 - t * t) * (ROOT * (1.0 + 3.0 * CUBIC * square))
         slope_ref[:, cols] = slope.astype(LOW)
-        ready(1 + blocks + j)
         total = total + dot(r, w_ref[1 + blocks + j], NN)
     out_ref[...] = (total * valid).astype(LOW)
     grad_out = g_ref[...].astype(FULL) * valid
@@ -955,25 +1136,20 @@
         du_ref[j] = du
         line = jnp.sum(du.astype(FULL), axis=0, keepdims=True)
 
-        @pl.when(first)
-        def _():
-            sum_up[:, cols] = line
-
-        @pl.when(jnp.logical_not(first))
-        def _():
-            sum_up[:, cols] += line
-
+        sum_up[:, cols] += line
         grad = grad + dot(du, w_ref[1 + j], NT)
     back, lines, shifts = normal_back(hat, rstd, grad, gain)
     dx2 = grad_out + back
     dx_ref[...] = dx2
     g2 = dx2.astype(LOW)
     g2_ref[...] = g2
-    do_ref[...] = dot(g2, w_ref[0], NT).astype(LOW)
-    add_row(sum_down, jnp.sum(g3.astype(FULL), axis=0, keepdims=True), first)
-    add_row(sum_five, jnp.sum(g2.astype(FULL), axis=0, keepdims=True), first)
-    add_row(sum_gain, lines, first)
-    add_row(sum_shift, shifts, first)
+    grad_mixed = dot(g2, w_ref[0], NT).astype(LOW)
+    do_ref[...] = grad_mixed
+    inner_ref[...] = inner_parts(grad_mixed, o_ref[...], width // HD)
+    sum_down[...] += jnp.sum(g3.astype(FULL), axis=0, keepdims=True)
+    sum_five[...] += jnp.sum(g2.astype(FULL), axis=0, keepdims=True)
+    sum_gain[...] += lines
+    sum_shift[...] += shifts
 
 
 def feed(length, x1, mixed, cotangent, w, p, bias_up, tile=256):
@@ -982,6 +1158,7 @@
     inner = blocks * width
     part = pl.BlockSpec((tile, width), lambda i: (i, 0))
     broad = pl.BlockSpec((blocks, tile, width), lambda i: (0, i, 0))
+    thin = pl.BlockSpec((tile, PAIR), lambda i: (i, 0))
     low = jax.ShapeDtypeStruct((rows, width), LOW)
     wide = jax.ShapeDtypeStruct((blocks, rows, width), LOW)
     line = jax.ShapeDtypeStruct((1, width), FULL)
@@ -992,9 +1169,9 @@
         2 * rows * (9 * width + 2 * inner) + 4 * inner * width,
         grid=(rows // tile,),
         in_specs=[SMEM, part, part, part, ANY, whole(p.shape), whole(bias_up.shape)],
-        out_specs=[part, broad, broad, part, part, part, part, part, whole((1, inner))] + [whole((1, width))] * 4,
+        out_specs=[part, broad, broad, part, part, part, part, part, thin, whole((1, inner))] + [whole((1, width))] * 4,
         out_shape=[low, wide, wide, low, low, jax.ShapeDtypeStruct((rows, width), FULL), low, low,
-                   jax.ShapeDtypeStruct((1, inner), FULL), line, line, line, line],
+                   jax.ShapeDtypeStruct((rows, PAIR), LOW), jax.ShapeDtypeStruct((1, inner), FULL), line, line, line, line],
         scratch_shapes=[pltpu.VMEM(w.shape, LOW), pltpu.VMEM((tile, inner), LOW), DMA((w.shape[0],))],
     )(length, x1, mixed, cotangent, w, p, bias_up)
 
@@ -1003,18 +1180,18 @@
     return pl.BlockSpec((1,) + w.shape[1:], lambda *_: (u, 0, 0))
 
 
-def cross_attend_back_kernel(n_ref, q_ref, k_ref, v_ref, o_ref, g_ref, l_ref, dq_ref, dkv_ref, acc_ref):
+def cross_attend_back_kernel(heads, n_ref, q_ref, k_ref, v_ref, g_ref, l_ref, i_ref, dq_ref, dkv_ref, acc_ref):
     def store(at, grad_k, grad_v):
         dkv_ref[0, at] = grad_k
         dkv_ref[1, at] = grad_v
 
     h = pl.program_id(0)
-    back_pair(False, k_ref.shape[1], h, n_ref[0], q_ref[0], k_ref[0], v_ref[0], o_ref[...], g_ref[...], l_ref[...], acc_ref, store)
+    back_pair(False, k_ref.shape[1], h, heads, n_ref[0], q_ref[0], k_ref[0], v_ref[0], g_ref[...], l_ref[...], i_ref[...], acc_ref, store)
     dq_ref[...] = acc_ref[...].astype(LOW)
 
 
-def cross_attend_back(count, q, kv, mixed, grad, level):
-    rows, width = mixed.shape
+def cross_attend_back(count, q, kv, grad, level, inner):
+    rows, width = grad.shape
     enc = kv.shape[1]
 
     def cut(part, n):
@@ -1022,16 +1199,16 @@
 
     column = pl.BlockSpec((rows, PAIR), lambda h: (0, h))
     return calls(
-        cross_attend_back_kernel,
+        functools.partial(cross_attend_back_kernel, width // HD),
         "cross_attend_back",
         4 * 10 * rows * enc * width,
         2 * (4 * rows + 4 * enc) * width,
         grid=(width // PAIR,),
-        in_specs=[SMEM, cut(0, rows), cut(0, enc), cut(1, enc), column, column, whole((rows, PAIR))],
+        in_specs=[SMEM, cut(0, rows), cut(0, enc), cut(1, enc), column, whole((rows, PAIR)), whole((rows, PAIR))],
         out_specs=[column, pl.BlockSpec((2, enc, PAIR), lambda h: (0, 0, h))],
         out_shape=[jax.ShapeDtypeStruct((rows, width), LOW), jax.ShapeDtypeStruct((2, enc, width), LOW)],
         scratch_shapes=[pltpu.VMEM((rows, PAIR), FULL)],
-    )(count, q, kv, kv, mixed, grad, level)
+    )(count, q, kv, kv, grad, level, inner)
 
 
 def memory_grad_kernel(e_ref, b_ref, w_ref, o_ref, de_ref, sum_v, acc_ref):
@@ -1071,9 +1248,13 @@
     )(memory, dkv, w)
 
 
-def cross_back_kernel(x1_ref, dq_ref, dx2_ref, wq_ref, wo_ref, p_ref, dx_ref, g1_ref, do_ref,
+def cross_back_kernel(x1_ref, dq_ref, dx2_ref, o_ref, wq_ref, wo_ref, p_ref, dx_ref, g1_ref, do_ref, inner_ref,
                       sum_q, sum_out, sum_gain, sum_shift):
-    first = pl.program_id(0) == 0
+    @pl.when(pl.program_id(0) == 0)
+    def _():
+        for ref in (sum_q, sum_out, sum_gain, sum_shift):
+            ref[...] = jnp.zeros_like(ref)
+
     grad = dot(dq_ref[...], wq_ref[0], NT) * SCALE
     hat, rstd = normal(x1_ref[...])
     back, lines, shifts = normal_back(hat, rstd, grad, p_ref[GAIN + 1 : GAIN + 2])
@@ -1081,14 +1262,16 @@
     dx_ref[...] = dx1
     g1 = dx1.astype(LOW)
     g1_ref[...] = g1
-    do_ref[...] = dot(g1, wo_ref[0], NT).astype(LOW)
-    add_row(sum_q, jnp.sum(dq_ref[...].astype(FULL), axis=0, keepdims=True) * SCALE, first)
-    add_row(sum_out, jnp.sum(g1.astype(FULL), axis=0, keepdims=True), first)
-    add_row(sum_gain, lines, first)
-    add_row(sum_shift, shifts, first)
-
-
-def cross_back(x1, dq, dx2, w, p, tile=256):
+    grad_mixed = dot(g1, wo_ref[0], NT).astype(LOW)
+    do_ref[...] = grad_mixed
+    inner_ref[...] = inner_parts(grad_mixed, o_ref[...], g1.shape[1] // HD)
+    sum_q[...] += jnp.sum(dq_ref[...].astype(FULL), axis=0, keepdims=True) * SCALE
+    sum_out[...] += jnp.sum(g1.astype(FULL), axis=0, keepdims=True)
+    sum_gain[...] += lines
+    sum_shift[...] += shifts
+
+
+def cross_back(x1, dq, dx2, mixed, w, p, tile=256):
     rows, width = x1.shape
     part = pl.BlockSpec((tile, width), lambda i: (i, 0))
     low = jax.ShapeDtypeStruct((rows, width), LOW)
@@ -1099,23 +1282,27 @@
         4 * rows * width * width,
         16 * rows * width + 4 * width * width,
         grid=(rows // tile,),
-        in_specs=[part, part, part, unit_of(w, 4), unit_of(w, 3), whole(p.shape)],
-        out_specs=[part, part, part] + [whole((1, width))] * 4,
-        out_shape=[jax.ShapeDtypeStruct((rows, width), FULL), low, low, line, line, line, line],
-    )(x1, dq, dx2, w, w, p)
+        in_specs=[part, part, part, part, unit_of(w, 4), unit_of(w, 3), whole(p.shape)],
+        out_specs=[part, part, part, pl.BlockSpec((tile, PAIR), lambda i: (i, 0))] + [whole((1, width))] * 4,
+        out_shape=[jax.ShapeDtypeStruct((rows, width), FULL), low, low, jax.ShapeDtypeStruct((rows, PAIR), LOW), line, line, line, line],
+    )(x1, dq, dx2, mixed, w, w, p)
 
 
 def self_back_kernel(x_ref, dq_ref, dkv_ref, dx1_ref, w_ref, p_ref, dx_ref, sum_q, sum_v, sum_gain, sum_shift):
-    first = pl.program_id(0) == 0
+    @pl.when(pl.program_id(0) == 0)
+    def _():
+        for ref in (sum_q, sum_v, sum_gain, sum_shift):
+            ref[...] = jnp.zeros_like(ref)
+
     dq = dq_ref[...]
     grad = dot(dq, w_ref[0], NT) * SCALE + dot(dkv_ref[0], w_ref[1], NT) + dot(dkv_ref[1], w_ref[2], NT)
     hat, rstd = normal(x_ref[...].astype(FULL))
     back, lines, shifts = normal_back(hat, rstd, grad, p_ref[GAIN : GAIN + 1])
     dx_ref[...] = (dx1_ref[...] + back).astype(LOW)
-    add_row(sum_q, jnp.sum(dq.astype(FULL), axis=0, keepdims=True) * SCALE, first)
-    add_row(sum_v, jnp.sum(dkv_ref[1].astype(FULL), axis=0, keepdims=True), first)
-    add_row(sum_gain, lines, first)
-    add_row(sum_shift, shifts, first)
+    sum_q[...] += jnp.sum(dq.astype(FULL), axis=0, keepdims=True) * SCALE
+    sum_v[...] += jnp.sum(dkv_ref[1].astype(FULL), axis=0, keepdims=True)
+    sum_gain[...] += lines
+    sum_shift[...] += shifts
 
 
 def self_back(x, dq, dkv, dx1, w, p, tile=256):
@@ -1173,24 +1360,20 @@
     depth, ring = mesh.shape["dp"] // 2, mesh.shape["fsdp"]
     own, width = self_out.shape
     blocks = ffn_up.shape[1] // width
-    inverse = jnp.zeros((slots,), jnp.int32).at[deal].set(jnp.arange(slots, dtype=jnp.int32))
     place = lax.axis_index(AXES)
     length = lax.dynamic_slice_in_dim(lengths, place, 1)
     enc_count = lax.dynamic_slice_in_dim(enc_counts, place, 1)
-    tokens = units.shape[1]
-    arrived = exchange(jnp.take(jnp.concatenate([units, encoder], axis=1), deal, axis=0))
-    x = arrived[:, :tokens].reshape(-1, width)
-    memory = arrived[:, tokens:].reshape(-1, width)
+    sent_x, sent_e, sent_c = deal_blocks(deal, [units, encoder, cotangent], False, "deal_in")
 
     up = ffn_up.reshape(own, slots, blocks, own).transpose(2, 0, 1, 3).reshape(blocks, own, width)
-    early = jnp.concatenate([self_qkv, self_out[None], cross_qkv])
     late = jnp.concatenate([cross_out[None], up, ffn_down.reshape(blocks, own, width)])
     rows = jnp.concatenate([biases, norm_gain, norm_shift, ffn_bias_down[None]])
     flat = jnp.concatenate([rows.reshape(-1), ffn_bias_up])
     size = -(-flat.shape[0] // 2048) * 2048
     little = jnp.pad(flat, (0, size - flat.shape[0])).reshape(1, size // 128, 128)
-    w_one, little = first_gather(mesh, early, little, 0)
-    w_one = w_one.reshape(early.shape[0], width, width)
+    w_one, little, x, memory = first_gather(mesh, [self_qkv, self_out, cross_qkv], little, [sent_x, sent_e], 0)
+    w_one = w_one.reshape(-1, width, width)
+    x, memory = x.reshape(-1, width), memory.reshape(-1, width)
     flat = little.reshape(slots, size).astype(FULL)
     p = flat[:, : rows.size].reshape((slots,) + rows.shape)
     p = jnp.moveaxis(p, 0, 1).reshape(rows.shape[0], -1)
@@ -1198,22 +1381,25 @@
     bias_up = flat[:, rows.size : rows.size + ffn_bias_up.size].reshape(slots, blocks, own)
     bias_up = bias_up.transpose(1, 0, 2).reshape(1, -1)
 
-    cot = exchange(jnp.take(after(cotangent, arrived), deal, axis=0)).reshape(-1, width)
-    w_two, a0, qkv, mixed0, level0, x1, a1, q1, kv1, mixed1, level1 = forward(
-        mesh, length, enc_count, x, memory, w_one, p, late, 1
+    w_two, cot, a0, qkv, mixed0, level0, x1, a1, q1, kv1, mixed1, level1 = forward(
+        mesh, length, enc_count, x, memory, w_one, p, late, sent_c, 1
     )
+    cot = cot.reshape(-1, width)
     w_two = w_two.reshape(late.shape[0], width, width)
-    (result, r, du, a2, g3, dx2, g2, grad_mixed1, bias_up_grad, bias_down_grad, bias_five, gain_two, shift_two) = feed(
+    (result, r, du, a2, g3, dx2, g2, grad_mixed1, inner1, bias_up_grad, bias_down_grad, bias_five, gain_two, shift_two) = feed(
         length, x1, mixed1, cot, w_two, p, bias_up
     )
     result = leave(result, slots)
-    dq1, dkv1 = cross_attend_back(enc_count, q1, kv1, mixed1, grad_mixed1, level1)
-    dx1, g1, grad_mixed0, bias_three, bias_two, gain_one, shift_one = cross_back(x1, dq1, dx2, w_one, p)
+    dq1, dkv1 = cross_attend_back(enc_count, q1, kv1, grad_mixed1, level1, inner1)
+    dx1, g1, grad_mixed0, inner0, bias_three, bias_two, gain_one, shift_one = cross_back(x1, dq1, dx2, mixed0, w_one, p)
     made, grad_memory, bias_four = memory_grad(memory, dkv1, w_one)
-    grad_memory = leave(after(grad_memory, result), slots)
-    sums_one, dq0, dkv0 = feed_scatter(mesh, length, a2, g3, du, r, qkv, mixed0, grad_mixed0, level0, 2)
+    grad_memory = after(grad_memory, result).reshape(slots, -1, width)
+    sums_one, dq0, dkv0, grad_memory = feed_scatter(
+        mesh, length, a2, g3, du, r, qkv, grad_mixed0, level0, inner0, grad_memory, 2
+    )
+    up_sum = sums_one[:blocks].reshape(blocks, own, slots, own).transpose(1, 2, 0, 3).reshape(own, -1)
+    down_sum = sums_one[blocks:].reshape(blocks * own, width)
     dx, bias_zero, bias_one, gain_zero, shift_zero = self_back(x, dq0, dkv0, dx1, w_one, p)
-    dx = leave(after(dx, grad_memory), slots)
 
     bias_up_grad = bias_up_grad.reshape(blocks, slots, own).transpose(1, 0, 2).reshape(slots, -1)
 
@@ -1234,20 +1420,23 @@
     terms = jnp.pad(terms, ((0, 0), (0, tiny * 128 - terms.shape[1]))).reshape(depth, 2, ring * tiny, 128)
     part = ring * own
     pairs = (mixed1, g2, a1, dq1, mixed0, g1, a0, dq0, dkv0)
-    sums_two, tiny_sums = last_scatter(mesh, made.reshape(2, depth, 2, part, width), pairs, terms, 3)
+    terms = after(terms, up_sum, down_sum)
+    self_qkv_sum, self_out_sum, cross_qkv_sum, cross_out_sum, tiny_sums, dx = last_scatter(
+        mesh, made.reshape(2, depth, 2, part, width), pairs, terms, dx.reshape(slots, -1, width), 3
+    )
+    result, dx, grad_memory = deal_blocks(deal, [result, dx, grad_memory], True, "deal_out")
     flat = tiny_sums.reshape(-1)
     lines = flat[: 13 * own].reshape(13, own)
-    up_sum = sums_one[:blocks].reshape(blocks, own, slots, own).transpose(1, 2, 0, 3).reshape(own, -1)
     return (
-        jnp.take(result, inverse, axis=0),
-        jnp.take(dx, inverse, axis=0),
-        jnp.take(grad_memory, inverse, axis=0),
-        sums_two[5:8],
-        sums_two[4],
-        jnp.concatenate([sums_two[2:3], sums_two[0:2]]),
-        sums_two[3],
+        result,
+        dx,
+        grad_memory,
+        self_qkv_sum,
+        self_out_sum,
+        cross_qkv_sum,
+        cross_out_sum,
         up_sum,
-        sums_one[blocks:].reshape(blocks * own, width),
+        down_sum,
         lines[:6],
         flat[13 * own : 13 * own + ffn_bias_up.size],
         lines[6],

time: 736 us -> 652 us (0.89)
  starting transfers between devices: 30.7 us -> 5.56 us
  local copies, waits for them, and re-layouts: 49.9 us -> 26.9 us
  Pallas kernels: 619 us -> 597 us
  other arithmetic: 23.6 us -> 3.7 us
    all_to_all x5 -> x1, starting transfers between devices: 30.7 us -> 5.56 us  [exchange(): return lax.all_to_all(array, AXES, split_axis=0, concat_axis=0, tiled=True)]
    select_n x6 -> x0, other arithmetic: 13.3 us -> none  [the longest x1 4.82 us: per_device(): jnp.take(dx, inverse, axis=0)]
    gather x5 -> x0, local copies, waits for them, and re-layouts: 12.9 us -> none  [the longest x1 3.98 us: per_device(): jnp.take(jnp.concatenate([units, encoder], axis=1), deal, axis=0)]
    pallas_call x1, Pallas kernels: 141 us -> 129 us  [forward(): pl.pallas_call(functools.partial(forward_kernel, depth, ring, count), out...]
    pallas_call x2 -> x4, Pallas kernels: 154 us -> 142 us  [the longest x1 111 us: first_gather(): pl.pallas_call(functools.partial(first_gather_kernel, depth, ring, tuple(...]
  transfers between devices with their start and end apart: 5 -> 1, of which waited for: 1 -> 1; matrix products, arithmetic and copies ran while one was open for 6% -> 0% of each run, Pallas kernels for 75% -> 6%
where the time goes in v4:
time: 652 us; the launch traced here: 644 us
  Pallas kernels  597 us (92%)
  local copies, waits for them, and re-layouts  26.9 us (4%)
  waiting for transfers between devices  9.91 us (2%)
    pallas_call x1, Pallas kernels, forward(): pl.pallas_call(functools.partial(forward_kernel, depth, ring, count), out...  129 us
    pallas_call x1, Pallas kernels, last_scatter(): pl.pallas_call(functools.partial(last_scatter_kernel, depth, ring), out_s...  123 us
    pallas_call x1, Pallas kernels, first_gather(): pl.pallas_call(functools.partial(first_gather_kernel, depth, ring, tuple(...  111 us
    pallas_call x1, Pallas kernels, feed_scatter(): pl.pallas_call(functools.partial(feed_scatter_kernel, depth, ring), out_s...  106 us
    pallas_call x1, Pallas kernels, feed(): calls(feed_kernel, 'feed', 2 * rows * width * (4 * inner + 2 * width), 2...  62.3 us
    pallas_call x1, Pallas kernels, cross_attend_back(): calls(functools.partial(cross_attend_back_kernel, width // HD), 'cross_at...  17.4 us
    pallas_call x1, Pallas kernels, self_back(): calls(self_back_kernel, 'self_back', 6 * rows * width * width, 14 * rows...  14.5 us
    pallas_call x1, Pallas kernels, cross_back(): calls(cross_back_kernel, 'cross_back', 4 * rows * width * width, 16 * row...  13.6 us
  transfers between devices with their start and end apart: 1, of which 1 were waited for; matrix products, arithmetic and copies ran while one was open for 0% of the time, Pallas kernels for 6%

profile of v4, /device:TPU:0, one launch (start us, length us, event | category | flops | bytes accessed | tf_op | source)
XLA Modules:
  0.0 644.3 jit_solution(17016198553222739672)
XLA Ops:
  1.5 1.3 fusion.3.refs_3_
  2.8 6.7 %deal_in.1 = (bf16[32,32,1024]{2,1,0:T(8,128)(2,1)}, bf16[32,8,1024]{2,1,0:T(8,128)(2,1)}, bf16[32,32,1024]{2,1,0:T(8,128)(2,1)}) custom-call(s32[32]{0:T(128)} %deal_ref.3, bf16[32,32,1024]{2,1,0:T(8,128)(2,1)} %refs_0_.2, bf16[32,8,1024]{2,1,0:T(8,128)(2,1)} %refs_1_.2, bf16[32,32,1024]{2,1,0:T(8,128)(2,1)} %refs_2_.2), custom_call_target="tpu_custom_call" | custom-call | tf_op jit(solution)/shard_map/deal_in/pallas_call | solution.py:475
  9.5 111.1 %first_gather.1 = (bf16[7,4,2,4,32,1024]{5,4,3,2,1,0:T(8,128)(2,1)}, bf16[1,4,2,4,16,128]{5,4,3,2,1,0:T(8,128)(2,1)}, bf16[32,32,1024]{2,1,0:T(8,128)(2,1)}, bf16[32,8,1024]{2,1,0:T(8,128)(2,1)}) custom-call(bf16[3,32,1024]{2,1,0:T(8,128)(2,1)} %refs_0_.3, bf16[32,1024]{1,0:T(8,128)(2,1)} %refs_1_.3, bf16[3,32,1024]{2,1,0:T(8,128)(2,1)} %refs_2_.3, ...), custom_call_target="tpu_custom_call" | custom-call | flops 60000002048 | bytes 67108864 | tf_op jit(solution)/shard_map/first_gather/pallas_call | solution.py:433
  120.6 0.9 copy.46
  123.1 0.8 reshape.134
  124.1 1.1 reshape.135
  126.7 0.9 pad_maximum_fusion.shard
  127.6 129.1 %forward_gather.1 = (bf16[9,4,2,4,32,1024]{5,4,3,2,1,0:T(8,128)(2,1)}, bf16[32,32,1024]{2,1,0:T(8,128)(2,1)}, bf16[1024,1024]{1,0:T(8,128)(2,1)}, bf16[3,1024,10...) custom-call(s32[1]{0:T(128)} %dynamic_slice.6.n_ref, ...), custom_call_target="tpu_custom_call" | custom-call | flops 70000001024 | bytes 67108864 | tf_op jit(solution)/shard_map/forward_gather/pallas_call | solution.py:751
  256.7 62.3 %feed.1 = (bf16[1024,1024]{1,0:T(8,128)(2,1)}, bf16[4,1024,1024]{2,1,0:T(8,128)(2,1)}, bf16[4,1024,1024]{2,1,0:T(8,128)(2,1)}, bf16[1024,1024]{1,0:T(8,128)(2,1)...) custom-call(s32[1]{0:T(128)} %dynamic_slice.6.n_ref, ...), custom_call_target="tpu_custom_call" | custom-call | flops 38654705664 | bytes 52428800 | tf_op jit(solution)/shard_map/feed/pallas_call | solution.py:1165
  319.0 5.6 all-to-all-start
  326.0 17.4 %cross_attend_back.1 = (bf16[1024,1024]{1,0:T(8,128)(2,1)}, bf16[2,256,1024]{2,1,0:T(8,128)(2,1)}) custom-call(s32[1]{0:T(128)} %dynamic_slice.7.m_ref.n_ref, bf16[1,1024,1024]{2,1,0:T(8,128)(2,1)} %get-tuple-element.92.q_ref, bf16[2,256,1024]{2,1,0:T(8,128)(2,1)} %get-tuple-element.93.k_ref.v_ref, bf16[2,256,1024]{2,1,0:T(8,128)(2,1)} %get-tuple-element.93.k_ref.v_ref, ...), custom_call_target="tpu_custom_call" | custom-call | flops 10737418240 | bytes 10485760 | tf_op jit(solution)/shard_map/cross_attend_back/pallas_call | solution.py:1201
  343.4 6.4 memory_grad.1
  349.8 13.6 %cross_back.1 = (f32[1024,1024]{1,0:T(8,128)}, bf16[1024,1024]{1,0:T(8,128)(2,1)}, bf16[1024,1024]{1,0:T(8,128)(2,1)}, bf16[1024,128]{1,0:T(8,128)(2,1)}, f32[1,...) custom-call(f32[1024,1024]{1,0:T(8,128)} %get-tuple-element.87.x1_ref, ...), custom_call_target="tpu_custom_call" | custom-call | flops 4294967296 | bytes 20971520 | tf_op jit(solution)/shard_map/cross_back/pallas_call | solution.py:1279
  363.4 9.9 %all-to-all-done.refs_0_ = bf16[32,32,1024]{2,1,0:T(8,128)(2,1)S(1)} async-done(((bf16[32,32,1024]{2,1,0:T(8,128)(2,1)}), bf16[32,32,1024]{2,1,0:T(8,128)(2,1)S(1)}, u32[]{:S(2)}, u32[]{:S(2)}) %all-to-all-start) | async-done | bytes 2097184 | tf_op jit(solution)/shard_map/all_to_all | solution.py:1328
  373.3 106.3 %feed_scatter.1 = (f32[8,32,1024]{2,1,0:T(8,128)}, bf16[1024,1024]{1,0:T(8,128)(2,1)}, bf16[2,1024,1024]{2,1,0:T(8,128)(2,1)}, bf16[32,8,1024]{2,1,0:T(8,128)(2,1)}) custom-call(s32[1]{0:T(128)} %dynamic_slice.6.n_ref, bf16[1024,1024]{1,0:T(8,128)(2,1)} %get-tuple-element.106.a2_hbm, bf16[1024,1024]{1,0:T(8,128)(2,1)} %get-tuple-element.107.g3_hbm, ...), custom_call_target="tpu_custom_call" | custom-call | flops 60000002048 | bytes 67108864 | tf_op jit(solution)/shard_map/feed_scatter/pallas_call | solution.py:942
  479.6 2.1 fusion.4
  482.4 3.1 copy.40
  485.5 4.4 reshape.150
  490.0 14.5 %self_back.1 = (bf16[1024,1024]{1,0:T(8,128)(2,1)}, f32[1,1024]{1,0:T(1,128)}, f32[1,1024]{1,0:T(1,128)}, f32[1,1024]{1,0:T(1,128)}, f32[1,1024]{1,0:T(1,128)}) custom-call(bf16[1024,1024]{1,0:T(8,128)(2,1)} %bitcast.43, bf16[1024,1024]{1,0:T(8,128)(2,1)} %get-tuple-element.116.dq_ref.dq0_hbm, bf16[2,1024,1024]{2,1,0:T(8,128)(2,1)} %get-tuple-element.117.dkv_ref.dkv_hbm, ...), custom_call_target="tpu_custom_call" | custom-call | flops 6442450944 | bytes 20971520 | tf_op jit(solution)/shard_map/self_back/pallas_call | solution.py:1312
  504.6 1.5 concatenate.18
  507.2 122.6 %last_scatter.1 = (f32[3,32,1024]{2,1,0:T(8,128)}, f32[32,1024]{1,0:T(8,128)}, f32[3,32,1024]{2,1,0:T(8,128)}, f32[32,1024]{1,0:T(8,128)}, f32[1,8,128]{2,1,0:T(8,128)}, /*index=5*/bf16[32,32,1024]{2,1,0:T(8,128)(2,1)}) custom-call(bf16[2,4,2,128,1024]{4,3,2,1,0:T(8,128)(2,1)} %bitcast.59, bf16[1024,1024]{1,0:T(8,128)(2,1)} %get-tuple-element.88.o_ref.o1_hbm, ...), custom_call_target="tpu_custom_call" | custom-call | flops 60000002048 | bytes 67108864 | tf_op jit(solution)/shard_map/last_scatter/pallas_call | solution.py:1048
  631.8 1.3 slice.50
  633.0 1.3 slice.51
  634.3 6.8 %deal_out.1 = (bf16[32,32,1024]{2,1,0:T(8,128)(2,1)}, bf16[32,32,1024]{2,1,0:T(8,128)(2,1)}, bf16[32,8,1024]{2,1,0:T(8,128)(2,1)}) custom-call(s32[32]{0:T(128)} %deal_ref.3, bf16[32,32,1024]{2,1,0:T(8,128)(2,1)} %copy-done, bf16[32,32,1024]{2,1,0:T(8,128)(2,1)} %get-tuple-element.136.refs_1_, bf16[32,8,1024]{2,1,0:T(8,128)(2,1)} %get-tuple-element.137.refs_2_), custom_call_target="tpu_custom_call" | custom-call | tf_op jit(solution)/shard_map/deal_out/pallas_call | solution.py:475
  (72 shorter events, 12.0 us)
Async XLA Ops:
  9.5 112.2 %copy-start.18 = (s32[32]{0:T(128)S(1)}, s32[32]{0:T(128)}, u32[]{:S(2)}) copy-start(s32[32]{0:T(128)} %param.21) | copy-start | bytes 388
  9.5 112.7 %copy-start.19 = (s32[32]{0:T(128)S(1)}, s32[32]{0:T(128)}, u32[]{:S(2)}) copy-start(s32[32]{0:T(128)} %param.22) | copy-start | bytes 388
  9.5 113.6 %copy-start.3 = (bf16[32,4096]{1,0:T(8,128)(2,1)S(1)}, bf16[32,4096]{1,0:T(8,128)(2,1)}, u32[]{:S(2)}) copy-start(bf16[32,4096]{1,0:T(8,128)(2,1)} %param.27) | copy-start | bytes 786436
  123.9 2.8 copy-start.4
  123.9 2.8 copy-start.7
  319.0 6.1 copy-start.8
  319.0 54.3 %all-to-all-start = ((bf16[32,32,1024]{2,1,0:T(8,128)(2,1)}), bf16[32,32,1024]{2,1,0:T(8,128)(2,1)S(1)}, u32[]{:S(2)}, u32[]{:S(2)}) async-start(bf16[32,32,1024]{2,1,0:T(8,128)(2,1)} %bitcast.41), calls=%async_computation | async-start | bytes 4194304 | tf_op jit(solution)/shard_map/all_to_all | solution.py:1328
  373.3 106.3 %copy-start = (bf16[32,32,1024]{2,1,0:T(8,128)(2,1)}, bf16[32,32,1024]{2,1,0:T(8,128)(2,1)S(1)}, u32[]{:S(2)}) copy-start(bf16[32,32,1024]{2,1,0:T(8,128)(2,1)S(1)} %all-to-all-done.refs_0_) | copy-start | bytes 6291460
  489.9 14.6 %copy-start.9 = (f32[1,1024]{1,0:T(1,128)S(1)}, f32[1,1024]{1,0:T(1,128)}, u32[]{:S(2)}) copy-start(f32[1,1024]{1,0:T(1,128)} %get-tuple-element.125) | copy-start | bytes 12292
  489.9 14.6 %copy-start.10 = (f32[1,1024]{1,0:T(1,128)S(1)}, f32[1,1024]{1,0:T(1,128)}, u32[]{:S(2)}) copy-start(f32[1,1024]{1,0:T(1,128)} %get-tuple-element.124) | copy-start | bytes 12292
  489.9 14.6 %copy-start.11 = (f32[1,1024]{1,0:T(1,128)S(1)}, f32[1,1024]{1,0:T(1,128)}, u32[]{:S(2)}) copy-start(f32[1,1024]{1,0:T(1,128)} %get-tuple-element.128) | copy-start | bytes 12292
  489.9 14.6 %copy-start.12 = (f32[1,1024]{1,0:T(1,128)S(1)}, f32[1,1024]{1,0:T(1,128)}, u32[]{:S(2)}) copy-start(f32[1,1024]{1,0:T(1,128)} %get-tuple-element.131) | copy-start | bytes 12292
  489.9 14.6 %copy-start.13 = (f32[1,1024]{1,0:T(1,128)S(1)}, f32[1,1024]{1,0:T(1,128)}, u32[]{:S(2)}) copy-start(f32[1,1024]{1,0:T(1,128)} %get-tuple-element.123) | copy-start | bytes 12292
  489.9 14.6 %copy-start.14 = (f32[1,1024]{1,0:T(1,128)S(1)}, f32[1,1024]{1,0:T(1,128)}, u32[]{:S(2)}) copy-start(f32[1,1024]{1,0:T(1,128)} %get-tuple-element.122) | copy-start | bytes 12292
  489.9 14.6 %copy-start.15 = (f32[1,1024]{1,0:T(1,128)S(1)}, f32[1,1024]{1,0:T(1,128)}, u32[]{:S(2)}) copy-start(f32[1,1024]{1,0:T(1,128)} %get-tuple-element.121) | copy-start | bytes 12292
  489.9 14.6 %copy-start.16 = (f32[1,1024]{1,0:T(1,128)S(1)}, f32[1,1024]{1,0:T(1,128)}, u32[]{:S(2)}) copy-start(f32[1,1024]{1,0:T(1,128)} %get-tuple-element.127) | copy-start | bytes 12292
  490.0 14.6 %copy-start.17 = (f32[1,1024]{1,0:T(1,128)S(1)}, f32[1,1024]{1,0:T(1,128)}, u32[]{:S(2)}) copy-start(f32[1,1024]{1,0:T(1,128)} %get-tuple-element.130) | copy-start | bytes 12292
  634.3 6.8 %copy-start.2 = (f32[3,32,1024]{2,1,0:T(8,128)S(1)}, f32[3,32,1024]{2,1,0:T(8,128)}, u32[]{:S(2)}) copy-start(f32[3,32,1024]{2,1,0:T(8,128)} %get-tuple-element.167) | copy-start | bytes 1179652
  634.3 7.6 %copy-start.6 = (f32[32,1024]{1,0:T(8,128)S(1)}, f32[32,1024]{1,0:T(8,128)}, u32[]{:S(2)}) copy-start(f32[32,1024]{1,0:T(8,128)} %get-tuple-element.168) | copy-start | bytes 393220
  634.3 8.2 %copy-start.1 = (f32[3,32,1024]{2,1,0:T(8,128)S(1)}, f32[3,32,1024]{2,1,0:T(8,128)}, u32[]{:S(2)}) copy-start(f32[3,32,1024]{2,1,0:T(8,128)} %get-tuple-element.169) | copy-start | bytes 1179652
  634.3 9.0 %copy-start.5 = (f32[32,1024]{1,0:T(8,128)S(1)}, f32[32,1024]{1,0:T(8,128)}, u32[]{:S(2)}) copy-start(f32[32,1024]{1,0:T(8,128)} %get-tuple-element.170) | copy-start | bytes 393220

commit v5 on v4

--- a/solution.py
+++ b/solution.py
@@ -43,6 +43,9 @@
         hail(self.z * 2 + self.c, self.left)
         hail(self.z * 2 + 1 - self.c, self.f)
         pl.semaphore_wait(barrier, self.depth + 2)
+
+    def index(self):
+        return (self.z * 2 + self.c) * self.ring + self.f
 
     def peers(self):
         return 2 * self.depth * self.ring
@@ -370,8 +373,12 @@
         for u in range(max(0, self.count - self.slots), self.count):
             self.core(u).wait_send()
 
+    def last_sums(self):
+        for u in range(self.count):
+            self.last_sum(u)
+
     def steps(self):
-        return self.count + self.place.half // 2 + 1
+        return self.count + self.place.half // 2
 
     def early(self, i):
         for t in range(1, self.place.half + 1, 2):
@@ -383,8 +390,6 @@
         for t in range(2, self.place.half + 1, 2):
             u = i - t // 2
             when(both(0 <= u, u < self.count), functools.partial(self.next_sum, u, t))
-        u = i - self.place.half // 2 - 1
-        when(both(0 <= u, u < self.count), lambda: self.last_sum(u))
 
 
 def remote_params(ident):
@@ -607,6 +612,7 @@
 ):
     place = Place(depth, ring)
     place.greet_all()
+    me = place.index()
     gather = Gather(place, count, shard, full, sems[:7], ahead=count)
     swap = Exchange(place, ((sent, arrived),), gather.steps() - 2, sems[7:])
     gather.begin()
@@ -668,7 +674,7 @@
         def store(at, value):
             o_ref[at, cols] = value
 
-        attend_pair(True, tile, h, n_ref[0], qkv_ref[0, :, cols], qkv_ref[1, :, cols], qkv_ref[2, :, cols], store, l0_ref)
+        attend_pair(True, tile, h, n_ref[me], qkv_ref[0, :, cols], qkv_ref[1, :, cols], qkv_ref[2, :, cols], store, l0_ref)
         when(h % 2 == 0, lambda: advance(2 + h // 2))
 
     loop(pairs, self_pair)
@@ -709,7 +715,7 @@
         def store(at, value):
             o_ref[at, cols] = value
 
-        attend_pair(False, tile, h, m_ref[0], q1_ref[:, cols], kv_ref[0, :, cols], kv_ref[1, :, cols], store, l1_ref)
+        attend_pair(False, tile, h, m_ref[me], q1_ref[:, cols], kv_ref[0, :, cols], kv_ref[1, :, cols], store, l1_ref)
         when(h % 2 == 0, lambda: advance(done + h // 2))
 
     loop(pairs, cross_pair)
@@ -836,150 +842,285 @@
             held[slot, at // 2, at % 2] = value[k * part : (k + 1) * part]
 
 
-def feed_scatter_kernel(
-    depth, ring, n_ref, a2_hbm, g3_hbm, du_hbm, r_hbm, qkv_hbm, grad_hbm, l_ref, i_ref, sent,
-    outs, dq_hbm, dkv_hbm, arrived,
-    a2_ref, g3_ref, moving, held, q_buf, acc_ref, dq_buf, dkv_buf, in_sem, move_sem, q_sem, out_sem, *rest,
+def back_scatter_kernel(
+    depth, ring, n_ref, m_ref, a2_hbm, g3_hbm, du_hbm, r_hbm, qkv_hbm, q1_hbm, kv_hbm, do1_hbm, l1_ref, i1_ref,
+    x1_hbm, dx2_hbm, o0_hbm, w_hbm, l0_ref, p_ref, sent,
+    up_out, down_out, dq1_hbm, dkv1_hbm, dx1_hbm, g1_hbm, dq_hbm, dkv_hbm, arrived, sum_q, sum_out, sum_gain, sum_shift,
+    kept_ref, moving, held, q_buf, acc_ref, dq_buf, dkv_buf, dq1_ref, kv_ref, dkv1_ref, w_ref,
+    x1_buf, dx2_buf, o_buf, dx1_buf, g1_buf, i0_ref, up_ref,
+    in_sem, move_sem, q_sem, out_sem, tile_in, tile_out, *rest,
 ):
     place = Place(depth, ring)
     place.greet_all()
+    me = place.index()
     blocks = du_hbm.shape[0]
     count = 2 * blocks
+    rows, width = do1_hbm.shape
+    pairs = width // PAIR
+    tile = x1_buf.shape[1]
+    tiles = rows // tile
+
+    own = up_out.shape[0]
 
     def put_sum(u, total):
-        outs[u] = total
-
-    sums = Scatter(place, count, outs.shape[1], held, put_sum, rest[:5], rest[5:11])
+        if u < blocks:
+            up_ref[u] = total
+        else:
+            down_out[(u - blocks) * own : (u - blocks + 1) * own] = total
+
+    def place_up():
+        for k in range(width // own):
+            lines = [up_ref[j, :, k * own : (k + 1) * own] for j in range(blocks)]
+            up_out[:, k * blocks * own : (k + 1) * blocks * own] = jnp.concatenate(lines, axis=1)
+
+    sums = Scatter(place, count, own, held, put_sum, rest[:5], rest[5:11])
     swap = Exchange(place, ((sent, arrived),), count, rest[11:])
-    pairs = grad_hbm.shape[1] // PAIR
-    swap.begin()
     slots = held.shape[0]
-    load_a = pltpu.make_async_copy(a2_hbm, a2_ref, in_sem.at[0])
-    load_g = pltpu.make_async_copy(g3_hbm, g3_ref, in_sem.at[1])
-
-    def move(u, array, j):
-        return pltpu.make_async_copy(array.at[j], moving.at[u % 2], move_sem.at[u % 2])
-
-    def start_move(u):
-        when(u < blocks, lambda: move(u, du_hbm, u).start())
-        when(u >= blocks, lambda: move(u, r_hbm, jnp.maximum(u - blocks, 0)).start())
+    load_a = pltpu.make_async_copy(a2_hbm, kept_ref, in_sem.at[0])
+    load_g = pltpu.make_async_copy(g3_hbm, kept_ref, in_sem.at[1])
+    load_kv = pltpu.make_async_copy(kv_hbm, kv_ref, in_sem.at[2])
+    load_w = [pltpu.make_async_copy(w_hbm.at[u], w_ref.at[k], in_sem.at[3 + k]) for k, u in enumerate((4, 3))]
+    send_dq1 = pltpu.make_async_copy(dq1_ref, dq1_hbm, in_sem.at[5])
+    send_dkv1 = pltpu.make_async_copy(dkv1_ref, dkv1_hbm, in_sem.at[6])
+
+    def move(u):
+        source = du_hbm.at[u] if u < blocks else r_hbm.at[u - blocks]
+        return pltpu.make_async_copy(source, moving, move_sem.at[0])
+
+    def columns(h):
+        return pl.ds(pl.multiple_of(h * PAIR, PAIR), PAIR)
+
+    def fetch_cross(h):
+        cols = columns(h)
+        sources = [q1_hbm.at[0, :, cols], do1_hbm.at[:, cols]]
+        return [pltpu.make_async_copy(s, q_buf.at[h % 2, k], q_sem.at[h % 2, k]) for k, s in enumerate(sources)]
 
     def fetch(h):
-        cols = pl.ds(pl.multiple_of(h * PAIR, PAIR), PAIR)
-        sources = [qkv_hbm.at[0, :, cols], qkv_hbm.at[1, :, cols], qkv_hbm.at[2, :, cols], grad_hbm.at[:, cols]]
-        return [pltpu.make_async_copy(s, q_buf.at[h % 2, k], q_sem.at[h % 2, k]) for k, s in enumerate(sources)]
+        cols = columns(h)
+        return [pltpu.make_async_copy(qkv_hbm.at[k, :, cols], q_buf.at[h % 2, k], q_sem.at[h % 2, k]) for k in range(3)]
 
     def put(h):
-        cols = pl.ds(pl.multiple_of(h * PAIR, PAIR), PAIR)
+        cols = columns(h)
         return [
             pltpu.make_async_copy(dq_buf.at[h % 2], dq_hbm.at[:, cols], out_sem.at[h % 2, 0]),
             pltpu.make_async_copy(dkv_buf.at[h % 2], dkv_hbm.at[:, :, cols], out_sem.at[h % 2, 1]),
         ]
 
+    def load_tile(i):
+        at, b = slice(i * tile, (i + 1) * tile), i % 2
+        sources = ((x1_hbm, x1_buf), (dx2_hbm, dx2_buf), (o0_hbm, o_buf))
+        return [pltpu.make_async_copy(s.at[at], d.at[b], tile_in.at[b, k]) for k, (s, d) in enumerate(sources)]
+
+    def store_tile(i):
+        at = slice(i * tile, (i + 1) * tile)
+        targets = ((dx1_buf, dx1_hbm), (g1_buf, g1_hbm))
+        return [pltpu.make_async_copy(s, d.at[at], tile_out.at[k]) for k, (s, d) in enumerate(targets)]
+
+    def start(copies):
+        for copy in copies:
+            copy.start()
+
+    def wait(copies):
+        for copy in copies:
+            copy.wait()
+
     load_a.start()
-    start_move(0)
-    for copy in fetch(0):
-        copy.start()
-    load_g.start()
+    move(0).start()
+    load_kv.start()
+    start(fetch_cross(0))
+    swap.begin()
+    start(load_w)
+    for ref in (sum_q, sum_out, sum_gain, sum_shift):
+        ref[...] = jnp.zeros_like(ref)
     load_a.wait()
 
     def weights(i):
-        when(i + 1 < count, lambda: start_move(i + 1))
-        when(i == blocks, load_g.wait)
-        move(i, du_hbm, 0).wait()
-        when(i >= slots, lambda: sums.core(i - slots).wait_send())
-        slot = i % slots
-        when(i < blocks, lambda: unit_grad(place, held, slot, a2_ref, moving.at[i % 2], None))
-        when(i >= blocks, lambda: unit_grad(place, held, slot, moving.at[i % 2], g3_ref, None))
+        if i == blocks:
+            load_g.wait()
+        move(i).wait()
+        if i >= slots:
+            sums.core(i - slots).wait_send()
+        if i < blocks:
+            unit_grad(place, held, i % slots, kept_ref, moving, None)
+            if i == blocks - 1:
+                load_g.start()
+        else:
+            unit_grad(place, held, i % slots, moving, kept_ref, None)
+        if i + 1 < count:
+            move(i + 1).start()
         sums.core(i).start()
 
-    def heads(h):
-        def next_fetch():
-            for copy in fetch(h + 1):
-                copy.start()
-
-        when(h + 1 < pairs, next_fetch)
-        for copy in fetch(h):
-            copy.wait()
-
-        def free():
-            for copy in put(h - 2):
-                copy.wait()
-
-        when(h >= 2, free)
-        b = h % 2
+    def cross_pair(h):
+        pl.when(h + 1 < pairs)(lambda: start(fetch_cross(h + 1)))
+        wait(fetch_cross(h))
+        b, cols = h % 2, columns(h)
+
+        def store(at, grad_k, grad_v):
+            dkv1_ref[0, at, cols] = grad_k
+            dkv1_ref[1, at, cols] = grad_v
+
+        back_pair(False, kv_ref.shape[1], h, 2 * pairs, m_ref[me], q_buf[b, 0], kv_ref[0, :, cols], kv_ref[1, :, cols],
+                  q_buf[b, 1], l1_ref[...], i1_ref[...], acc_ref, store)
+        dq1_ref[:, cols] = acc_ref[...].astype(LOW)
+
+    def between(i):
+        at, b = slice(i * tile, (i + 1) * tile), i % 2
+        if i + 1 < tiles:
+            start(load_tile(i + 1))
+        wait(load_tile(i))
+        dq = dq1_ref[at]
+        grad = dot(dq, w_ref[0], NT) * SCALE
+        hat, rstd = normal(x1_buf[b])
+        back, lines, shifts = normal_back(hat, rstd, grad, p_ref[GAIN + 1 : GAIN + 2])
+        dx1 = dx2_buf[b] + back
+        g1 = dx1.astype(LOW)
+        if i > 0:
+            wait(store_tile(i - 1))
+        dx1_buf[...] = dx1
+        g1_buf[...] = g1
+        start(store_tile(i))
+        grad_mixed = dot(g1, w_ref[1], NT).astype(LOW)
+        dq1_ref[at] = grad_mixed
+        i0_ref[at] = inner_parts(grad_mixed, o_buf[b], 2 * pairs)
+        sum_q[...] += jnp.sum(dq.astype(FULL), axis=0, keepdims=True) * SCALE
+        sum_out[...] += jnp.sum(g1.astype(FULL), axis=0, keepdims=True)
+        sum_gain[...] += lines
+        sum_shift[...] += shifts
+
+    def self_pair(h):
+        pl.when(h + 1 < pairs)(lambda: start(fetch(h + 1)))
+        wait(fetch(h))
+        pl.when(h >= 2)(lambda: wait(put(h - 2)))
+        b, cols = h % 2, columns(h)
 
         def store(at, grad_k, grad_v):
             dkv_buf[b, 0, at] = grad_k
             dkv_buf[b, 1, at] = grad_v
 
-        back_pair(True, 256, h, 2 * pairs, n_ref[0], q_buf[b, 0], q_buf[b, 1], q_buf[b, 2], q_buf[b, 3], l_ref[...], i_ref[...], acc_ref, store)
+        back_pair(True, 256, h, 2 * pairs, n_ref[me], q_buf[b, 0], q_buf[b, 1], q_buf[b, 2], dq1_ref[:, cols],
+                  l0_ref[...], i0_ref[...], acc_ref, store)
         dq_buf[b] = acc_ref[...].astype(LOW)
-        for copy in put(h):
-            copy.start()
-
-    def step(i):
-        when(i < count, lambda: weights(i))
+        start(put(h))
+
+    def run(part, low, high):
+        loop(high - low, lambda j: part(low + j))
+
+    def work(i):
+        if i < 2:
+            if i == 0:
+                load_kv.wait()
+            run(cross_pair, i * (pairs // 2), (i + 1) * (pairs // 2))
+            if i == 1:
+                send_dq1.start()
+                send_dkv1.start()
+                start(load_tile(0))
+                start(fetch(0))
+                wait(load_w)
+        elif i < 4:
+            if i == 2:
+                send_dq1.wait()
+            for j in range((i - 2) * tiles // 2, (i - 1) * tiles // 2):
+                between(j)
+            if i == 3:
+                wait(store_tile(tiles - 1))
+        else:
+            run(self_pair, shares[i - 4], shares[i - 3])
+
+    steps = sums.steps()
+    left = steps - 4
+    shares = [pairs - ((left - k) * pairs + left - 1) // left for k in range(left + 1)]
+    for i in range(steps):
+        if i < count:
+            weights(i)
         sums.early(i)
-        when(i < pairs, lambda: heads(i))
+        work(i)
         sums.late(i)
         swap.step(i)
-
-    loop(max(sums.steps(), pairs), step)
-    for h in range(max(0, pairs - 2), pairs):
-        for copy in put(h):
-            copy.wait()
+    for h in range(pairs - 2, pairs):
+        wait(put(h))
+    send_dkv1.wait()
+    sums.last_sums()
+    place_up()
     sums.finish()
     swap.finish()
 
 
-def feed_scatter(mesh, length, a2, g3, du, r, qkv, grad, level, inner, sent, ident):
+def back_scatter(mesh, length, enc_count, a2, g3, du, r, qkv, q1, kv1, do1, level1, inner1, x1, dx2, mixed0, w, level0, p, sent, ident):
     depth, ring = mesh.shape["dp"] // 2, mesh.shape["fsdp"]
     blocks, rows, width = du.shape
     own = width // (2 * depth * ring)
     count = 2 * blocks
+    enc = kv1.shape[1]
+    tile = 256
     big = pltpu.VMEM((rows, width), LOW)
+    low = jax.ShapeDtypeStruct((rows, width), LOW)
+    line = jax.ShapeDtypeStruct((1, width), FULL)
     return pl.pallas_call(
-        functools.partial(feed_scatter_kernel, depth, ring),
+        functools.partial(back_scatter_kernel, depth, ring),
         out_shape=[
-            jax.ShapeDtypeStruct((count, own, width), FULL),
-            jax.ShapeDtypeStruct((rows, width), LOW),
+            jax.ShapeDtypeStruct((own, blocks * width), FULL),
+            jax.ShapeDtypeStruct((blocks * own, width), FULL),
+            low,
+            jax.ShapeDtypeStruct((2, enc, width), LOW),
+            jax.ShapeDtypeStruct((rows, width), FULL),
+            low,
+            low,
             jax.ShapeDtypeStruct((2, rows, width), LOW),
             jax.ShapeDtypeStruct(sent.shape, sent.dtype),
+            line,
+            line,
+            line,
+            line,
         ],
-        in_specs=[SMEM] + [ANY] * 6 + [VMEM, VMEM, ANY],
-        out_specs=[VMEM, ANY, ANY, ANY],
+        in_specs=[SMEM, SMEM] + [ANY] * 8 + [VMEM, VMEM] + [ANY] * 4 + [VMEM, VMEM, ANY],
+        out_specs=[VMEM] * 2 + [ANY] * 7 + [VMEM] * 4,
         scratch_shapes=[
             big,
             big,
-            pltpu.VMEM((2, rows, width), LOW),
-            pltpu.VMEM((3, depth, 2, ring * own, width), LOW),
-            pltpu.VMEM((2, 4, rows, PAIR), LOW),
+            pltpu.VMEM((2, depth, 2, ring * own, width), LOW),
+            pltpu.VMEM((2, 3, rows, PAIR), LOW),
             pltpu.VMEM((rows, PAIR), FULL),
             pltpu.VMEM((2, rows, PAIR), LOW),
             pltpu.VMEM((2, 2, rows, PAIR), LOW),
+            big,
+            pltpu.VMEM((2, enc, width), LOW),
+            pltpu.VMEM((2, enc, width), LOW),
+            pltpu.VMEM((2, width, width), LOW),
+            pltpu.VMEM((2, tile, width), FULL),
+            pltpu.VMEM((2, tile, width), FULL),
+            pltpu.VMEM((2, tile, width), LOW),
+            pltpu.VMEM((tile, width), FULL),
+            pltpu.VMEM((tile, width), LOW),
+            pltpu.VMEM((rows, PAIR), LOW),
+            pltpu.VMEM((blocks, own, width), FULL),
+            DMA((7,)),
+            DMA((1,)),
+            DMA((2, 3)),
+            DMA((2, 2)),
+            DMA((2, 3)),
             DMA((2,)),
-            DMA((2,)),
-            DMA((2, 4)),
-            DMA((2, 2)),
         ]
         + Scatter.refs(mesh, count, own, width, LOW)
         + Scatter.sems(mesh, count)
         + Exchange.sems(mesh, 1),
         compiler_params=remote_params(ident),
-        cost_estimate=pl.CostEstimate(flops=60_000_000_000, bytes_accessed=2 * 33_554_432, transcendentals=0),
-        name="feed_scatter",
-    )(length, a2, g3, du, r, qkv, grad, level, inner, sent)
+        cost_estimate=pl.CostEstimate(flops=90_000_000_000, bytes_accessed=2 * 33_554_432, transcendentals=0),
+        name="back_scatter",
+    )(length, enc_count, a2, g3, du, r, qkv, q1, kv1, do1, level1, inner1, x1, dx2, mixed0, w, level0, p, sent)
 
 
 def last_scatter_kernel(
-    depth, ring, made_hbm, o1_hbm, g2_hbm, a1_hbm, dq1_hbm, o0_hbm, g1_hbm, a0_hbm, dq0_hbm, dkv_hbm, tiny_ref, sent,
-    s_qkv, s_out, c_qkv, c_out, tiny_out, arrived, left, right, held, tiny_held, left_sem, right_sem, made_sem, *rest,
+    depth, ring, e_hbm, dkv1_hbm, w_hbm, x_hbm, dx1_hbm, o1_hbm, g2_hbm, a1_hbm, dq1_hbm, o0_hbm, g1_hbm, a0_hbm, dq0_hbm,
+    dkv_hbm, p_ref, tiny_ref,
+    s_qkv, s_out, c_qkv, c_out, tiny_out, arrived, arrived_e, sent, sent_e,
+    left, right, held, tiny_held, e_ref, dkv1_ref, w_ref, de_ref, x_buf, dq_buf, dkv_buf, dx1_buf, dx_buf,
+    sum_q, sum_v, sum_m, sum_gain, sum_shift, left_sem, right_sem, in_sem, w_sem, tile_in, tile_out, *rest,
 ):
     place = Place(depth, ring)
     place.greet_all()
-    made = made_hbm.shape[0]
+    made = 2
     spots = [c_qkv.at[1], c_qkv.at[2], c_qkv.at[0], c_out, s_out, s_qkv.at[0], s_qkv.at[1], s_qkv.at[2]]
+    own = s_out.shape[0]
 
     def put_sum(u, total):
         spots[u][...] = total
@@ -991,10 +1132,14 @@
     scaled = (0, 3)
     count = made + len(pairs)
     small = Scatter(place, 1, tiny_out.shape[1], tiny_held, put_tiny, rest[:5], rest[5:11])
-    sums = Scatter(place, count, s_out.shape[0], held, put_sum, rest[11:16], rest[16:22])
-    swap = Exchange(place, ((sent, arrived),), count, rest[22:])
-    swap.begin()
+    sums = Scatter(place, count, own, held, put_sum, rest[11:16], rest[16:22])
     slots = held.shape[0]
+    rows, width = x_hbm.shape
+    tile = x_buf.shape[1]
+    tiles = rows // tile
+    begun = 3
+    swap = Exchange(place, ((sent, arrived), (sent_e, arrived_e)), count - begun, rest[22:])
+    leaves = dx_buf.shape[1]
 
     def load(k):
         a, b = pairs[k]
@@ -1003,48 +1148,131 @@
             pltpu.make_async_copy(b, right.at[k % 2], right_sem.at[k % 2]),
         ]
 
-    given = [pltpu.make_async_copy(made_hbm.at[u], held.at[u], made_sem.at[u]) for u in range(made)]
-    for copy in given:
-        copy.start()
+    def load_tile(i):
+        at, b = slice(i * tile, (i + 1) * tile), i % 2
+        sources = ((x_hbm.at[at], x_buf), (dq0_hbm.at[at], dq_buf), (dkv_hbm.at[:, at], dkv_buf), (dx1_hbm.at[at], dx1_buf))
+        return [pltpu.make_async_copy(s, d.at[b], tile_in.at[b, k]) for k, (s, d) in enumerate(sources)]
+
+    def store_tile(i):
+        many = tile // leaves
+        return pltpu.make_async_copy(dx_buf, sent.at[i * many : (i + 1) * many], tile_out.at[0])
+
+    def start(copies):
+        for copy in copies:
+            copy.start()
+
+    def wait(copies):
+        for copy in copies:
+            copy.wait()
+
+    load_e = [pltpu.make_async_copy(e_hbm, e_ref, in_sem.at[0]), pltpu.make_async_copy(dkv1_hbm, dkv1_ref, in_sem.at[1])]
+    load_m = [pltpu.make_async_copy(w_hbm.at[5 + j], w_ref.at[j], w_sem.at[j]) for j in range(2)]
+    load_w = [pltpu.make_async_copy(w_hbm.at[j], w_ref.at[j], w_sem.at[j]) for j in range(3)]
+    send_e = pltpu.make_async_copy(de_ref, sent_e, in_sem.at[2])
+    start(load_e)
+    start(load_m)
+    start(load_tile(0))
     for k in range(2):
-        for copy in load(k):
-            copy.start()
+        start(load(k))
     tiny_held[0] = tiny_ref[...]
-    small.core(0).start()
+    for ref in (sum_q, sum_v, sum_gain, sum_shift):
+        ref[...] = jnp.zeros_like(ref)
+    wait(load_e)
+
+    def weights(i):
+        if i >= slots:
+            sums.core(i - slots).wait_send()
+        if i < made:
+            unit_grad(place, held, i % slots, e_ref, dkv1_ref.at[i], None)
+        else:
+            k = i - made
+            wait(load(k))
+            unit_grad(place, held, i % slots, left.at[k % 2], right.at[k % 2], SCALE if k in scaled else None)
+            if k + 2 < len(pairs):
+                start(load(k + 2))
+        sums.core(i).start()
+
+    def memory_back():
+        wait(load_m)
+        back = dot(dkv1_ref[0], w_ref[0], NT) + dot(dkv1_ref[1], w_ref[1], NT)
+        de_ref[...] = back.astype(LOW).reshape(de_ref.shape)
+        send_e.start()
+        start(load_w)
+        sum_m[...] = jnp.sum(dkv1_ref[1].astype(FULL), axis=0, keepdims=True)
+
+    def part(i):
+        b = i % 2
+        if i + 1 < tiles:
+            start(load_tile(i + 1))
+        wait(load_tile(i))
+        if i == 0:
+            wait(load_w)
+        dq = dq_buf[b]
+        grad = dot(dq, w_ref[0], NT) * SCALE + dot(dkv_buf[b, 0], w_ref[1], NT) + dot(dkv_buf[b, 1], w_ref[2], NT)
+        hat, rstd = normal(x_buf[b].astype(FULL))
+        back, lines, shifts = normal_back(hat, rstd, grad, p_ref[GAIN : GAIN + 1])
+        dx = (dx1_buf[b] + back).astype(LOW)
+        if i > 0:
+            store_tile(i - 1).wait()
+        dx_buf[...] = dx.reshape(dx_buf.shape)
+        store_tile(i).start()
+        sum_q[...] += jnp.sum(dq.astype(FULL), axis=0, keepdims=True) * SCALE
+        sum_v[...] += jnp.sum(dkv_buf[b, 1].astype(FULL), axis=0, keepdims=True)
+        sum_gain[...] += lines
+        sum_shift[...] += shifts
+
+    def place_lines():
+        for line, ref in ((0, sum_q), (1, sum_v), (4, sum_m), (7, sum_gain), (10, sum_shift)):
+            row, lane = line * own // 128, line * own % 128
+            for k in range(width // own):
+                d, g = k // ring, k % ring
+                at = g * tiny_out.shape[1] + row
+                tiny_held[0, d // 2, d % 2, at : at + 1, lane : lane + own] = ref[:, k * own : (k + 1) * own]
+
+    def work(i):
+        if i == 0:
+            memory_back()
+        elif i == 1:
+            for j in range(tiles // 2):
+                part(j)
+        elif i == 2:
+            for j in range(tiles // 2, tiles):
+                part(j)
+            store_tile(tiles - 1).wait()
+            send_e.wait()
+            swap.begin()
+            place_lines()
+            small.core(0).start()
+
     for i in range(sums.steps()):
         if i < count:
-            k = i - made
-            if i < made:
-                given[i].wait()
-            else:
-                for copy in load(k):
-                    copy.wait()
-                if i >= slots:
-                    sums.core(i - slots).wait_send()
-                unit_grad(place, held, i % slots, left.at[k % 2], right.at[k % 2], SCALE if k in scaled else None)
-                if k + 2 < len(pairs):
-                    for copy in load(k + 2):
-                        copy.start()
-            sums.core(i).start()
-        if i < small.steps():
-            small.early(i)
+            weights(i)
         sums.early(i)
-        if i < small.steps():
-            small.late(i)
+        if 0 <= i - begun < small.steps():
+            small.early(i - begun)
+        work(i)
         sums.late(i)
-        swap.step(i)
+        if 0 <= i - begun < small.steps():
+            small.late(i - begun)
+        if i >= begun - 1:
+            swap.step(i - begun + 1)
+    small.last_sums()
+    sums.last_sums()
     small.finish()
     sums.finish()
     swap.finish()
 
 
-def last_scatter(mesh, made, pairs, tiny, sent, ident):
+def last_scatter(mesh, memory, dkv1, w, x, dx1, pairs, p, tiny, like, like_e, ident):
     depth, ring = mesh.shape["dp"] // 2, mesh.shape["fsdp"]
-    n, width = made.shape[0], made.shape[-1]
-    rows = pairs[0].shape[0]
-    own = made.shape[3] // ring
-    count = n + 6
+    rows, width = x.shape
+    enc = memory.shape[0]
+    own = width // (2 * depth * ring)
+    count = 8
+    tile = 256
     tiny_rows = tiny.shape[2] // ring
+    line = pltpu.VMEM((1, width), FULL)
+    moved = [jax.ShapeDtypeStruct(like, LOW), jax.ShapeDtypeStruct(like_e, LOW)]
     return pl.pallas_call(
         functools.partial(last_scatter_kernel, depth, ring),
         out_shape=[
@@ -1053,28 +1281,46 @@
             jax.ShapeDtypeStruct((3, own, width), FULL),
             jax.ShapeDtypeStruct((own, width), FULL),
             jax.ShapeDtypeStruct((1, tiny_rows, tiny.shape[3]), FULL),
-            jax.ShapeDtypeStruct(sent.shape, sent.dtype),
-        ],
-        in_specs=[ANY] * (1 + len(pairs)) + [VMEM, ANY],
-        out_specs=[VMEM] * 5 + [ANY],
+        ]
+        + moved
+        + moved,
+        in_specs=[ANY] * (5 + len(pairs)) + [VMEM, VMEM],
+        out_specs=[VMEM] * 5 + [ANY] * 4,
         scratch_shapes=[
             pltpu.VMEM((2, rows, width), LOW),
             pltpu.VMEM((2, rows, width), LOW),
-            pltpu.VMEM((3,) + made.shape[1:], LOW),
+            pltpu.VMEM((2, depth, 2, ring * own, width), LOW),
             pltpu.VMEM((1,) + tiny.shape, FULL),
+            pltpu.VMEM((enc, width), LOW),
+            pltpu.VMEM((2, enc, width), LOW),
+            pltpu.VMEM((3, width, width), LOW),
+            pltpu.VMEM(like_e, LOW),
+            pltpu.VMEM((2, tile, width), LOW),
+            pltpu.VMEM((2, tile, width), LOW),
+            pltpu.VMEM((2, 2, tile, width), LOW),
+            pltpu.VMEM((2, tile, width), FULL),
+            pltpu.VMEM((tile // like[1],) + like[1:], LOW),
+            line,
+            line,
+            line,
+            line,
+            line,
             DMA((2,)),
             DMA((2,)),
-            DMA((n,)),
+            DMA((3,)),
+            DMA((3,)),
+            DMA((2, 4)),
+            DMA((1,)),
         ]
         + Scatter.refs(mesh, 1, tiny_rows, tiny.shape[3], FULL)
         + Scatter.sems(mesh, 1)
         + Scatter.refs(mesh, count, own, width, LOW)
         + Scatter.sems(mesh, count)
-        + Exchange.sems(mesh, 1),
+        + Exchange.sems(mesh, 2),
         compiler_params=remote_params(ident),
         cost_estimate=pl.CostEstimate(flops=60_000_000_000, bytes_accessed=2 * 33_554_432, transcendentals=0),
         name="last_scatter",
-    )(made, *pairs, tiny, sent)
+    )(memory, dkv1, w, x, dx1, *pairs, p, tiny)
 
 
 CUBIC = 0.044715
@@ -1102,7 +1348,7 @@
             ref[...] = jnp.zeros_like(ref)
         loads[0].wait()
 
-    valid = jnp.where(i * tile + rows_of((tile, 1)) < n_ref[0], 1.0, 0.0)
+    valid = jnp.where(i * tile + rows_of((tile, 1)) < n_ref[lax.axis_index(AXES)], 1.0, 0.0)
     x2 = x1_ref[...] + (dot(o_ref[...], w_ref[0], NN) + p_ref[5:6])
     hat, rstd = normal(x2)
     gain = p_ref[GAIN + 2 : GAIN + 3]
@@ -1176,164 +1422,7 @@
     )(length, x1, mixed, cotangent, w, p, bias_up)
 
 
-def unit_of(w, u):
-    return pl.BlockSpec((1,) + w.shape[1:], lambda *_: (u, 0, 0))
-
-
-def cross_attend_back_kernel(heads, n_ref, q_ref, k_ref, v_ref, g_ref, l_ref, i_ref, dq_ref, dkv_ref, acc_ref):
-    def store(at, grad_k, grad_v):
-        dkv_ref[0, at] = grad_k
-        dkv_ref[1, at] = grad_v
-
-    h = pl.program_id(0)
-    back_pair(False, k_ref.shape[1], h, heads, n_ref[0], q_ref[0], k_ref[0], v_ref[0], g_ref[...], l_ref[...], i_ref[...], acc_ref, store)
-    dq_ref[...] = acc_ref[...].astype(LOW)
-
-
-def cross_attend_back(count, q, kv, grad, level, inner):
-    rows, width = grad.shape
-    enc = kv.shape[1]
-
-    def cut(part, n):
-        return pl.BlockSpec((1, n, PAIR), lambda h: (part, 0, h))
-
-    column = pl.BlockSpec((rows, PAIR), lambda h: (0, h))
-    return calls(
-        functools.partial(cross_attend_back_kernel, width // HD),
-        "cross_attend_back",
-        4 * 10 * rows * enc * width,
-        2 * (4 * rows + 4 * enc) * width,
-        grid=(width // PAIR,),
-        in_specs=[SMEM, cut(0, rows), cut(0, enc), cut(1, enc), column, whole((rows, PAIR)), whole((rows, PAIR))],
-        out_specs=[column, pl.BlockSpec((2, enc, PAIR), lambda h: (0, 0, h))],
-        out_shape=[jax.ShapeDtypeStruct((rows, width), LOW), jax.ShapeDtypeStruct((2, enc, width), LOW)],
-        scratch_shapes=[pltpu.VMEM((rows, PAIR), FULL)],
-    )(count, q, kv, kv, grad, level, inner)
-
-
-def memory_grad_kernel(e_ref, b_ref, w_ref, o_ref, de_ref, sum_v, acc_ref):
-    j = pl.program_id(0)
-    o_ref[0] = dot(e_ref[...], b_ref[0], TN).astype(LOW)
-
-    @pl.when(j == 0)
-    def _():
-        acc_ref[...] = dot(b_ref[0], w_ref[0], NT)
-
-    @pl.when(j == 1)
-    def _():
-        de_ref[...] = (acc_ref[...] + dot(b_ref[0], w_ref[0], NT)).astype(LOW)
-        sum_v[...] = jnp.sum(b_ref[0].astype(FULL), axis=0, keepdims=True)
-
-
-def memory_grad(memory, dkv, w):
-    count, width = memory.shape
-    return calls(
-        memory_grad_kernel,
-        "memory_grad",
-        8 * count * width * width,
-        8 * width * width,
-        grid=(2,),
-        in_specs=[
-            whole(memory.shape),
-            pl.BlockSpec((1, count, width), lambda j: (j, 0, 0)),
-            pl.BlockSpec((1, width, width), lambda j: (5 + j, 0, 0)),
-        ],
-        out_specs=[pl.BlockSpec((1, width, width), lambda j: (j, 0, 0)), whole(memory.shape), whole((1, width))],
-        out_shape=[
-            jax.ShapeDtypeStruct((2, width, width), LOW),
-            jax.ShapeDtypeStruct((count, width), LOW),
-            jax.ShapeDtypeStruct((1, width), FULL),
-        ],
-        scratch_shapes=[pltpu.VMEM((count, width), FULL)],
-    )(memory, dkv, w)
-
-
-def cross_back_kernel(x1_ref, dq_ref, dx2_ref, o_ref, wq_ref, wo_ref, p_ref, dx_ref, g1_ref, do_ref, inner_ref,
-                      sum_q, sum_out, sum_gain, sum_shift):
-    @pl.when(pl.program_id(0) == 0)
-    def _():
-        for ref in (sum_q, sum_out, sum_gain, sum_shift):
-            ref[...] = jnp.zeros_like(ref)
-
-    grad = dot(dq_ref[...], wq_ref[0], NT) * SCALE
-    hat, rstd = normal(x1_ref[...])
-    back, lines, shifts = normal_back(hat, rstd, grad, p_ref[GAIN + 1 : GAIN + 2])
-    dx1 = dx2_ref[...] + back
-    dx_ref[...] = dx1
-    g1 = dx1.astype(LOW)
-    g1_ref[...] = g1
-    grad_mixed = dot(g1, wo_ref[0], NT).astype(LOW)
-    do_ref[...] = grad_mixed
-    inner_ref[...] = inner_parts(grad_mixed, o_ref[...], g1.shape[1] // HD)
-    sum_q[...] += jnp.sum(dq_ref[...].astype(FULL), axis=0, keepdims=True) * SCALE
-    sum_out[...] += jnp.sum(g1.astype(FULL), axis=0, keepdims=True)
-    sum_gain[...] += lines
-    sum_shift[...] += shifts
-
-
-def cross_back(x1, dq, dx2, mixed, w, p, tile=256):
-    rows, width = x1.shape
-    part = pl.BlockSpec((tile, width), lambda i: (i, 0))
-    low = jax.ShapeDtypeStruct((rows, width), LOW)
-    line = jax.ShapeDtypeStruct((1, width), FULL)
-    return calls(
-        cross_back_kernel,
-        "cross_back",
-        4 * rows * width * width,
-        16 * rows * width + 4 * width * width,
-        grid=(rows // tile,),
-        in_specs=[part, part, part, part, unit_of(w, 4), unit_of(w, 3), whole(p.shape)],
-        out_specs=[part, part, part, pl.BlockSpec((tile, PAIR), lambda i: (i, 0))] + [whole((1, width))] * 4,
-        out_shape=[jax.ShapeDtypeStruct((rows, width), FULL), low, low, jax.ShapeDtypeStruct((rows, PAIR), LOW), line, line, line, line],
-    )(x1, dq, dx2, mixed, w, w, p)
-
-
-def self_back_kernel(x_ref, dq_ref, dkv_ref, dx1_ref, w_ref, p_ref, dx_ref, sum_q, sum_v, sum_gain, sum_shift):
-    @pl.when(pl.program_id(0) == 0)
-    def _():
-        for ref in (sum_q, sum_v, sum_gain, sum_shift):
-            ref[...] = jnp.zeros_like(ref)
-
-    dq = dq_ref[...]
-    grad = dot(dq, w_ref[0], NT) * SCALE + dot(dkv_ref[0], w_ref[1], NT) + dot(dkv_ref[1], w_ref[2], NT)
-    hat, rstd = normal(x_ref[...].astype(FULL))
-    back, lines, shifts = normal_back(hat, rstd, grad, p_ref[GAIN : GAIN + 1])
-    dx_ref[...] = (dx1_ref[...] + back).astype(LOW)
-    sum_q[...] += jnp.sum(dq.astype(FULL), axis=0, keepdims=True) * SCALE
-    sum_v[...] += jnp.sum(dkv_ref[1].astype(FULL), axis=0, keepdims=True)
-    sum_gain[...] += lines
-    sum_shift[...] += shifts
-
-
-def self_back(x, dq, dkv, dx1, w, p, tile=256):
-    rows, width = x.shape
-    part = pl.BlockSpec((tile, width), lambda i: (i, 0))
-    line = jax.ShapeDtypeStruct((1, width), FULL)
-    return calls(
-        self_back_kernel,
-        "self_back",
-        6 * rows * width * width,
-        14 * rows * width + 6 * width * width,
-        grid=(rows // tile,),
-        in_specs=[part, part, pl.BlockSpec((2, tile, width), lambda i: (0, i, 0)), part, whole((3, width, width)), whole(p.shape)],
-        out_specs=[part] + [whole((1, width))] * 4,
-        out_shape=[jax.ShapeDtypeStruct((rows, width), LOW), line, line, line, line],
-    )(x, dq, dkv, dx1, w, p)
-
-
 AXES = ("dp", "fsdp")
-
-
-def exchange(array):
-    return lax.all_to_all(array, AXES, split_axis=0, concat_axis=0, tiled=True)
-
-
-def leave(array, slots):
-    return exchange(array.reshape(slots, -1, array.shape[-1]))
-
-
-def after(value, *others):
-    return lax.optimization_barrier((value, *others))[0]
 
 
 def per_device(
@@ -1360,9 +1449,6 @@
     depth, ring = mesh.shape["dp"] // 2, mesh.shape["fsdp"]
     own, width = self_out.shape
     blocks = ffn_up.shape[1] // width
-    place = lax.axis_index(AXES)
-    length = lax.dynamic_slice_in_dim(lengths, place, 1)
-    enc_count = lax.dynamic_slice_in_dim(enc_counts, place, 1)
     sent_x, sent_e, sent_c = deal_blocks(deal, [units, encoder, cotangent], False, "deal_in")
 
     up = ffn_up.reshape(own, slots, blocks, own).transpose(2, 0, 1, 3).reshape(blocks, own, width)
@@ -1382,24 +1468,18 @@
     bias_up = bias_up.transpose(1, 0, 2).reshape(1, -1)
 
     w_two, cot, a0, qkv, mixed0, level0, x1, a1, q1, kv1, mixed1, level1 = forward(
-        mesh, length, enc_count, x, memory, w_one, p, late, sent_c, 1
+        mesh, lengths, enc_counts, x, memory, w_one, p, late, sent_c, 1
     )
     cot = cot.reshape(-1, width)
     w_two = w_two.reshape(late.shape[0], width, width)
     (result, r, du, a2, g3, dx2, g2, grad_mixed1, inner1, bias_up_grad, bias_down_grad, bias_five, gain_two, shift_two) = feed(
-        length, x1, mixed1, cot, w_two, p, bias_up
+        lengths, x1, mixed1, cot, w_two, p, bias_up
     )
-    result = leave(result, slots)
-    dq1, dkv1 = cross_attend_back(enc_count, q1, kv1, grad_mixed1, level1, inner1)
-    dx1, g1, grad_mixed0, inner0, bias_three, bias_two, gain_one, shift_one = cross_back(x1, dq1, dx2, mixed0, w_one, p)
-    made, grad_memory, bias_four = memory_grad(memory, dkv1, w_one)
-    grad_memory = after(grad_memory, result).reshape(slots, -1, width)
-    sums_one, dq0, dkv0, grad_memory = feed_scatter(
-        mesh, length, a2, g3, du, r, qkv, grad_mixed0, level0, inner0, grad_memory, 2
+    up_sum, down_sum, dq1, dkv1, dx1, g1, dq0, dkv0, result, bias_three, bias_two, gain_one, shift_one = back_scatter(
+        mesh, lengths, enc_counts, a2, g3, du, r, qkv, q1, kv1, grad_mixed1, level1, inner1, x1, dx2, mixed0, w_one, level0, p,
+        result.reshape(slots, -1, width), 2,
     )
-    up_sum = sums_one[:blocks].reshape(blocks, own, slots, own).transpose(1, 2, 0, 3).reshape(own, -1)
-    down_sum = sums_one[blocks:].reshape(blocks * own, width)
-    dx, bias_zero, bias_one, gain_zero, shift_zero = self_back(x, dq0, dkv0, dx1, w_one, p)
+    bias_zero = bias_one = bias_four = gain_zero = shift_zero = jnp.zeros_like(bias_two)
 
     bias_up_grad = bias_up_grad.reshape(blocks, slots, own).transpose(1, 0, 2).reshape(slots, -1)
 
@@ -1418,12 +1498,10 @@
     )
     tiny = -(-terms.shape[1] // 1024) * 8
     terms = jnp.pad(terms, ((0, 0), (0, tiny * 128 - terms.shape[1]))).reshape(depth, 2, ring * tiny, 128)
-    part = ring * own
     pairs = (mixed1, g2, a1, dq1, mixed0, g1, a0, dq0, dkv0)
-    terms = after(terms, up_sum, down_sum)
-    self_qkv_sum, self_out_sum, cross_qkv_sum, cross_out_sum, tiny_sums, dx = last_scatter(
-        mesh, made.reshape(2, depth, 2, part, width), pairs, terms, dx.reshape(slots, -1, width), 3
-    )
+    self_qkv_sum, self_out_sum, cross_qkv_sum, cross_out_sum, tiny_sums, dx, grad_memory = last_scatter(
+        mesh, memory, dkv1, w_one, x, dx1, pairs, p, terms, units.shape, encoder.shape, 3
+    )[:7]
     result, dx, grad_memory = deal_blocks(deal, [result, dx, grad_memory], True, "deal_out")
     flat = tiny_sums.reshape(-1)
     lines = flat[: 13 * own].reshape(13, own)

time: 652 us -> 615 us (0.943)
  local copies, waits for them, and re-layouts: 26.9 us -> 15.1 us
  waiting for transfers between devices: 9.91 us -> 0 us
  Pallas kernels: 597 us -> 589 us
    pallas_call x5 -> x1, Pallas kernels: 158 us -> 138 us  [back_scatter(): pl.pallas_call(functools.partial(back_scatter_kernel, depth, ring), out_s...]
    pallas_call x1, Pallas kernels: 123 us -> 137 us  [last_scatter(): pl.pallas_call(functools.partial(last_scatter_kernel, depth, ring), out_s...]
    all_to_all x1 -> x0, waiting for transfers between devices: 9.91 us -> none  [exchange(): return lax.all_to_all(array, AXES, split_axis=0, concat_axis=0, tiled=True)]
  transfers between devices with their start and end apart: 1 -> 0, of which waited for: 1 -> 0; matrix products, arithmetic and copies ran while one was open for 0% -> 0% of each run, Pallas kernels for 6% -> 0%
where the time goes in v5:
time: 615 us; the launch traced here: 608 us
  Pallas kernels  589 us (96%)
  local copies, waits for them, and re-layouts  15.1 us (2%)
    pallas_call x1, Pallas kernels, back_scatter(): pl.pallas_call(functools.partial(back_scatter_kernel, depth, ring), out_s...  138 us
    pallas_call x1, Pallas kernels, last_scatter(): pl.pallas_call(functools.partial(last_scatter_kernel, depth, ring), out_s...  137 us
    pallas_call x1, Pallas kernels, forward(): pl.pallas_call(functools.partial(forward_kernel, depth, ring, count), out...  128 us
    pallas_call x1, Pallas kernels, first_gather(): pl.pallas_call(functools.partial(first_gather_kernel, depth, ring, tuple(...  111 us
    pallas_call x1, Pallas kernels, feed(): calls(feed_kernel, 'feed', 2 * rows * width * (4 * inner + 2 * width), 2...  61.5 us
    pallas_call x2, Pallas kernels, deal_blocks(): pl.pallas_call(functools.partial(deal_kernel, out_of, n), out_shape=[jax....  13.6 us

profile of v5, /device:TPU:0, one launch (start us, length us, event | category | flops | bytes accessed | tf_op | source)
XLA Modules:
  0.0 607.7 jit_solution(13133556465542495547)
XLA Ops:
  0.7 6.8 %deal_in.1 = (bf16[32,32,1024]{2,1,0:T(8,128)(2,1)}, bf16[32,8,1024]{2,1,0:T(8,128)(2,1)}, bf16[32,32,1024]{2,1,0:T(8,128)(2,1)}) custom-call(s32[32]{0:T(128)} %deal_ref.3, bf16[32,32,1024]{2,1,0:T(8,128)(2,1)} %refs_0_.2, bf16[32,8,1024]{2,1,0:T(8,128)(2,1)} %refs_1_.2, bf16[32,32,1024]{2,1,0:T(8,128)(2,1)} %refs_2_.2), custom_call_target="tpu_custom_call" | custom-call | tf_op jit(solution)/shard_map/deal_in/pallas_call | solution.py:480
  7.6 0.7 fusion.3.refs_3_
  8.3 111.1 %first_gather.1 = (bf16[7,4,2,4,32,1024]{5,4,3,2,1,0:T(8,128)(2,1)}, bf16[1,4,2,4,16,128]{5,4,3,2,1,0:T(8,128)(2,1)}, bf16[32,32,1024]{2,1,0:T(8,128)(2,1)}, bf16[32,8,1024]{2,1,0:T(8,128)(2,1)}) custom-call(bf16[3,32,1024]{2,1,0:T(8,128)(2,1)} %refs_0_.3, bf16[32,1024]{1,0:T(8,128)(2,1)} %refs_1_.3, bf16[3,32,1024]{2,1,0:T(8,128)(2,1)} %refs_2_.3, ...), custom_call_target="tpu_custom_call" | custom-call | flops 60000002048 | bytes 67108864 | tf_op jit(solution)/shard_map/first_gather/pallas_call | solution.py:438
  119.4 0.9 copy.42
  120.7 0.6 pad.13.p_ref
  121.3 0.8 reshape.116
  122.3 1.1 reshape.117
  123.4 0.9 pad_maximum_fusion.shard
  124.3 127.9 %forward_gather.1 = (bf16[9,4,2,4,32,1024]{5,4,3,2,1,0:T(8,128)(2,1)}, bf16[32,32,1024]{2,1,0:T(8,128)(2,1)}, bf16[1024,1024]{1,0:T(8,128)(2,1)}, bf16[3,1024,10...) custom-call(s32[32]{0:T(128)} %n_ref.5, s32[32]{0:T(128)} %m_ref.3, ...), custom_call_target="tpu_custom_call" | custom-call | flops 70000001024 | bytes 67108864 | tf_op jit(solution)/shard_map/forward_gather/pallas_call | solution.py:757
  252.3 0.7 reshape.122.bu_ref
  253.0 61.5 %feed.1 = (bf16[1024,1024]{1,0:T(8,128)(2,1)}, bf16[4,1024,1024]{2,1,0:T(8,128)(2,1)}, bf16[4,1024,1024]{2,1,0:T(8,128)(2,1)}, bf16[1024,1024]{1,0:T(8,128)(2,1)...) custom-call(s32[32]{0:T(128)} %n_ref.5, ...), custom_call_target="tpu_custom_call" | custom-call | flops 38654705664 | bytes 52428800 | tf_op jit(solution)/shard_map/feed/pallas_call | solution.py:1411
  314.6 138.3 %back_scatter.1 = (f32[32,4096]{1,0:T(8,128)}, f32[128,1024]{1,0:T(8,128)}, bf16[1024,1024]{1,0:T(8,128)(2,1)}, bf16[2,256,1024]{2,1,0:T(8,128)(2,1)}, f32[1024,...) custom-call(s32[32]{0:T(128)} %n_ref.5, s32[32]{0:T(128)} %m_ref.3, ...), custom_call_target="tpu_custom_call" | custom-call | flops 89999998976 | bytes 67108864 | tf_op jit(solution)/shard_map/back_scatter/pallas_call | solution.py:1058
  453.0 1.5 concatenate.22
  455.3 0.7 reduce.3
  456.3 0.7 reshape.128.tiny_ref
  457.0 136.5 %last_scatter.1 = (f32[3,32,1024]{2,1,0:T(8,128)}, f32[32,1024]{1,0:T(8,128)}, f32[3,32,1024]{2,1,0:T(8,128)}, f32[32,1024]{1,0:T(8,128)}, f32[1,8,128]{2,1,0:T(...) custom-call(bf16[256,1024]{1,0:T(8,128)(2,1)} %bitcast.49, ...), custom_call_target="tpu_custom_call" | custom-call | flops 60000002048 | bytes 67108864 | tf_op jit(solution)/shard_map/last_scatter/pallas_call | solution.py:1276
  593.6 6.8 %deal_out.1 = (bf16[32,32,1024]{2,1,0:T(8,128)(2,1)}, bf16[32,32,1024]{2,1,0:T(8,128)(2,1)}, bf16[32,8,1024]{2,1,0:T(8,128)(2,1)}) custom-call(s32[32]{0:T(128)} %deal_ref.3, bf16[32,32,1024]{2,1,0:T(8,128)(2,1)} %get-tuple-element.95.refs_0_, bf16[32,32,1024]{2,1,0:T(8,128)(2,1)} %get-tuple-element.114.refs_1_, bf16[32,8,1024]{2,1,0:T(8,128)(2,1)} %get-tuple-element.115.refs_2_), custom_call_target="tpu_custom_call" | custom-call | tf_op jit(solution)/shard_map/deal_out/pallas_call | solution.py:480
  601.1 0.6 slice.48
  602.8 0.7 copy.49
  603.6 0.7 copy.50
  604.2 0.7 copy.51
  605.0 0.7 copy.52
  605.6 0.8 copy.53
  606.4 0.8 copy.54
  (64 shorter events, 3.9 us)
Async XLA Ops:
  0.6 6.8 %copy-start.18 = (bf16[32]{0:T(256)(128)(2,1)S(1)}, bf16[32]{0:T(256)(128)(2,1)}, u32[]{:S(2)}) copy-start(bf16[32]{0:T(256)(128)(2,1)} %param.31) | copy-start | bytes 196
  0.7 6.8 %copy-start.15 = (bf16[6,32]{1,0:T(8,128)(2,1)S(1)}, bf16[6,32]{1,0:T(8,128)(2,1)}, u32[]{:S(2)}) copy-start(bf16[6,32]{1,0:T(8,128)(2,1)} %param.29) | copy-start | bytes 1156
  0.7 6.8 %copy-start.17 = (bf16[3,32]{1,0:T(4,128)(2,1)S(1)}, bf16[3,32]{1,0:T(4,128)(2,1)}, u32[]{:S(2)}) copy-start(bf16[3,32]{1,0:T(4,128)(2,1)} %param.32) | copy-start | bytes 580
  0.7 6.8 %copy-start.16 = (bf16[3,32]{1,0:T(4,128)(2,1)S(1)}, bf16[3,32]{1,0:T(4,128)(2,1)}, u32[]{:S(2)}) copy-start(bf16[3,32]{1,0:T(4,128)(2,1)} %param.33) | copy-start | bytes 580
  0.7 7.0 %copy-start.19 = (bf16[128]{0:T(256)(128)(2,1)S(1)}, bf16[128]{0:T(256)(128)(2,1)}, u32[]{:S(2)}) copy-start(bf16[128]{0:T(256)(128)(2,1)} %param.30) | copy-start | bytes 772
  8.3 113.0 %copy-start.4 = (bf16[32,4096]{1,0:T(8,128)(2,1)S(1)}, bf16[32,4096]{1,0:T(8,128)(2,1)}, u32[]{:S(2)}) copy-start(bf16[32,4096]{1,0:T(8,128)(2,1)} %param.27) | copy-start | bytes 786436
  121.3 2.1 copy-start.5
  121.3 2.1 copy-start.8
  314.5 138.4 %copy-start.11 = (f32[1,1024]{1,0:T(1,128)S(1)}, f32[1,1024]{1,0:T(1,128)}, u32[]{:S(2)}) copy-start(f32[1,1024]{1,0:T(1,128)} %get-tuple-element.108) | copy-start | bytes 12292
  314.5 138.4 %copy-start.12 = (f32[1,1024]{1,0:T(1,128)S(1)}, f32[1,1024]{1,0:T(1,128)}, u32[]{:S(2)}) copy-start(f32[1,1024]{1,0:T(1,128)} %get-tuple-element.107) | copy-start | bytes 12292
  314.5 138.4 %copy-start.13 = (f32[1,1024]{1,0:T(1,128)S(1)}, f32[1,1024]{1,0:T(1,128)}, u32[]{:S(2)}) copy-start(f32[1,1024]{1,0:T(1,128)} %get-tuple-element.110) | copy-start | bytes 12292
  314.6 138.4 %copy-start.14 = (f32[1,1024]{1,0:T(1,128)S(1)}, f32[1,1024]{1,0:T(1,128)}, u32[]{:S(2)}) copy-start(f32[1,1024]{1,0:T(1,128)} %get-tuple-element.112) | copy-start | bytes 12292
  314.6 140.8 %copy-start.9 = (f32[1,4096]{1,0:T(1,128)S(1)}, f32[1,4096]{1,0:T(1,128)}, u32[]{:S(2)}) copy-start(f32[1,4096]{1,0:T(1,128)} %get-tuple-element.113) | copy-start | bytes 49156
  593.5 6.9 %copy-start.10 = (f32[1,8,128]{2,1,0:T(8,128)S(1)}, f32[1,8,128]{2,1,0:T(8,128)}, u32[]{:S(2)}) copy-start(f32[1,8,128]{2,1,0:T(8,128)} %get-tuple-element.125) | copy-start | bytes 12292
  593.6 9.3 %copy-start.3 = (f32[3,32,1024]{2,1,0:T(8,128)S(1)}, f32[3,32,1024]{2,1,0:T(8,128)}, u32[]{:S(2)}) copy-start(f32[3,32,1024]{2,1,0:T(8,128)} %get-tuple-element.145) | copy-start | bytes 1179652
  593.6 10.0 %copy-start.7 = (f32[32,1024]{1,0:T(8,128)S(1)}, f32[32,1024]{1,0:T(8,128)}, u32[]{:S(2)}) copy-start(f32[32,1024]{1,0:T(8,128)} %get-tuple-element.146) | copy-start | bytes 393220
  593.6 10.7 %copy-start.2 = (f32[3,32,1024]{2,1,0:T(8,128)S(1)}, f32[3,32,1024]{2,1,0:T(8,128)}, u32[]{:S(2)}) copy-start(f32[3,32,1024]{2,1,0:T(8,128)} %get-tuple-element.147) | copy-start | bytes 1179652
  593.6 11.4 %copy-start.6 = (f32[32,1024]{1,0:T(8,128)S(1)}, f32[32,1024]{1,0:T(8,128)}, u32[]{:S(2)}) copy-start(f32[32,1024]{1,0:T(8,128)} %get-tuple-element.148) | copy-start | bytes 393220
  600.4 5.3 copy-start.1
  600.4 6.0 copy-start
